TPU v7x, 128 devices: a whole 4x4x4 slice. The times are simulated.
128 devices in a mesh: row: 4 (over x), col: 32 (over z, y, core).
Axes of the slice: x: 4, y: 4, z: 4, core: 2. Of those that a mesh axis runs over, the one named last changes fastest.
Arguments:
- frames: bfloat16 [32768, 128], P('col'), may hold values from -3 to 3
- width_class: int32 [32768], P('col'), may hold values from 0 to 3
- start: float32 [16, 32768], P(None, 'col'), may hold values from -6 to 6
Outputs:
- embedding: float32 [16, 32768], P(None, 'col')
- log_degree: float32 [32768], P('col')
All inputs are finite; a program needn't handle non-finite values.
Results may differ from a plain program's by a relative error of at most 0.0053.
Values may be sent and summed in bfloat16 or wider, within the bound.
No kernel may reach another device: no remote copies, remote signals or barrier semaphores. Data moves between devices by JAX's collectives and lax.ppermute only.
A program may use at most 128 MiB of HBM per device.

v0:
```python
import math

import jax
import jax.numpy as jnp
from jax import lax
from jax.sharding import PartitionSpec as P

ITERS = 3


base_width = 2.8
width_growth = 1.3


def kernel_tile(row_frames, row_sq, row_inv, col_frames, col_sq, col_inv):
    products = lax.dot_general(
        row_frames, col_frames, (((1,), (1,)), ((), ())), preferred_element_type=jnp.float32
    )
    distance = row_sq[:, None] + col_sq[None, :] - 2.0 * products
    return jnp.exp(-(distance * row_inv[:, None]) * col_inv[None, :]).astype(jnp.bfloat16)


def body(frames, width_class, start):
    row_count = lax.axis_size("row")
    col_count = lax.axis_size("col")
    row_index = lax.axis_index("row")
    col_index = lax.axis_index("col")
    block_len = frames.shape[0]
    total_len = block_len * col_count
    gathered, class_all = (
        lax.all_gather(frames, "col", axis=0, tiled=True),
        lax.all_gather(width_class.astype(jnp.bfloat16), "col", axis=0, tiled=True),
    )
    sq_norm = jnp.sum(jnp.square(gathered.astype(jnp.float32)), axis=1)
    inv_width = 1.0 / (base_width * jnp.power(width_growth, class_all.astype(jnp.float32)))
    tile_slots = (col_count + row_count - 1) // row_count

    def locate(position):
        target = row_index + row_count * position
        return (target, col_index, target <= col_index)

    def apply_kernel(vectors):
        vec_rows = vectors.shape[0]
        every_vec = lax.all_gather(vectors, "col", axis=1, tiled=True)
        empty_sum = jnp.zeros((vec_rows, total_len), jnp.float32)

        def add_row(partial_value, block_at, contrib):
            current_part = lax.dynamic_slice_in_dim(
                partial_value, block_at * block_len, block_len, 1
            )
            return lax.dynamic_update_slice_in_dim(
                partial_value, current_part + contrib, block_at * block_len, 1
            )

        def tile_term(position, partial_value):
            target, column, usable = locate(position)

            def with_tile(partial_value):
                row_start = target * block_len
                col_start = column * block_len
                kernel = kernel_tile(
                    lax.dynamic_slice_in_dim(gathered, row_start, block_len, 0),
                    lax.dynamic_slice_in_dim(sq_norm, row_start, block_len, 0),
                    lax.dynamic_slice_in_dim(inv_width, row_start, block_len, 0),
                    lax.dynamic_slice_in_dim(gathered, col_start, block_len, 0),
                    lax.dynamic_slice_in_dim(sq_norm, col_start, block_len, 0),
                    lax.dynamic_slice_in_dim(inv_width, col_start, block_len, 0),
                )
                row_vec = lax.dynamic_slice_in_dim(every_vec, row_start, block_len, 1)
                col_vec = lax.dynamic_slice_in_dim(every_vec, col_start, block_len, 1)
                into_row = lax.dot_general(
                    col_vec, kernel, (((1,), (1,)), ((), ())), preferred_element_type=jnp.float32
                )
                into_col = lax.dot_general(
                    row_vec, kernel, (((1,), (0,)), ((), ())), preferred_element_type=jnp.float32
                )
                into_col = jnp.where(target == column, 0.0, into_col)
                partial_value = add_row(partial_value, target, into_row)
                return add_row(partial_value, column, into_col)

            def skip_tile(partial_value):
                return partial_value

            return lax.cond(usable, with_tile, skip_tile, partial_value)

        partial_value = lax.fori_loop(0, tile_slots, tile_term, empty_sum)
        column_part = lax.psum_scatter(partial_value, "col", scatter_dimension=1, tiled=True)
        return lax.psum(column_part, "row")

    unit_row = jnp.ones((1, block_len), jnp.bfloat16)
    density = apply_kernel(unit_row)[0] / total_len
    inv_density = (1.0 / density).astype(jnp.bfloat16)
    degree = apply_kernel(inv_density[None, :])[0] / (total_len * density)
    log_degree = jnp.log(degree)
    weight = 1.0 / (density * jnp.sqrt(degree))
    current = start
    for iteration in range(ITERS):
        scaled = (weight[None, :] * current).astype(jnp.bfloat16)
        projected = weight[None, :] * apply_kernel(scaled)
        gram_matrix = lax.psum(
            jnp.dot(projected, projected.T, precision=lax.Precision.HIGHEST), "col"
        )
        factor = jnp.linalg.cholesky(gram_matrix)
        current = lax.linalg.triangular_solve(factor, projected, left_side=True, lower=True)
    return (math.sqrt(total_len) * current, log_degree)


def solution(mesh):
    in_specs = (P("col", None), P("col"), P(None, "col"))
    out_specs = (P(None, "col"), P("col"))
    return jax.shard_map(body, mesh=mesh, in_specs=in_specs, out_specs=out_specs, check_vma=False)
```

profile of v0, /device:TPU:1, one launch (start us, length us, event | category | flops | bytes accessed | tf_op | source)
XLA Modules:
  0.0 1281.4 jit_solution(3610727450908750060)
XLA Ops:
  8.6 27.0 %all_gather.20 = bf16[32768]{0:T(1024)(128)(2,1)S(1)} all-gather(bf16[1024]{0:T(1024)(128)(2,1)S(1)} %convert_element_type.74), channel_id=1, replica_groups=mesh['row'=4,'col'=32] {'col'}, dimensions={0}, use_global_device_ids=true | all-gather | bytes 67584 | tf_op jit(solution)/shard_map/all_gather | solution.py:32
  35.7 31.4 %all-gather.5.cloned.1.call-done = bf16[32768,128]{1,0:T(8,128)(2,1)} async-done(((bf16[1024,128]{1,0:T(8,128)(2,1)}), bf16[32768,128]{1,0:T(8,128)(2,1)}) %all-gather.5.cloned.1.call-update) | async-done | bytes 8388624 | tf_op jit(solution)/shard_map/all_gather | solution.py:31
  67.0 6.8 multiply_reduce_fusion
  73.9 3.9 while.80
  73.9 3.5 conditional.10
  77.7 8.2 copy.20
  86.1 137.0 %reduce-scatter.16.cloned.1.call-done = f32[1024,1]{1,0:T(8,128)} async-done(((f32[32768,1]{1,0:T(8,128)}), f32[1024,1]{1,0:T(8,128)}) %reduce-scatter.16.cloned.1.call-update) | async-done | bytes 4112
  224.3 8.3 psum.56
  232.6 28.0 %all_gather.21 = bf16[1,32768]{1,0:T(2,128)(2,1)S(1)} all-gather(bf16[1,1024]{1,0:T(2,128)(2,1)S(1)} %divide_convert_fusion), channel_id=1, replica_groups=mesh['row'=4,'col'=32] {'col'}, dimensions={1}, use_global_device_ids=true | all-gather | bytes 67584 | tf_op jit(solution)/shard_map/all_gather | solution.py:44
  260.7 3.8 while.81
  260.7 3.5 conditional.11
  264.6 8.2 copy.22
  272.9 134.4 %reduce-scatter.18.cloned.1.call-done = f32[1024,1]{1,0:T(8,128)} async-done(((f32[32768,1]{1,0:T(8,128)}), f32[1024,1]{1,0:T(8,128)}) %reduce-scatter.18.cloned.1.call-update) | async-done | bytes 4112
  408.5 8.4 psum.57
  418.2 43.9 %all-gather.7.cloned.1.call-done = bf16[16,32768]{1,0:T(8,128)(2,1)} async-done(((bf16[16,1024]{1,0:T(8,128)(2,1)}), bf16[16,32768]{1,0:T(8,128)(2,1)}) %all-gather.7.cloned.1.call-update) | async-done | bytes 1048592 | tf_op jit(solution)/shard_map/all_gather | solution.py:44
  463.6 6.4 while.82
  463.6 6.4 conditional.12
  470.1 120.4 %reduce-scatter.10.cloned.1.call-done = f32[16,1024]{1,0:T(8,128)} async-done(((f32[16,32768]{1,0:T(8,128)}), f32[16,1024]{1,0:T(8,128)}) %reduce-scatter.10.cloned.1.call-update) | async-done | bytes 65552 | tf_op jit(solution)/shard_map/reduce_scatter | solution.py:87
  590.6 41.7 %all-reduce.4.cloned.1.call-done = f32[16,1024]{1,0:T(8,128)} async-done(((f32[16,1024]{1,0:T(8,128)}), f32[16,1024]{1,0:T(8,128)}) %all-reduce.4.cloned.1.call-update) | async-done | bytes 65552 | tf_op jit(solution)/shard_map/psum | solution.py:88
  633.3 66.1 %psum.59 = f32[16,16]{0,1:T(8,128)S(1)} all-reduce(f32[16,16]{0,1:T(8,128)S(1)} %fusion.59), channel_id=1, replica_groups=mesh['row'=4,'col'=32] {'col'}, use_global_device_ids=true, to_apply=%region_19.20 | all-reduce | flops 256 | bytes 2048 | tf_op jit(solution)/shard_map/psum | solution.py:100
  705.3 41.5 %all-gather.9.cloned.1.call-done = bf16[16,32768]{1,0:T(8,128)(2,1)} async-done(((bf16[16,1024]{1,0:T(8,128)(2,1)}), bf16[16,32768]{1,0:T(8,128)(2,1)}) %all-gather.9.cloned.1.call-update) | async-done | bytes 1048592 | tf_op jit(solution)/shard_map/all_gather | solution.py:44
  748.3 6.4 while.83
  748.3 6.4 conditional.13
  754.8 120.4 %reduce-scatter.12.cloned.1.call-done = f32[16,1024]{1,0:T(8,128)} async-done(((f32[16,32768]{1,0:T(8,128)}), f32[16,1024]{1,0:T(8,128)}) %reduce-scatter.12.cloned.1.call-update) | async-done | bytes 65552 | tf_op jit(solution)/shard_map/reduce_scatter | solution.py:87
  875.3 42.0 %all-reduce.6.cloned.1.call-done = f32[16,1024]{1,0:T(8,128)} async-done(((f32[16,1024]{1,0:T(8,128)}), f32[16,1024]{1,0:T(8,128)}) %all-reduce.6.cloned.1.call-update) | async-done | bytes 65552 | tf_op jit(solution)/shard_map/psum | solution.py:88
  918.3 65.9 %psum.61 = f32[16,16]{0,1:T(8,128)S(1)} all-reduce(f32[16,16]{0,1:T(8,128)S(1)} %fusion.56), channel_id=1, replica_groups=mesh['row'=4,'col'=32] {'col'}, use_global_device_ids=true, to_apply=%region_28.0 | all-reduce | flops 256 | bytes 2048 | tf_op jit(solution)/shard_map/psum | solution.py:100
  990.1 41.5 %all-gather.11.cloned.1.call-done = bf16[16,32768]{1,0:T(8,128)(2,1)} async-done(((bf16[16,1024]{1,0:T(8,128)(2,1)}), bf16[16,32768]{1,0:T(8,128)(2,1)}) %all-gather.11.cloned.1.call-update) | async-done | bytes 1048592 | tf_op jit(solution)/shard_map/all_gather | solution.py:44
  1033.1 6.4 while.84
  1033.1 6.4 conditional.14
  1039.6 120.4 %reduce-scatter.14.cloned.1.call-done = f32[16,1024]{1,0:T(8,128)} async-done(((f32[16,32768]{1,0:T(8,128)}), f32[16,1024]{1,0:T(8,128)}) %reduce-scatter.14.cloned.1.call-update) | async-done | bytes 65552 | tf_op jit(solution)/shard_map/reduce_scatter | solution.py:87
  1160.0 41.7 %all-reduce.8.cloned.1.call-done = f32[16,1024]{1,0:T(8,128)} async-done(((f32[16,1024]{1,0:T(8,128)}), f32[16,1024]{1,0:T(8,128)}) %all-reduce.8.cloned.1.call-update) | async-done | bytes 65552 | tf_op jit(solution)/shard_map/psum | solution.py:88
  1202.8 65.9 %psum.63 = f32[16,16]{0,1:T(8,128)S(1)} all-reduce(f32[16,16]{0,1:T(8,128)S(1)} %fusion.53), channel_id=1, replica_groups=mesh['row'=4,'col'=32] {'col'}, use_global_device_ids=true, to_apply=%region_35.38 | all-reduce | flops 256 | bytes 2048 | tf_op jit(solution)/shard_map/psum | solution.py:100
  (125 shorter events, 57.4 us)
Async XLA Ops:
  7.2 59.9 %all-gather.5.cloned.1.call-start = ((), (), s32[]{:S(2)}) async-start(), calls=%async_computation.5 | async-start | bytes 8650752 | tf_op jit(solution)/shard_map/all_gather | solution.py:31
  7.9 215.2 %reduce-scatter.16.cloned.1.call-start = ((), (), s32[]{:S(2)}) async-start(), calls=%async_computation.15 | async-start | bytes 17301504
  86.0 321.3 %reduce-scatter.18.cloned.1.call-start = ((), (), s32[]{:S(2)}) async-start(), calls=%async_computation.16 | async-start | bytes 17301504
  272.8 144.7 %copy-start = (f32[16,1024]{1,0:T(8,128)S(1)}, f32[16,1024]{1,0:T(8,128)}, u32[]{:S(2)}) copy-start(f32[16,1024]{1,0:T(8,128)} %param.28) | copy-start | bytes 196612
  272.8 189.3 %all-gather.7.cloned.1.call-start = ((), (), s32[]{:S(2)}) async-start(), calls=%async_computation.6 | async-start | bytes 1081344 | tf_op jit(solution)/shard_map/all_gather | solution.py:44
  418.2 172.3 %reduce-scatter.10.cloned.1.call-start = ((), (), s32[]{:S(2)}) async-start(), calls=%async_computation.7 | async-start | bytes 2162688 | tf_op jit(solution)/shard_map/reduce_scatter | solution.py:87
  470.1 162.2 %all-reduce.4.cloned.1.call-start = ((), (), s32[]{:S(2)}) async-start(), calls=%async_computation.8 | async-start | bytes 131072 | tf_op jit(solution)/shard_map/psum | solution.py:88
  590.5 156.3 %all-gather.9.cloned.1.call-start = ((), (), s32[]{:S(2)}) async-start(), calls=%async_computation.9 | async-start | bytes 1081344 | tf_op jit(solution)/shard_map/all_gather | solution.py:44
  705.3 169.9 %reduce-scatter.12.cloned.1.call-start = ((), (), s32[]{:S(2)}) async-start(), calls=%async_computation.10 | async-start | bytes 2162688 | tf_op jit(solution)/shard_map/reduce_scatter | solution.py:87
  754.8 162.5 %all-reduce.6.cloned.1.call-start = ((), (), s32[]{:S(2)}) async-start(), calls=%async_computation.11 | async-start | bytes 131072 | tf_op jit(solution)/shard_map/psum | solution.py:88
  875.2 156.4 %all-gather.11.cloned.1.call-start = ((), (), s32[]{:S(2)}) async-start(), calls=%async_computation.12 | async-start | bytes 1081344 | tf_op jit(solution)/shard_map/all_gather | solution.py:44
  990.1 169.9 %reduce-scatter.14.cloned.1.call-start = ((), (), s32[]{:S(2)}) async-start(), calls=%async_computation.13 | async-start | bytes 2162688 | tf_op jit(solution)/shard_map/reduce_scatter | solution.py:87
  1039.6 162.2 %all-reduce.8.cloned.1.call-start = ((), (), s32[]{:S(2)}) async-start(), calls=%async_computation.14 | async-start | bytes 131072 | tf_op jit(solution)/shard_map/psum | solution.py:88
Sparse Core Ops, SparseCore 0:
  10.3 56.7 all-gather.4
  86.1 136.8 reduce-scatter.15
  272.9 134.2 reduce-scatter.17
  418.3 43.8 all-gather.6
  470.2 120.2 reduce-scatter.9
  592.7 39.5 all-reduce.3
  705.4 41.4 all-gather.8
  754.9 120.2 reduce-scatter.11
  877.6 39.5 all-reduce.5
  990.2 41.4 all-gather.10
  1039.7 120.2 reduce-scatter.13
  1162.1 39.5 all-reduce.7
where the time goes:
time: 1290 us; the launch traced here: 1280 us
  waiting for transfers between devices  917 us (71%)
  blocking collectives  270 us (21%)
  matrix products  34.5 us (3%)
  local copies, waits for them, and re-layouts  23.8 us (2%)
  other arithmetic  20.9 us (2%)
  between operations  14.4 us (1%)
    reduce_scatter x3, waiting for transfers between devices, apply_kernel(): lax.psum_scatter(partial_value, 'col', scatter_dimension=1, tiled=True)  361 us
    unnamed x14, waiting for transfers between devices  272 us
    psum x3, blocking collectives, body(): lax.psum(jnp.dot(projected, projected.T, precision=lax.Precision.HIGHEST)...  198 us
    all_gather x3, waiting for transfers between devices, apply_kernel(): every_vec = lax.all_gather(vectors, 'col', axis=1, tiled=True)  127 us
    psum x3, waiting for transfers between devices, apply_kernel(): return lax.psum(column_part, 'row')  125 us
    all_gather x1, waiting for transfers between devices, body(): lax.all_gather(frames, 'col', axis=0, tiled=True)  31.4 us
    all_gather x1, blocking collectives, apply_kernel(): every_vec = lax.all_gather(vectors, 'col', axis=1, tiled=True)  28 us
    all_gather x1, blocking collectives, body(): lax.all_gather(width_class.astype(jnp.bfloat16), 'col', axis=0, tiled=True)  27 us
  transfers between devices with their start and end apart: 12, of which 12 were waited for; matrix products, arithmetic and copies ran while one was open for 0% of the time, Pallas kernels for 0%

commit v1 on v0

v1 whole, which is shorter than its diff:
```python
import functools
import math

import jax
import jax.numpy as jnp
from jax import lax
from jax.experimental import pallas as pl
from jax.experimental.pallas import tpu as pltpu
from jax.sharding import Mesh
from jax.sharding import PartitionSpec as P


ITERS = 3
F = 128
CB = 1024
QB = CB // 4
NJ = 2 * CB
NI = 16 * QB
KV = 16
NTOT = 32768
CLS = QB + 4 * KV
PROWS = CLS + 16
base_width = 2.8
width_growth = 1.3
F32 = jnp.float32
BF16 = jnp.bfloat16
VM = pltpu.VMEM
NN = (((1,), (0,)), ((), ()))
NT = (((1,), (1,)), ((), ()))
TN = (((0,), (0,)), ((), ()))


def dot(a, b, dims):
    return lax.dot_general(a, b, dims, preferred_element_type=F32)


def call(kernel, name, outs, args, flops=0, byte_count=0, aliases=None):
    def spec(a):
        if a.dtype == jnp.int32 and a.ndim == 1:
            return pl.BlockSpec(memory_space=pltpu.SMEM)
        return pl.BlockSpec(memory_space=VM)

    return pl.pallas_call(
        kernel,
        out_shape=outs,
        in_specs=[spec(a) for a in args],
        out_specs=jax.tree.map(lambda _: pl.BlockSpec(memory_space=VM), outs),
        compiler_params=pltpu.CompilerParams(vmem_limit_bytes=24 << 20),
        cost_estimate=pl.CostEstimate(flops=flops, bytes_accessed=byte_count, transcendentals=0),
        name=name,
    )(*args)


def sds(shape, dtype=F32):
    return jax.ShapeDtypeStruct(shape, dtype)


def vmem(shape, dtype=F32):
    return pltpu.VMEM(shape, dtype)


def keep(a):
    return pltpu.with_memory_space_constraint(a, VM)


def pack_kernel(pos, frames, classes, start, piece, mine):
    x = pos[0]
    piece[0:QB, :] = frames[pl.ds(pl.multiple_of(x * QB, QB), QB), :]
    quarter = start[:, pl.ds(pl.multiple_of(x * QB, QB), QB)]
    high = quarter.astype(BF16)
    low = (quarter - high.astype(F32)).astype(BF16)
    for h in range(2):
        at = QB + 2 * h * KV
        piece[at : at + KV, :] = high[:, h * 128 : (h + 1) * 128]
        piece[at + KV : at + 2 * KV, :] = low[:, h * 128 : (h + 1) * 128]
    cls = classes[...].astype(F32)
    cls = jnp.concatenate([cls, jnp.zeros_like(cls)], axis=0).astype(BF16)
    piece[CLS:PROWS, :] = cls
    mine[0:CB, :] = frames[...]
    mine[CB : CB + 16, :] = cls


def stack_kernel(a, b, c, d, out):
    for n, ref in enumerate((a, b, c, d)):
        out[n] = ref[...]


def augment(rows, own_first):
    wide = rows.astype(F32)
    half = -0.5 * jnp.sum(wide * wide, axis=1, keepdims=True)
    p1 = half.astype(BF16).astype(F32)
    p2 = (half - p1).astype(BF16).astype(F32)
    p3 = half - p1 - p2
    lane = lax.broadcasted_iota(jnp.int32, (rows.shape[0], 128), 1)
    first = 0 if own_first else 3
    ones = jnp.logical_and(lane >= 3 - first, lane < 6 - first)
    extra = jnp.where(ones, 1.0, 0.0)
    for n, part in enumerate((p1, p2, p3)):
        extra = jnp.where(lane == first + n, part, extra)
    return jnp.concatenate([rows, extra.astype(BF16)], axis=1)


def inverse_width(cls):
    return jnp.exp2(cls * (-math.log2(width_growth))) * (1.0 / base_width)


def make_rows(piece_list, x, aug_j, coef_j, k_ref, row0, sum_j):
    augs, coefs = [], []
    for ref in piece_list:
        augs.append(augment(ref[0:QB, :], True))
        cls = ref[CLS:PROWS, :].astype(F32)
        row = lax.broadcasted_iota(jnp.int32, cls.shape, 0)
        ones = jnp.ones((16, 128), BF16)
        for h in range(2):
            one_row = jnp.where(row == 2 * x + h, cls, 0.0).astype(BF16)
            coefs.append(inverse_width(dot(one_row, ones, TN)[:, :1]))
    aug_i = jnp.concatenate(augs, axis=0)
    coef_i = jnp.concatenate(coefs, axis=0)
    half = 512
    ones_row = jnp.ones((8, half), BF16)
    parts = []
    for n in range(4 * QB // half):
        lo = n * half
        m = dot(aug_i[lo : lo + half], aug_j[...], NT)
        kb = jnp.exp2(m * coef_i[lo : lo + half] * coef_j[...]).astype(BF16)
        k_ref[row0 + lo : row0 + lo + half, :] = kb
        sum_j[...] += dot(ones_row, kb, NN)
        kf = kb.astype(F32)
        acc = kf[:, :128]
        for t in range(1, NJ // 128):
            acc = acc + kf[:, t * 128 : (t + 1) * 128]
        parts.append(acc)
    acc = jnp.concatenate(parts, axis=0)
    ones = jnp.ones((8, 128), BF16)
    a1 = acc.astype(BF16)
    r1 = acc - a1.astype(F32)
    a2 = r1.astype(BF16)
    a3 = (r1 - a2.astype(F32)).astype(BF16)
    return dot(ones, a1, NT) + dot(ones, a2, NT) + dot(ones, a3, NT)


def put_pieces(idx, group, sums, out):
    for n in range(4):
        out[pl.ds(idx[4 * group + n], 1), :] = sums[0:1, n * QB : (n + 1) * QB]


def gen_a_kernel(pos, idx, mine, other, line, aug_j, coef_j, k0, sum_j, sum_i):
    c = pos[1]

    def side(first, second):
        for n, ref in enumerate((first, second)):
            aug_j[n * CB : (n + 1) * CB, :] = augment(ref[0:CB, :], False)
            coef = inverse_width(ref[CB : CB + 16, :].astype(F32)) * (2.0 * math.log2(math.e))
            for r in range(8):
                lo = n * CB + r * 128
                coef_j[:, lo : lo + 128] = coef[r : r + 1, :]

    @pl.when(c == 0)
    def _():
        side(mine, other)

    @pl.when(c != 0)
    def _():
        side(other, mine)

    sum_j[...] = jnp.zeros_like(sum_j)
    sum_i[...] = jnp.zeros_like(sum_i)
    sums = make_rows([line.at[n] for n in range(4)], pos[0], aug_j, coef_j, k0, 0, sum_j)
    put_pieces(idx, 0, sums, sum_i)


def gen_b_kernel(pos, idx, g1, g2, g3, aug_j, coef_j, sum_j_in, sum_i_in, k1, out_j, out_i, sum_j):
    sum_j[...] = sum_j_in[...]
    out_i[...] = sum_i_in[...]
    for g, ref in enumerate((g1, g2, g3)):
        pieces = [ref.at[n] for n in range(4)]
        sums = make_rows(pieces, pos[0], aug_j, coef_j, k1, g * 4 * QB, sum_j)
        put_pieces(idx, g + 1, sums, out_i)
    out_j[...] = sum_j[0:1, :]


def add2_kernel(a0, a1, b0, b1, b2, b3, oa, ob):
    oa[...] = a0[...] + a1[...]
    ob[...] = (b0[...] + b1[...]) + (b2[...] + b3[...])


def spread_pieces(idx, table, scratch):
    for n in range(16):
        scratch[0:1, n * QB : (n + 1) * QB] = table[pl.ds(idx[n], 1), :]


def degree_kernel(idx, k0, k1, j0, j1, j2, j3, i0, i1, i2, i3, dj, di, gj, gi, tab, row):
    sj = ((j0[...] + j1[...]) + (j2[...] + j3[...])) * (1.0 / NTOT)
    si = ((i0[...] + i1[...]) + (i2[...] + i3[...])) * (1.0 / NTOT)
    dj[...] = sj
    di[...] = si
    tab[...] = 1.0 / si
    spread_pieces(idx, tab, row)
    inv_i = jnp.broadcast_to(row[0:1, :], (8, NI)).astype(BF16)
    inv_j = jnp.broadcast_to(1.0 / sj, (8, NJ)).astype(BF16)
    n0 = k0.shape[0]
    g = dot(inv_i[:, :n0], k0[...], NN) + dot(inv_i[:, n0:], k1[...], NN)
    gj[...] = g[0:1, :]
    gi[...] = jnp.zeros_like(gi)
    put_pieces(idx, 0, dot(inv_j, k0[...], NT), gi)
    for n in range(3):
        part = dot(inv_j, k1[n * 4 * QB : (n + 1) * 4 * QB, :], NT)
        put_pieces(idx, n + 1, part, gi)


def split_out(c, y, extra, own, away):
    @pl.when(c == 0)
    def _():
        own[:, :CB] = y[:, :CB]
        away[:, :CB] = y[:, CB:]

    @pl.when(c != 0)
    def _():
        own[:, :CB] = y[:, CB:]
        away[:, :CB] = y[:, :CB]

    if extra is not None:
        own[:, CB:] = extra
        away[:, CB:] = extra


def apply_k(v, k0, k1):
    n0 = k0.shape[0]
    return dot(v[:, :n0], k0[...], NN) + dot(v[:, n0:], k1[...], NN)


def first_kernel(
    pos, idx, k0, k1, line, g1, g2, g3, dj, di, j0, j1, j2, j3, i0, i1, i2, i3,
    own, away, weight_i, weight_own, log_degree, tab, row, vec,
):
    c = pos[1]
    degree_j = ((j0[...] + j1[...]) + (j2[...] + j3[...])) / (NTOT * dj[...])
    degree_i = ((i0[...] + i1[...]) + (i2[...] + i3[...])) / (NTOT * di[...])
    weight_j = 1.0 / (dj[...] * jnp.sqrt(degree_j))
    tab[...] = 1.0 / (di[...] * jnp.sqrt(degree_i))
    spread_pieces(idx, tab, row)
    weight_i[...] = row[...]
    log_j = jnp.log(degree_j)

    @pl.when(c == 0)
    def _():
        weight_own[...] = weight_j[:, :CB]
        log_degree[...] = log_j[:, :CB]

    @pl.when(c != 0)
    def _():
        weight_own[...] = weight_j[:, CB:]
        log_degree[...] = log_j[:, CB:]

    for g, ref in enumerate((line, g1, g2, g3)):
        for n in range(4):
            at = (4 * g + n) * QB
            for h in range(2):
                both = ref[n, QB + 2 * h * KV : QB + 2 * (h + 1) * KV, :].astype(F32)
                part = both[:KV] + both[KV:]
                lo = at + h * 128
                vec[:, lo : lo + 128] = (part * row[0:1, lo : lo + 128]).astype(BF16)
    y = apply_k(vec, k0, k1)
    split_out(c, y, None, own, away)


def next_kernel(pos, idx, k0, k1, weight_i, pieces, own, away, vec, parts):
    c = pos[1]
    for n in range(16):
        at = n * QB
        p = pieces[idx[n]]
        v = p * weight_i[0:1, at : at + QB]
        hi = v.astype(BF16)
        vec[0:KV, at : at + QB] = hi
        vec[KV:, at : at + QB] = (v - hi.astype(F32)).astype(BF16)
        p1 = p.astype(BF16)
        r1 = p - p1.astype(F32)
        p2 = r1.astype(BF16)
        parts[0:KV, at : at + QB] = p1
        parts[KV : 2 * KV, at : at + QB] = p2
        parts[2 * KV :, at : at + QB] = (r1 - p2.astype(F32)).astype(BF16)
    s = dot(parts[...], parts[...], NT)
    rows = s[0:KV] + s[KV : 2 * KV] + s[2 * KV :]
    gram = rows[:, 0:KV] + rows[:, KV : 2 * KV] + rows[:, 2 * KV :]
    gram = jnp.concatenate([gram, jnp.zeros((KV, 128 - KV), F32)], axis=1)
    y2 = apply_k(vec, k0, k1)
    split_out(c, y2[0:KV] + y2[KV:], gram, own, away)


def core_sum_kernel(pos, own, away, q0, q1, q2, q3):
    x = pos[0]
    total = own[...] + away[...]
    width = own.shape[1]
    q0_refs = (q0, q1, q2, q3)
    for t in range(4):
        for d in range(4):

            @pl.when((x + d) % 4 == t)
            def _(t=t, d=d):
                q0_refs[d][:, :QB] = total[:, t * QB : (t + 1) * QB]

    if width > CB:
        for ref in q0_refs:
            ref[:, QB:] = total[:, CB:]


def core_add_kernel(own, away, out):
    out[...] = own[...] + away[...]


def eliminate(gram, y):
    row = lax.broadcasted_iota(jnp.int32, (KV, 1), 0)
    for k in range(KV):
        scale = 1.0 / jnp.sqrt(gram[k : k + 1, k : k + 1])
        col = jnp.where(row > k, gram[:, k : k + 1], 0.0) * scale
        g_row = gram[k : k + 1, :] * scale
        y_row = y[k : k + 1, :] * scale
        gram = gram - col * g_row
        y = jnp.where(row == k, y_row, y - col * y_row)
    return y


def quarter_of(ref, x):
    return ref[0:1, pl.ds(pl.multiple_of(x * QB, QB), QB)]


def project_kernel(with_gram, pos, weight_own, q0, q1, q2, q3, out):
    total = (q0[...] + q1[...]) + (q2[...] + q3[...])
    y = total[:, :QB]
    if with_gram:
        y = eliminate(total[:, QB:], y)
    p = y * quarter_of(weight_own, pos[0])
    for n in range(16):
        out[n] = p


def last_kernel(weight_own, q0, q1, q2, q3, proj, grams):
    total = (q0[...] + q1[...]) + (q2[...] + q3[...])
    y = eliminate(total[:, CB:], total[:, :CB])
    p = y * weight_own[...]
    proj[...] = p
    gram = lax.dot_general(p, p, NT, precision=lax.Precision.HIGHEST, preferred_element_type=F32)
    gram = jnp.concatenate([gram, jnp.zeros((KV, 128 - KV), F32)], axis=1)
    for n in range(32):
        grams[n] = gram


def finish_kernel(proj, grams, out):
    gram = grams[0]
    for n in range(1, 32):
        gram = gram + grams[n]
    out[...] = eliminate(gram, proj[...]) * math.sqrt(NTOT)


def device_number(x, z, y, c):
    return (((x % 4) * 4 + z % 4) * 4 + y % 4) * 2 + c % 2


def shift(v, source):
    pairs = [
        (device_number(*source(x, z, y, c)), device_number(x, z, y, c))
        for x in range(4)
        for z in range(4)
        for y in range(4)
        for c in range(2)
    ]
    return lax.ppermute(v, ("x", "z", "y", "c"), pairs)


def from_line(v, d, second=False):
    def source(x, z, y, c):
        along_y = (c == 0) != second
        return (x, z, y + d, c) if along_y else (x, z + d, y, c)

    return shift(v, source)


def from_x(v, d):
    return shift(v, lambda x, z, y, c: (x + d, z, y, c))


def from_y(v, d):
    return shift(v, lambda x, z, y, c: (x, z, y + d, c))


def from_z(v, d):
    return shift(v, lambda x, z, y, c: (x, z + d, y, c))


def from_core(v):
    return shift(v, lambda x, z, y, c: (x, z, y, c + 1))


def body(frames, width_class, start):
    x, z, y, c = (lax.axis_index(a) for a in ("x", "z", "y", "c"))
    pos = jnp.stack([x, c]).astype(jnp.int32)
    second, first = jnp.arange(16, dtype=jnp.int32) // 4, jnp.arange(16, dtype=jnp.int32) % 4
    piece_y = (y + jnp.where(c == 0, first, second)) % 4
    piece_z = (z + jnp.where(c == 0, second, first)) % 4
    idx = (piece_y * 4 + piece_z).astype(jnp.int32)

    piece, mine = call(
        pack_kernel,
        "pack",
        [sds((PROWS, F), BF16), sds((CB + 16, F), BF16)],
        (pos, frames, width_class.reshape(8, 128), start),
    )
    line = [piece] + [from_line(piece, d) for d in (1, 2, 3)]
    other = from_core(mine)
    line = call(stack_kernel, "stack", sds((4, PROWS, F), BF16), line)
    groups = [from_line(line, d, True) for d in (1, 2, 3)]
    aug_j, coef_j, k0, sum_j, sum_i = call(
        gen_a_kernel,
        "rows_a",
        [
            sds((NJ, 2 * F), BF16),
            sds((1, NJ)),
            vmem((4 * QB, NJ), BF16),
            sds((8, NJ)),
            sds((16, QB)),
        ],
        (pos, idx, mine, other, line),
        flops=4 * QB * NJ * 512,
    )
    k1, sum_j, sum_i = pl.pallas_call(
        gen_b_kernel,
        out_shape=[vmem((12 * QB, NJ), BF16), sds((1, NJ)), sds((16, QB))],
        in_specs=[pl.BlockSpec(memory_space=pltpu.SMEM)] * 2 + [pl.BlockSpec(memory_space=VM)] * 7,
        out_specs=[pl.BlockSpec(memory_space=VM)] * 3,
        scratch_shapes=[pltpu.VMEM((8, NJ), F32)],
        compiler_params=pltpu.CompilerParams(vmem_limit_bytes=24 << 20),
        name="rows_b",
    )(pos, idx, *groups, aug_j, coef_j, sum_j, sum_i)

    def sum_sides(on_j, on_i, step):
        j_terms = [on_j, from_core(on_j)]
        i_terms = [on_i] + [from_y(on_i, d) for d in (1, 2, 3)]
        on_j, on_i = call(
            add2_kernel, step, [sds((1, NJ)), sds((16, QB))], (*j_terms, *i_terms)
        )
        j_terms = [on_j] + [from_x(on_j, d) for d in (1, 2, 3)]
        i_terms = [on_i] + [from_z(on_i, d) for d in (1, 2, 3)]
        return (*j_terms, *i_terms)

    def call_big(kernel, name, outs, args, scratch):
        specs = [
            pl.BlockSpec(memory_space=pltpu.SMEM if a.dtype == jnp.int32 else VM) for a in args
        ]
        return pl.pallas_call(
            kernel,
            out_shape=outs,
            in_specs=specs,
            out_specs=[pl.BlockSpec(memory_space=VM)] * len(outs),
            scratch_shapes=scratch,
            compiler_params=pltpu.CompilerParams(vmem_limit_bytes=24 << 20),
            name=name,
        )(*args)

    terms = sum_sides(sum_j, sum_i, "density_sum")
    table, row = pltpu.VMEM((16, QB), F32), pltpu.VMEM((1, NI), F32)
    dens_j, dens_i, sum_j, sum_i = call_big(
        degree_kernel,
        "degree",
        [sds((1, NJ)), sds((16, QB)), sds((1, NJ)), sds((16, QB))],
        (idx, keep(k0), keep(k1), *terms),
        [table, row],
    )
    terms = sum_sides(sum_j, sum_i, "degree_sum")
    own, away, weight_i, weight_own, log_degree = call_big(
        first_kernel,
        "first",
        [sds((KV, CB)), sds((KV, CB)), sds((1, NI)), sds((1, CB)), sds((1, CB))],
        (pos, idx, keep(k0), keep(k1), line, *groups, dens_j, dens_i, *terms),
        [table, row, pltpu.VMEM((KV, NI), BF16)],
    )
    for iteration in range(1, ITERS):
        width = own.shape[1] - CB + QB
        quarters = call(
            core_sum_kernel, f"core_sum{iteration}", [sds((KV, width))] * 4, (pos, own, from_core(away))
        )
        quarters = [quarters[0]] + [from_x(quarters[4 - d], d) for d in (1, 2, 3)]
        pieces = call(
            functools.partial(project_kernel, iteration > 1),
            f"project{iteration}",
            sds((16, KV, QB)),
            (pos, weight_own, *quarters),
        )
        pieces = lax.all_to_all(pieces, ("y", "z"), 0, 0)
        own, away = call_big(
            next_kernel,
            f"next{iteration}",
            [sds((KV, CB + 128)), sds((KV, CB + 128))],
            (pos, idx, keep(k0), keep(k1), weight_i, pieces),
            [pltpu.VMEM((2 * KV, NI), BF16), pltpu.VMEM((3 * KV, NI), BF16)],
        )
    total = call(core_add_kernel, "core_add", sds((KV, CB + 128)), (own, from_core(away)))
    totals = [total] + [from_x(total, d) for d in (1, 2, 3)]
    proj, grams = call(
        last_kernel, "last", [sds((KV, CB)), sds((32, KV, 128))], (weight_own, *totals)
    )
    grams = lax.all_to_all(grams, ("z", "y", "c"), 0, 0)
    embedding = call(finish_kernel, "finish", sds((KV, CB)), (proj, grams))
    return embedding, log_degree.reshape(CB)


def solution(mesh):
    grid = Mesh(mesh.devices.reshape(4, 4, 4, 2), ("x", "z", "y", "c"))
    col = ("z", "y", "c")
    in_specs = (P(col, None), P(col), P(None, col))
    out_specs = (P(None, col), P(col))
    return jax.shard_map(body, mesh=grid, in_specs=in_specs, out_specs=out_specs, check_vma=False)
```

time: 1290 us -> 169 us (0.13)
  waiting for transfers between devices: 917 us -> 23.9 us
  blocking collectives: 270 us -> 37.1 us
  starting transfers between devices: 0.48 us -> 63.6 us
  Pallas kernels: 0 us -> 37.6 us
  matrix products: 34.5 us -> 0 us
  local copies, waits for them, and re-layouts: 23.8 us -> 2.48 us
  other arithmetic: 20.9 us -> 0.09 us
  between operations: 14.4 us -> 1.25 us
    reduce_scatter x3 -> x0, waiting for transfers between devices: 361 us -> none  [apply_kernel(): lax.psum_scatter(partial_value, 'col', scatter_dimension=1, tiled=True)]
    unnamed x14 -> x0, waiting for transfers between devices: 272 us -> none
    psum x5 -> x0, blocking collectives: 215 us -> none  [the longest x3 198 us: body(): lax.psum(jnp.dot(projected, projected.T, precision=lax.Precision.HIGHEST)...]
    all_gather x4 -> x0, waiting for transfers between devices: 158 us -> none  [the longest x3 127 us: apply_kernel(): every_vec = lax.all_gather(vectors, 'col', axis=1, tiled=True)]
    psum x3 -> x0, waiting for transfers between devices: 125 us -> none  [apply_kernel(): return lax.psum(column_part, 'row')]
    ppermute x0 -> x39, starting transfers between devices: none -> 63.6 us  [shift(): return lax.ppermute(v, ('x', 'z', 'y', 'c'), pairs)]
    all_gather x2 -> x0, blocking collectives: 55 us -> none  [the longest x1 28 us: apply_kernel(): every_vec = lax.all_gather(vectors, 'col', axis=1, tiled=True)]
    pallas_call x0 -> x17, Pallas kernels: none -> 37.6 us  [the longest x4 16.8 us: call_big(): pl.pallas_call(kernel, out_shape=outs, in_specs=specs, out_specs=[pl.Bloc...]
  transfers between devices with their start and end apart: 12 -> 39, of which waited for: 12 -> 21; matrix products, arithmetic and copies ran while one was open for 0% -> 0% of each run, Pallas kernels for 0% -> 2%
where the time goes in v1:
time: 169 us; the launch traced here: 166 us
  starting transfers between devices  63.6 us (38%)
  Pallas kernels  37.6 us (22%)
  blocking collectives  37.1 us (22%)
  waiting for transfers between devices  23.9 us (14%)
  local copies, waits for them, and re-layouts  2.48 us (1%)
    ppermute x39, starting transfers between devices, shift(): return lax.ppermute(v, ('x', 'z', 'y', 'c'), pairs)  63.6 us
    ppermute x39, waiting for transfers between devices, shift(): return lax.ppermute(v, ('x', 'z', 'y', 'c'), pairs)  23.9 us
    all_to_all x2, blocking collectives, body(): pieces = lax.all_to_all(pieces, ('y', 'z'), 0, 0)  23.2 us
    pallas_call x4, Pallas kernels, call_big(): pl.pallas_call(kernel, out_shape=outs, in_specs=specs, out_specs=[pl.Bloc...  16.8 us
    all_to_all x1, blocking collectives, body(): grams = lax.all_to_all(grams, ('z', 'y', 'c'), 0, 0)  13.9 us
    pallas_call x12, Pallas kernels, call(): pl.pallas_call(kernel, out_shape=outs, in_specs=[spec(a) for a in args],...  12.1 us
    pallas_call x1, Pallas kernels, body(): pl.pallas_call(gen_b_kernel, out_shape=[vmem((12 * QB, NJ), BF16), sds((1...  8.73 us
  transfers between devices with their start and end apart: 39, of which 21 were waited for; matrix products, arithmetic and copies ran while one was open for 0% of the time, Pallas kernels for 2%

profile of v1, /device:TPU:1, one launch (start us, length us, event | category | flops | bytes accessed | tf_op | source)
XLA Modules:
  0.0 166.1 jit_solution(10760858989728748799)
XLA Ops:
  3.8 2.5 %collective-permute-start.3 = (bf16[336,128]{1,0:T(8,128)(2,1)S(1)}, bf16[336,128]{1,0:T(8,128)(2,1)S(1)}, u32[]{:S(2)}, u32[]{:S(2)}) collective-permute-start(bf16[336,128]{1,0:T(8,128)(2,1)S(1)} %get-tuple-element.40.a), channel_id=1, source_target_pairs={{6,0},{25,1},{0,2},{27,3},{2,4},{29,5},{4,6},{31,7},{14,8},{1,9},{... | collective-permute-start | bytes 258056 | tf_op jit(solution)/shard_map/ppermute | solution.py:367
  6.3 3.3 %collective-permute-start.2 = (bf16[336,128]{1,0:T(8,128)(2,1)S(1)}, bf16[336,128]{1,0:T(8,128)(2,1)S(1)}, u32[]{:S(2)}, u32[]{:S(2)}) collective-permute-start(bf16[336,128]{1,0:T(8,128)(2,1)S(1)} %get-tuple-element.40.a), channel_id=1, source_target_pairs={{4,0},{17,1},{6,2},{19,3},{0,4},{21,5},{2,6},{23,7},{12,8},{25,9},... | collective-permute-start | bytes 258056 | tf_op jit(solution)/shard_map/ppermute | solution.py:367
  11.2 1.5 collective-permute-done.2.c
  14.3 2.9 %collective-permute-start.5 = (bf16[4,336,128]{2,1,0:T(8,128)(2,1)S(1)}, bf16[4,336,128]{2,1,0:T(8,128)(2,1)S(1)}, u32[]{:S(2)}, u32[]{:S(2)}) collective-permute-start(bf16[4,336,128]{2,1,0:T(8,128)(2,1)S(1)} %stack.13.line), channel_id=1, source_target_pairs={{16,0},{5,1},{18,2},{7,3},{20,4},{1,5},{22,6},{3,7},{24,8},{13,9},... | collective-permute-start | bytes 1032200 | tf_op jit(solution)/shard_map/ppermute | solution.py:367
  18.0 4.0 %rows_a.1 = (bf16[2048,256]{1,0:T(8,128)(2,1)S(1)}, f32[1,2048]{1,0:T(1,128)S(1)}, bf16[1024,2048]{1,0:T(8,128)(2,1)S(1)}, f32[8,2048]{1,0:T(8,128)S(1)}, f32[16,256]{1,0:T(8,128)S(1)}) custom-call(s32[2]{0:T(128)S(1)} %pad_add_fusion.pos, s32[16]{0:T(128)S(1)} %fusion.idx, bf16[1040,128]{1,0:T(8,128)(2,1)S(1)} %get-tuple-element.39.mine, ...), custom_call_target="tpu_custom_call" | custom-call | flops 1073741824 | tf_op jit(solution)/shard_map/rows_a/pallas_call | solution.py:43
  22.1 3.8 %collective-permute-done.5.g2 = bf16[4,336,128]{2,1,0:T(8,128)(2,1)S(1)} collective-permute-done((bf16[4,336,128]{2,1,0:T(8,128)(2,1)S(1)}, bf16[4,336,128]{2,1,0:T(8,128)(2,1)S(1)}, u32[]{:S(2)}, u32[]{:S(2)}) %collective-permute-start.5) | collective-permute-done | bytes 344096 | tf_op jit(solution)/shard_map/ppermute | solution.py:367
  25.9 8.7 %rows_b.1 = (bf16[3072,2048]{1,0:T(8,128)(2,1)S(1)}, f32[1,2048]{1,0:T(1,128)S(1)}, f32[16,256]{1,0:T(8,128)S(1)}) custom-call(s32[2]{0:T(128)S(1)} %pad_add_fusion.pos, s32[16]{0:T(128)S(1)} %fusion.idx, bf16[4,336,128]{2,1,0:T(8,128)(2,1)S(1)} %collective-permute-done.4.g1, bf16[4,336,128]{2,1,0:T(8,128)(2,1)S(1)} %collective-permute-done.5.g2, ...), custom_call_target="tpu_custom_call" | custom-call | tf_op jit(solution)/shard_map/rows_b/pallas_call | solution.py:425
  35.6 2.1 %collective-permute-start.9 = (f32[16,256]{1,0:T(8,128)S(1)}, f32[16,256]{1,0:T(8,128)S(1)}, u32[]{:S(2)}, u32[]{:S(2)}) collective-permute-start(f32[16,256]{1,0:T(8,128)S(1)} %get-tuple-element.48.b0), channel_id=1, source_target_pairs={{4,0},{5,1},{6,2},{7,3},{0,4},{1,5},{2,6},{3,7},{12,8},{13,9},{14,... | collective-permute-start | bytes 49160 | tf_op jit(solution)/shard_map/ppermute | solution.py:367
  38.7 3.2 %collective-permute-start.7 = (f32[1,2048]{1,0:T(1,128)S(1)}, f32[1,2048]{1,0:T(1,128)S(1)}, u32[]{:S(2)}, u32[]{:S(2)}) collective-permute-start(f32[1,2048]{1,0:T(1,128)S(1)} %get-tuple-element.47.a0), channel_id=1, source_target_pairs={{1,0},{0,1},{3,2},{2,3},{5,4},{4,5},{7,6},{6,7},{9,8},{8,9},{11,10... | collective-permute-start | bytes 24584 | tf_op jit(solution)/shard_map/ppermute | solution.py:367
  42.8 1.5 collective-permute-start.13
  45.5 1.8 %collective-permute-start.15 = (f32[16,256]{1,0:T(8,128)S(1)}, f32[16,256]{1,0:T(8,128)S(1)}, u32[]{:S(2)}, u32[]{:S(2)}) collective-permute-start(f32[16,256]{1,0:T(8,128)S(1)} %get-tuple-element.50.i0), channel_id=1, source_target_pairs={{16,0},{17,1},{18,2},{19,3},{20,4},{21,5},{22,6},{23,7},{24,8},{25... | collective-permute-start | bytes 49160 | tf_op jit(solution)/shard_map/ppermute | solution.py:367
  48.6 2.4 %collective-permute-start.12 = (f32[1,2048]{1,0:T(1,128)S(1)}, f32[1,2048]{1,0:T(1,128)S(1)}, u32[]{:S(2)}, u32[]{:S(2)}) collective-permute-start(f32[1,2048]{1,0:T(1,128)S(1)} %get-tuple-element.49.j0), channel_id=1, source_target_pairs={{64,0},{65,1},{66,2},{67,3},{68,4},{69,5},{70,6},{71,7},{72,8},{73... | collective-permute-start | bytes 24584 | tf_op jit(solution)/shard_map/ppermute | solution.py:367
  53.6 7.1 %degree.1 = (f32[1,2048]{1,0:T(1,128)S(1)}, f32[16,256]{1,0:T(8,128)S(1)}, f32[1,2048]{1,0:T(1,128)S(1)}, f32[16,256]{1,0:T(8,128)S(1)}) custom-call(s32[16]{0:T(128)S(1)} %fusion.idx, bf16[1024,2048]{1,0:T(8,128)(2,1)S(1)} %get-tuple-element.41.k0, bf16[3072,2048]{1,0:T(8,128)(2,1)S(1)} %get-tuple-element.46.k1, f32[1,2048]{1,0:T(1,128)S(1)} %get-tuple-element.49.j0, ...), custom_call_target="tpu_custom_call" | custom-call | tf_op jit(solution)/shard_map/degree/pallas_call | solution.py:449
  62.6 2.0 %collective-permute-start.18 = (f32[16,256]{1,0:T(8,128)S(1)}, f32[16,256]{1,0:T(8,128)S(1)}, u32[]{:S(2)}, u32[]{:S(2)}) collective-permute-start(f32[16,256]{1,0:T(8,128)S(1)} %get-tuple-element.54.b0), channel_id=1, source_target_pairs={{2,0},{3,1},{4,2},{5,3},{6,4},{7,5},{0,6},{1,7},{10,8},{11,9},{12,... | collective-permute-start | bytes 49160 | tf_op jit(solution)/shard_map/ppermute | solution.py:367
  64.6 5.4 %collective-permute-start.17 = (f32[1,2048]{1,0:T(1,128)S(1)}, f32[1,2048]{1,0:T(1,128)S(1)}, u32[]{:S(2)}, u32[]{:S(2)}) collective-permute-start(f32[1,2048]{1,0:T(1,128)S(1)} %get-tuple-element.53.a0), channel_id=1, source_target_pairs={{1,0},{0,1},{3,2},{2,3},{5,4},{4,5},{7,6},{6,7},{9,8},{8,9},{11,10... | collective-permute-start | bytes 24584 | tf_op jit(solution)/shard_map/ppermute | solution.py:367
  73.8 3.5 %collective-permute-start.22 = (f32[1,2048]{1,0:T(1,128)S(1)}, f32[1,2048]{1,0:T(1,128)S(1)}, u32[]{:S(2)}, u32[]{:S(2)}) collective-permute-start(f32[1,2048]{1,0:T(1,128)S(1)} %get-tuple-element.55.j0), channel_id=1, source_target_pairs={{64,0},{65,1},{66,2},{67,3},{68,4},{69,5},{70,6},{71,7},{72,8},{73... | collective-permute-start | bytes 24584 | tf_op jit(solution)/shard_map/ppermute | solution.py:367
  79.8 3.5 %first.1 = (f32[16,1024]{1,0:T(8,128)S(1)}, f32[16,1024]{1,0:T(8,128)S(1)}, f32[1,4096]{1,0:T(1,128)S(1)}, f32[1,1024]{1,0:T(1,128)S(1)}, f32[1,1024]{1,0:T(1,128)}) custom-call(s32[2]{0:T(128)S(1)} %pad_add_fusion.pos, s32[16]{0:T(128)S(1)} %fusion.idx, bf16[1024,2048]{1,0:T(8,128)(2,1)S(1)} %get-tuple-element.41.k0, ...), custom_call_target="tpu_custom_call" | custom-call | tf_op jit(solution)/shard_map/first/pallas_call | solution.py:449
  83.3 4.3 %collective-permute-start.27 = (f32[16,1024]{1,0:T(8,128)S(1)}, f32[16,1024]{1,0:T(8,128)S(1)}, u32[]{:S(2)}, u32[]{:S(2)}) collective-permute-start(f32[16,1024]{1,0:T(8,128)S(1)} %get-tuple-element.60), channel_id=1, source_target_pairs={{1,0},{0,1},{3,2},{2,3},{5,4},{4,5},{7,6},{6,7},{9,8},{8,9},{11,10... | collective-permute-start | bytes 196616 | tf_op jit(solution)/shard_map/ppermute | solution.py:367
  91.8 2.5 %collective-permute-done.29.q2 = f32[16,256]{1,0:T(8,128)S(1)} collective-permute-done((f32[16,256]{1,0:T(8,128)S(1)}, f32[16,256]{1,0:T(8,128)S(1)}, u32[]{:S(2)}, u32[]{:S(2)}) %collective-permute-start.29) | collective-permute-done | bytes 16416 | tf_op jit(solution)/shard_map/ppermute | solution.py:367
  95.3 12.6 %all_to_all.15.pieces = f32[16,16,256]{2,1,0:T(8,128)S(1)} all-to-all(f32[16,16,256]{2,1,0:T(8,128)S(1)} %project1.1), channel_id=1, replica_groups=mesh['x'=4,'z'=4,'y'=4,'c'=2] {'y','z'}, dimensions={0} | all-to-all | bytes 524288 | tf_op jit(solution)/shard_map/all_to_all | solution.py:488
  107.9 3.1 %next1.1 = (f32[16,1152]{1,0:T(8,128)S(1)}, f32[16,1152]{1,0:T(8,128)S(1)}) custom-call(s32[2]{0:T(128)S(1)} %pad_add_fusion.pos, s32[16]{0:T(128)S(1)} %fusion.idx, bf16[1024,2048]{1,0:T(8,128)(2,1)S(1)} %get-tuple-element.41.k0, bf16[3072,2048]{1,0:T(8,128)(2,1)S(1)} %get-tuple-element.46.k1, f32[1,4096]{1,0:T(1,128)S(1)} %get-tuple-element.58.weight_i, ...), custom_call_target="tpu_custom_call" | custom-call | tf_op jit(solution)/shard_map/next1/pallas_call | solution.py:449
  111.0 3.4 %collective-permute-start.31 = (f32[16,1152]{1,0:T(8,128)S(1)}, f32[16,1152]{1,0:T(8,128)S(1)}, u32[]{:S(2)}, u32[]{:S(2)}) collective-permute-start(f32[16,1152]{1,0:T(8,128)S(1)} %get-tuple-element.66), channel_id=1, source_target_pairs={{1,0},{0,1},{3,2},{2,3},{5,4},{4,5},{7,6},{6,7},{9,8},{8,9},{11,10... | collective-permute-start | bytes 221192 | tf_op jit(solution)/shard_map/ppermute | solution.py:367
  118.7 2.7 %collective-permute-done.33.q2 = f32[16,384]{1,0:T(8,128)S(1)} collective-permute-done((f32[16,384]{1,0:T(8,128)S(1)}, f32[16,384]{1,0:T(8,128)S(1)}, u32[]{:S(2)}, u32[]{:S(2)}) %collective-permute-start.33) | collective-permute-done | bytes 24608 | tf_op jit(solution)/shard_map/ppermute | solution.py:367
  121.6 1.9 %project2.1 = f32[16,16,256]{2,1,0:T(8,128)S(1)} custom-call(s32[2]{0:T(128)S(1)} %pad_add_fusion.pos, f32[1,1024]{1,0:T(1,128)S(1)} %get-tuple-element.57.weight_own, f32[16,384]{1,0:T(8,128)S(1)} %get-tuple-element.67.q0, f32[16,384]{1,0:T(8,128)S(1)} %collective-permute-done.32.q1, f32[16,384]{1,0:T(8,128)S(1)} %collective-permute-done.33.q2, ...), custom_call_target="tpu_custom_call" | custom-call | tf_op jit(solution)/shard_map/project2/pallas_call | solution.py:43
  123.6 10.6 %all_to_all.16.pieces = f32[16,16,256]{2,1,0:T(8,128)S(1)} all-to-all(f32[16,16,256]{2,1,0:T(8,128)S(1)} %project2.1), channel_id=1, replica_groups=mesh['x'=4,'z'=4,'y'=4,'c'=2] {'y','z'}, dimensions={0} | all-to-all | bytes 524288 | tf_op jit(solution)/shard_map/all_to_all | solution.py:488
  134.1 3.1 %next2.1 = (f32[16,1152]{1,0:T(8,128)S(1)}, f32[16,1152]{1,0:T(8,128)S(1)}) custom-call(s32[2]{0:T(128)S(1)} %pad_add_fusion.pos, s32[16]{0:T(128)S(1)} %fusion.idx, bf16[1024,2048]{1,0:T(8,128)(2,1)S(1)} %get-tuple-element.41.k0, bf16[3072,2048]{1,0:T(8,128)(2,1)S(1)} %get-tuple-element.46.k1, f32[1,4096]{1,0:T(1,128)S(1)} %get-tuple-element.58.weight_i, ...), custom_call_target="tpu_custom_call" | custom-call | tf_op jit(solution)/shard_map/next2/pallas_call | solution.py:449
  137.2 3.3 %collective-permute-start.35 = (f32[16,1152]{1,0:T(8,128)S(1)}, f32[16,1152]{1,0:T(8,128)S(1)}, u32[]{:S(2)}, u32[]{:S(2)}) collective-permute-start(f32[16,1152]{1,0:T(8,128)S(1)} %get-tuple-element.72), channel_id=1, source_target_pairs={{1,0},{0,1},{3,2},{2,3},{5,4},{4,5},{7,6},{6,7},{9,8},{8,9},{11,10... | collective-permute-start | bytes 221192 | tf_op jit(solution)/shard_map/ppermute | solution.py:367
  141.5 2.3 %collective-permute-start.37 = (f32[16,1152]{1,0:T(8,128)S(1)}, f32[16,1152]{1,0:T(8,128)S(1)}, u32[]{:S(2)}, u32[]{:S(2)}) collective-permute-start(f32[16,1152]{1,0:T(8,128)S(1)} %core_add.1.q0), channel_id=1, source_target_pairs={{64,0},{65,1},{66,2},{67,3},{68,4},{69,5},{70,6},{71,7},{72,8},{73... | collective-permute-start | bytes 221192 | tf_op jit(solution)/shard_map/ppermute | solution.py:367
  144.9 2.1 %collective-permute-done.38.q3 = f32[16,1152]{1,0:T(8,128)S(1)} collective-permute-done((f32[16,1152]{1,0:T(8,128)S(1)}, f32[16,1152]{1,0:T(8,128)S(1)}, u32[]{:S(2)}, u32[]{:S(2)}) %collective-permute-start.38) | collective-permute-done | bytes 73760 | tf_op jit(solution)/shard_map/ppermute | solution.py:367
  148.0 1.6 last.1
  149.7 13.9 %all_to_all.17.grams = f32[32,16,128]{2,1,0:T(8,128)S(1)} all-to-all(f32[32,16,128]{2,1,0:T(8,128)S(1)} %get-tuple-element.74), channel_id=1, replica_groups=mesh['x'=4,'z'=4,'y'=4,'c'=2] {'z','y','c'}, dimensions={0} | all-to-all | bytes 524288 | tf_op jit(solution)/shard_map/all_to_all | solution.py:501
  163.6 2.1 %finish.1 = f32[16,1024]{1,0:T(8,128)} custom-call(f32[16,1024]{1,0:T(8,128)S(1)} %get-tuple-element.73.proj, f32[32,16,128]{2,1,0:T(8,128)S(1)} %all_to_all.17.grams), custom_call_target="tpu_custom_call" | custom-call | tf_op jit(solution)/shard_map/finish/pallas_call | solution.py:43
  (74 shorter events, 36.1 us)
Async XLA Ops:
  3.8 7.4 %collective-permute-start.3 = (bf16[336,128]{1,0:T(8,128)(2,1)S(1)}, bf16[336,128]{1,0:T(8,128)(2,1)S(1)}, u32[]{:S(2)}, u32[]{:S(2)}) collective-permute-start(bf16[336,128]{1,0:T(8,128)(2,1)S(1)} %get-tuple-element.40.a), channel_id=1, source_target_pairs={{6,0},{25,1},{0,2},{27,3},{2,4},{29,5},{4,6},{31,7},{14,8},{1,9},{... | collective-permute-start | bytes 258056 | tf_op jit(solution)/shard_map/ppermute | solution.py:367
  6.3 6.4 %collective-permute-start.2 = (bf16[336,128]{1,0:T(8,128)(2,1)S(1)}, bf16[336,128]{1,0:T(8,128)(2,1)S(1)}, u32[]{:S(2)}, u32[]{:S(2)}) collective-permute-start(bf16[336,128]{1,0:T(8,128)(2,1)S(1)} %get-tuple-element.40.a), channel_id=1, source_target_pairs={{4,0},{17,1},{6,2},{19,3},{0,4},{21,5},{2,6},{23,7},{12,8},{25,9},... | collective-permute-start | bytes 258056 | tf_op jit(solution)/shard_map/ppermute | solution.py:367
  10.3 7.7 %collective-permute-start = (bf16[1040,128]{1,0:T(8,128)(2,1)S(1)}, bf16[1040,128]{1,0:T(8,128)(2,1)S(1)}, u32[]{:S(2)}, u32[]{:S(2)}) collective-permute-start(bf16[1040,128]{1,0:T(8,128)(2,1)S(1)} %get-tuple-element.39.mine), channel_id=1, source_target_pairs={{1,0},{0,1},{3,2},{2,3},{5,4},{4,5},{7,6},{6,7},{9,8},{8,9},{11,10... | collective-permute-start | bytes 798728 | tf_op jit(solution)/shard_map/ppermute | solution.py:367
  13.3 8.8 %collective-permute-start.6 = (bf16[4,336,128]{2,1,0:T(8,128)(2,1)S(1)}, bf16[4,336,128]{2,1,0:T(8,128)(2,1)S(1)}, u32[]{:S(2)}, u32[]{:S(2)}) collective-permute-start(bf16[4,336,128]{2,1,0:T(8,128)(2,1)S(1)} %stack.13.line), channel_id=1, source_target_pairs={{24,0},{7,1},{26,2},{1,3},{28,4},{3,5},{30,6},{5,7},{0,8},{15,9},{... | collective-permute-start | bytes 1032200 | tf_op jit(solution)/shard_map/ppermute | solution.py:367
  14.3 11.5 %collective-permute-start.5 = (bf16[4,336,128]{2,1,0:T(8,128)(2,1)S(1)}, bf16[4,336,128]{2,1,0:T(8,128)(2,1)S(1)}, u32[]{:S(2)}, u32[]{:S(2)}) collective-permute-start(bf16[4,336,128]{2,1,0:T(8,128)(2,1)S(1)} %stack.13.line), channel_id=1, source_target_pairs={{16,0},{5,1},{18,2},{7,3},{20,4},{1,5},{22,6},{3,7},{24,8},{13,9},... | collective-permute-start | bytes 1032200 | tf_op jit(solution)/shard_map/ppermute | solution.py:367
  17.2 8.6 %collective-permute-start.4 = (bf16[4,336,128]{2,1,0:T(8,128)(2,1)S(1)}, bf16[4,336,128]{2,1,0:T(8,128)(2,1)S(1)}, u32[]{:S(2)}, u32[]{:S(2)}) collective-permute-start(bf16[4,336,128]{2,1,0:T(8,128)(2,1)S(1)} %stack.13.line), channel_id=1, source_target_pairs={{8,0},{3,1},{10,2},{5,3},{12,4},{7,5},{14,6},{1,7},{16,8},{11,9},{... | collective-permute-start | bytes 1032200 | tf_op jit(solution)/shard_map/ppermute | solution.py:367
  34.6 8.2 %collective-permute-start.10 = (f32[16,256]{1,0:T(8,128)S(1)}, f32[16,256]{1,0:T(8,128)S(1)}, u32[]{:S(2)}, u32[]{:S(2)}) collective-permute-start(f32[16,256]{1,0:T(8,128)S(1)} %get-tuple-element.48.b0), channel_id=1, source_target_pairs={{6,0},{7,1},{0,2},{1,3},{2,4},{3,5},{4,6},{5,7},{14,8},{15,9},{8,1... | collective-permute-start | bytes 49160 | tf_op jit(solution)/shard_map/ppermute | solution.py:367
  35.6 7.2 %collective-permute-start.9 = (f32[16,256]{1,0:T(8,128)S(1)}, f32[16,256]{1,0:T(8,128)S(1)}, u32[]{:S(2)}, u32[]{:S(2)}) collective-permute-start(f32[16,256]{1,0:T(8,128)S(1)} %get-tuple-element.48.b0), channel_id=1, source_target_pairs={{4,0},{5,1},{6,2},{7,3},{0,4},{1,5},{2,6},{3,7},{12,8},{13,9},{14,... | collective-permute-start | bytes 49160 | tf_op jit(solution)/shard_map/ppermute | solution.py:367
  37.7 5.1 %collective-permute-start.8 = (f32[16,256]{1,0:T(8,128)S(1)}, f32[16,256]{1,0:T(8,128)S(1)}, u32[]{:S(2)}, u32[]{:S(2)}) collective-permute-start(f32[16,256]{1,0:T(8,128)S(1)} %get-tuple-element.48.b0), channel_id=1, source_target_pairs={{2,0},{3,1},{4,2},{5,3},{6,4},{7,5},{0,6},{1,7},{10,8},{11,9},{12,... | collective-permute-start | bytes 49160 | tf_op jit(solution)/shard_map/ppermute | solution.py:367
  38.7 4.0 %collective-permute-start.7 = (f32[1,2048]{1,0:T(1,128)S(1)}, f32[1,2048]{1,0:T(1,128)S(1)}, u32[]{:S(2)}, u32[]{:S(2)}) collective-permute-start(f32[1,2048]{1,0:T(1,128)S(1)} %get-tuple-element.47.a0), channel_id=1, source_target_pairs={{1,0},{0,1},{3,2},{2,3},{5,4},{4,5},{7,6},{6,7},{9,8},{8,9},{11,10... | collective-permute-start | bytes 24584 | tf_op jit(solution)/shard_map/ppermute | solution.py:367
  42.8 8.2 %collective-permute-start.13 = (f32[1,2048]{1,0:T(1,128)S(1)}, f32[1,2048]{1,0:T(1,128)S(1)}, u32[]{:S(2)}, u32[]{:S(2)}) collective-permute-start(f32[1,2048]{1,0:T(1,128)S(1)} %get-tuple-element.49.j0), channel_id=1, source_target_pairs={{96,0},{97,1},{98,2},{99,3},{100,4},{101,5},{102,6},{103,7},{104,8... | collective-permute-start | bytes 24584 | tf_op jit(solution)/shard_map/ppermute | solution.py:367
  44.3 9.3 %collective-permute-start.16 = (f32[16,256]{1,0:T(8,128)S(1)}, f32[16,256]{1,0:T(8,128)S(1)}, u32[]{:S(2)}, u32[]{:S(2)}) collective-permute-start(f32[16,256]{1,0:T(8,128)S(1)} %get-tuple-element.50.i0), channel_id=1, source_target_pairs={{24,0},{25,1},{26,2},{27,3},{28,4},{29,5},{30,6},{31,7},{0,8},{1,9... | collective-permute-start | bytes 49160 | tf_op jit(solution)/shard_map/ppermute | solution.py:367
  45.5 8.0 %collective-permute-start.15 = (f32[16,256]{1,0:T(8,128)S(1)}, f32[16,256]{1,0:T(8,128)S(1)}, u32[]{:S(2)}, u32[]{:S(2)}) collective-permute-start(f32[16,256]{1,0:T(8,128)S(1)} %get-tuple-element.50.i0), channel_id=1, source_target_pairs={{16,0},{17,1},{18,2},{19,3},{20,4},{21,5},{22,6},{23,7},{24,8},{25... | collective-permute-start | bytes 49160 | tf_op jit(solution)/shard_map/ppermute | solution.py:367
  47.4 6.2 %collective-permute-start.14 = (f32[16,256]{1,0:T(8,128)S(1)}, f32[16,256]{1,0:T(8,128)S(1)}, u32[]{:S(2)}, u32[]{:S(2)}) collective-permute-start(f32[16,256]{1,0:T(8,128)S(1)} %get-tuple-element.50.i0), channel_id=1, source_target_pairs={{8,0},{9,1},{10,2},{11,3},{12,4},{13,5},{14,6},{15,7},{16,8},{17,9... | collective-permute-start | bytes 49160 | tf_op jit(solution)/shard_map/ppermute | solution.py:367
  60.7 10.1 %collective-permute-start.20 = (f32[16,256]{1,0:T(8,128)S(1)}, f32[16,256]{1,0:T(8,128)S(1)}, u32[]{:S(2)}, u32[]{:S(2)}) collective-permute-start(f32[16,256]{1,0:T(8,128)S(1)} %get-tuple-element.54.b0), channel_id=1, source_target_pairs={{6,0},{7,1},{0,2},{1,3},{2,4},{3,5},{4,6},{5,7},{14,8},{15,9},{8,1... | collective-permute-start | bytes 49160 | tf_op jit(solution)/shard_map/ppermute | solution.py:367
  62.2 8.7 %collective-permute-start.19 = (f32[16,256]{1,0:T(8,128)S(1)}, f32[16,256]{1,0:T(8,128)S(1)}, u32[]{:S(2)}, u32[]{:S(2)}) collective-permute-start(f32[16,256]{1,0:T(8,128)S(1)} %get-tuple-element.54.b0), channel_id=1, source_target_pairs={{4,0},{5,1},{6,2},{7,3},{0,4},{1,5},{2,6},{3,7},{12,8},{13,9},{14,... | collective-permute-start | bytes 49160 | tf_op jit(solution)/shard_map/ppermute | solution.py:367
  62.6 8.3 %collective-permute-start.18 = (f32[16,256]{1,0:T(8,128)S(1)}, f32[16,256]{1,0:T(8,128)S(1)}, u32[]{:S(2)}, u32[]{:S(2)}) collective-permute-start(f32[16,256]{1,0:T(8,128)S(1)} %get-tuple-element.54.b0), channel_id=1, source_target_pairs={{2,0},{3,1},{4,2},{5,3},{6,4},{7,5},{0,6},{1,7},{10,8},{11,9},{12,... | collective-permute-start | bytes 49160 | tf_op jit(solution)/shard_map/ppermute | solution.py:367
  64.6 6.2 %collective-permute-start.17 = (f32[1,2048]{1,0:T(1,128)S(1)}, f32[1,2048]{1,0:T(1,128)S(1)}, u32[]{:S(2)}, u32[]{:S(2)}) collective-permute-start(f32[1,2048]{1,0:T(1,128)S(1)} %get-tuple-element.53.a0), channel_id=1, source_target_pairs={{1,0},{0,1},{3,2},{2,3},{5,4},{4,5},{7,6},{6,7},{9,8},{8,9},{11,10... | collective-permute-start | bytes 24584 | tf_op jit(solution)/shard_map/ppermute | solution.py:367
  70.9 6.4 %collective-permute-start.23 = (f32[1,2048]{1,0:T(1,128)S(1)}, f32[1,2048]{1,0:T(1,128)S(1)}, u32[]{:S(2)}, u32[]{:S(2)}) collective-permute-start(f32[1,2048]{1,0:T(1,128)S(1)} %get-tuple-element.55.j0), channel_id=1, source_target_pairs={{96,0},{97,1},{98,2},{99,3},{100,4},{101,5},{102,6},{103,7},{104,8... | collective-permute-start | bytes 24584 | tf_op jit(solution)/shard_map/ppermute | solution.py:367
  70.9 8.9 %collective-permute-start.26 = (f32[16,256]{1,0:T(8,128)S(1)}, f32[16,256]{1,0:T(8,128)S(1)}, u32[]{:S(2)}, u32[]{:S(2)}) collective-permute-start(f32[16,256]{1,0:T(8,128)S(1)} %get-tuple-element.56.i0), channel_id=1, source_target_pairs={{24,0},{25,1},{26,2},{27,3},{28,4},{29,5},{30,6},{31,7},{0,8},{1,9... | collective-permute-start | bytes 49160 | tf_op jit(solution)/shard_map/ppermute | solution.py:367
  71.2 8.6 %collective-permute-start.25 = (f32[16,256]{1,0:T(8,128)S(1)}, f32[16,256]{1,0:T(8,128)S(1)}, u32[]{:S(2)}, u32[]{:S(2)}) collective-permute-start(f32[16,256]{1,0:T(8,128)S(1)} %get-tuple-element.56.i0), channel_id=1, source_target_pairs={{16,0},{17,1},{18,2},{19,3},{20,4},{21,5},{22,6},{23,7},{24,8},{25... | collective-permute-start | bytes 49160 | tf_op jit(solution)/shard_map/ppermute | solution.py:367
  72.4 7.4 %collective-permute-start.24 = (f32[16,256]{1,0:T(8,128)S(1)}, f32[16,256]{1,0:T(8,128)S(1)}, u32[]{:S(2)}, u32[]{:S(2)}) collective-permute-start(f32[16,256]{1,0:T(8,128)S(1)} %get-tuple-element.56.i0), channel_id=1, source_target_pairs={{8,0},{9,1},{10,2},{11,3},{12,4},{13,5},{14,6},{15,7},{16,8},{17,9... | collective-permute-start | bytes 49160 | tf_op jit(solution)/shard_map/ppermute | solution.py:367
  73.8 4.5 %collective-permute-start.22 = (f32[1,2048]{1,0:T(1,128)S(1)}, f32[1,2048]{1,0:T(1,128)S(1)}, u32[]{:S(2)}, u32[]{:S(2)}) collective-permute-start(f32[1,2048]{1,0:T(1,128)S(1)} %get-tuple-element.55.j0), channel_id=1, source_target_pairs={{64,0},{65,1},{66,2},{67,3},{68,4},{69,5},{70,6},{71,7},{72,8},{73... | collective-permute-start | bytes 24584 | tf_op jit(solution)/shard_map/ppermute | solution.py:367
  83.3 5.2 %collective-permute-start.27 = (f32[16,1024]{1,0:T(8,128)S(1)}, f32[16,1024]{1,0:T(8,128)S(1)}, u32[]{:S(2)}, u32[]{:S(2)}) collective-permute-start(f32[16,1024]{1,0:T(8,128)S(1)} %get-tuple-element.60), channel_id=1, source_target_pairs={{1,0},{0,1},{3,2},{2,3},{5,4},{4,5},{7,6},{6,7},{9,8},{8,9},{11,10... | collective-permute-start | bytes 196616 | tf_op jit(solution)/shard_map/ppermute | solution.py:367
  90.2 4.1 %collective-permute-start.29 = (f32[16,256]{1,0:T(8,128)S(1)}, f32[16,256]{1,0:T(8,128)S(1)}, u32[]{:S(2)}, u32[]{:S(2)}) collective-permute-start(f32[16,256]{1,0:T(8,128)S(1)} %get-tuple-element.63), channel_id=1, source_target_pairs={{64,0},{65,1},{66,2},{67,3},{68,4},{69,5},{70,6},{71,7},{72,8},{73... | collective-permute-start | bytes 49160 | tf_op jit(solution)/shard_map/ppermute | solution.py:367
  111.0 4.3 %collective-permute-start.31 = (f32[16,1152]{1,0:T(8,128)S(1)}, f32[16,1152]{1,0:T(8,128)S(1)}, u32[]{:S(2)}, u32[]{:S(2)}) collective-permute-start(f32[16,1152]{1,0:T(8,128)S(1)} %get-tuple-element.66), channel_id=1, source_target_pairs={{1,0},{0,1},{3,2},{2,3},{5,4},{4,5},{7,6},{6,7},{9,8},{8,9},{11,10... | collective-permute-start | bytes 221192 | tf_op jit(solution)/shard_map/ppermute | solution.py:367
  117.2 4.2 %collective-permute-start.33 = (f32[16,384]{1,0:T(8,128)S(1)}, f32[16,384]{1,0:T(8,128)S(1)}, u32[]{:S(2)}, u32[]{:S(2)}) collective-permute-start(f32[16,384]{1,0:T(8,128)S(1)} %get-tuple-element.69), channel_id=1, source_target_pairs={{64,0},{65,1},{66,2},{67,3},{68,4},{69,5},{70,6},{71,7},{72,8},{73... | collective-permute-start | bytes 73736 | tf_op jit(solution)/shard_map/ppermute | solution.py:367
  117.6 4.1 %collective-permute-start.34 = (f32[16,384]{1,0:T(8,128)S(1)}, f32[16,384]{1,0:T(8,128)S(1)}, u32[]{:S(2)}, u32[]{:S(2)}) collective-permute-start(f32[16,384]{1,0:T(8,128)S(1)} %get-tuple-element.70), channel_id=1, source_target_pairs={{96,0},{97,1},{98,2},{99,3},{100,4},{101,5},{102,6},{103,7},{104,8... | collective-permute-start | bytes 73736 | tf_op jit(solution)/shard_map/ppermute | solution.py:367
  137.2 4.2 %collective-permute-start.35 = (f32[16,1152]{1,0:T(8,128)S(1)}, f32[16,1152]{1,0:T(8,128)S(1)}, u32[]{:S(2)}, u32[]{:S(2)}) collective-permute-start(f32[16,1152]{1,0:T(8,128)S(1)} %get-tuple-element.72), channel_id=1, source_target_pairs={{1,0},{0,1},{3,2},{2,3},{5,4},{4,5},{7,6},{6,7},{9,8},{8,9},{11,10... | collective-permute-start | bytes 221192 | tf_op jit(solution)/shard_map/ppermute | solution.py:367
  141.4 5.6 %collective-permute-start.38 = (f32[16,1152]{1,0:T(8,128)S(1)}, f32[16,1152]{1,0:T(8,128)S(1)}, u32[]{:S(2)}, u32[]{:S(2)}) collective-permute-start(f32[16,1152]{1,0:T(8,128)S(1)} %core_add.1.q0), channel_id=1, source_target_pairs={{96,0},{97,1},{98,2},{99,3},{100,4},{101,5},{102,6},{103,7},{104,8... | collective-permute-start | bytes 221192 | tf_op jit(solution)/shard_map/ppermute | solution.py:367
  141.5 5.6 %collective-permute-start.37 = (f32[16,1152]{1,0:T(8,128)S(1)}, f32[16,1152]{1,0:T(8,128)S(1)}, u32[]{:S(2)}, u32[]{:S(2)}) collective-permute-start(f32[16,1152]{1,0:T(8,128)S(1)} %core_add.1.q0), channel_id=1, source_target_pairs={{64,0},{65,1},{66,2},{67,3},{68,4},{69,5},{70,6},{71,7},{72,8},{73... | collective-permute-start | bytes 221192 | tf_op jit(solution)/shard_map/ppermute | solution.py:367
  143.8 4.3 %collective-permute-start.36 = (f32[16,1152]{1,0:T(8,128)S(1)}, f32[16,1152]{1,0:T(8,128)S(1)}, u32[]{:S(2)}, u32[]{:S(2)}) collective-permute-start(f32[16,1152]{1,0:T(8,128)S(1)} %core_add.1.q0), channel_id=1, source_target_pairs={{32,0},{33,1},{34,2},{35,3},{36,4},{37,5},{38,6},{39,7},{40,8},{41... | collective-permute-start | bytes 221192 | tf_op jit(solution)/shard_map/ppermute | solution.py:367
  (10 other events, 24.6 us)

commit v2 on v1

v2 whole, which is shorter than its diff:
```python
import functools
import math

import jax
import jax.numpy as jnp
from jax import lax
from jax.experimental import pallas as pl
from jax.experimental.pallas import tpu as pltpu
from jax.sharding import Mesh
from jax.sharding import PartitionSpec as P


ITERS = 3
F = 128
CB = 1024
QB = CB // 4
NJ = 2 * CB
NI = 16 * QB
KV = 16
NTOT = 32768
GROUPS = (0, 1, 3, 2)
LAST_GROUP = GROUPS[-1]
CLS = QB + 4 * KV
PROWS = CLS + 16
base_width = 2.8
width_growth = 1.3
F32 = jnp.float32
BF16 = jnp.bfloat16
VM = pltpu.VMEM
NN = (((1,), (0,)), ((), ()))
NT = (((1,), (1,)), ((), ()))
TN = (((0,), (0,)), ((), ()))


def dot(a, b, dims):
    return lax.dot_general(a, b, dims, preferred_element_type=F32)


def call(kernel, name, outs, args, flops=0, scratch=(), far=()):
    def spec(n, a):
        if a.dtype == jnp.int32 and a.ndim == 1:
            return pl.BlockSpec(memory_space=pltpu.SMEM)
        return pl.BlockSpec(memory_space=pltpu.HBM if n in far else VM)

    return pl.pallas_call(
        kernel,
        out_shape=outs,
        in_specs=[spec(n, a) for n, a in enumerate(args)],
        out_specs=jax.tree.map(lambda _: pl.BlockSpec(memory_space=VM), outs),
        scratch_shapes=scratch,
        compiler_params=pltpu.CompilerParams(vmem_limit_bytes=24 << 20),
        cost_estimate=pl.CostEstimate(flops=flops, bytes_accessed=0, transcendentals=0),
        name=name,
    )(*args)


def sds(shape, dtype=F32):
    return jax.ShapeDtypeStruct(shape, dtype)


def vmem(shape, dtype=F32):
    return pltpu.VMEM(shape, dtype)


def keep(a):
    return pltpu.with_memory_space_constraint(a, VM)


def pack_kernel(pos, frames, classes, start, piece, cls_out, quarter, own_classes, sems):
    at = pl.multiple_of(pos[0] * QB, QB)
    copies = (
        pltpu.make_async_copy(frames.at[pl.ds(at, QB), :], piece.at[0:QB, :], sems.at[0]),
        pltpu.make_async_copy(start.at[:, pl.ds(at, QB)], quarter, sems.at[1]),
        pltpu.make_async_copy(classes, own_classes, sems.at[2]),
    )
    for copy in copies:
        copy.start()
    for copy in copies:
        copy.wait()
    cls = own_classes[...].astype(F32)
    cls = jnp.concatenate([cls, jnp.zeros_like(cls)], axis=0).astype(BF16)
    piece[CLS:PROWS, :] = cls
    cls_out[...] = cls
    high = quarter[...].astype(BF16)
    low = (quarter[...] - high.astype(F32)).astype(BF16)
    for h in range(2):
        at = QB + 2 * h * KV
        piece[at : at + KV, :] = high[:, h * 128 : (h + 1) * 128]
        piece[at + KV : at + 2 * KV, :] = low[:, h * 128 : (h + 1) * 128]


def stack_kernel(a, b, c, d, ready, out):
    del ready
    for n, ref in enumerate((a, b, c, d)):
        out[n] = ref[...]


def augment(rows, own_first):
    wide = rows.astype(F32)
    half = -0.5 * jnp.sum(wide * wide, axis=1, keepdims=True)
    p1 = half.astype(BF16).astype(F32)
    p2 = (half - p1).astype(BF16).astype(F32)
    p3 = half - p1 - p2
    lane = lax.broadcasted_iota(jnp.int32, (rows.shape[0], 128), 1)
    first = 0 if own_first else 3
    ones = jnp.logical_and(lane >= 3 - first, lane < 6 - first)
    extra = jnp.where(ones, 1.0, 0.0)
    for n, part in enumerate((p1, p2, p3)):
        extra = jnp.where(lane == first + n, part, extra)
    return jnp.concatenate([rows, extra.astype(BF16)], axis=1)


def inverse_width(cls):
    return jnp.exp2(cls * (-math.log2(width_growth))) * (1.0 / base_width)


def side_kernel(pos, mine, mine_cls, other, other_cls, aug_j, coef_j):
    c = pos[1]

    def side(blocks):
        for n, (rows, cls) in enumerate(blocks):
            aug_j[n * CB : (n + 1) * CB, :] = augment(rows[...], False)
            coef = inverse_width(cls[...].astype(F32)) * (2.0 * math.log2(math.e))
            for r in range(8):
                lo = n * CB + r * 128
                coef_j[:, lo : lo + 128] = coef[r : r + 1, :]

    @pl.when(c == 0)
    def _():
        side(((mine, mine_cls), (other, other_cls)))

    @pl.when(c != 0)
    def _():
        side(((other, other_cls), (mine, mine_cls)))


def spread(sum_j, out):
    for n in range(128):
        lo = n % 2 * CB + n // 2 % 4 * QB
        out[n] = sum_j[:, lo : lo + QB]


def rows_kernel(group, pos, pieces, aug_j, coef_j, *refs):
    k_ref, out, sum_j = refs[-3:]
    x = pos[0]
    sum_j[...] = jnp.zeros_like(sum_j) if group == 0 else refs[0][...]
    augs, coefs = [], []
    row = lax.broadcasted_iota(jnp.int32, (16, 128), 0)
    ones = jnp.ones((16, 128), BF16)
    for n in range(4):
        augs.append(augment(pieces[n, 0:QB, :], True))
        cls = pieces[n, CLS:PROWS, :].astype(F32)
        for h in range(2):
            one_row = jnp.where(row == 2 * x + h, cls, 0.0).astype(BF16)
            coefs.append(inverse_width(dot(one_row, ones, TN)[:, :1]))
    aug_i = jnp.concatenate(augs, axis=0)
    coef_i = jnp.concatenate(coefs, axis=0)
    half = 512
    ones_row = jnp.ones((8, half), BF16)
    for lo in range(0, 4 * QB, half):
        m = dot(aug_i[lo : lo + half], aug_j[...], NT)
        kb = jnp.exp2(m * coef_i[lo : lo + half] * coef_j[...]).astype(BF16)
        k_ref[lo : lo + half, :] = kb
        sum_j[...] += dot(ones_row, kb, NN)[0:1]
    if group == LAST_GROUP:
        spread(sum_j, out)
    else:
        out[...] = sum_j[...]


def side_i(pos, table, row):
    for n in range(16):
        at = pos[2 + n] * 8
        terms = [table[at + k] for k in range(8)]
        while len(terms) > 1:
            terms = [a + b for a, b in zip(terms[::2], terms[1::2])]
        row[:, n * QB : (n + 1) * QB] = terms[0]


def apply_k(v, ks, columns=slice(None)):
    n0 = NI // len(ks)
    terms = [dot(v[:, n * n0 : (n + 1) * n0], k[:, columns], NN) for n, k in enumerate(ks)]
    return (terms[0] + terms[1]) + (terms[2] + terms[3])


def degree_kernel(pos, k0, k1, k2, k3, table, dens_i, out, sum_j):
    side_i(pos, table, dens_i)
    dens_i[...] = dens_i[...] * (1.0 / NTOT)
    inverse = jnp.broadcast_to(1.0 / dens_i[...], (8, NI)).astype(BF16)
    sum_j[...] = apply_k(inverse, (k0, k1, k2, k3))[0:1]
    spread(sum_j, out)


def half(c):
    return pl.ds(pl.multiple_of(c * CB, CB), CB)


def first_kernel(
    pos, k0, k1, k2, k3, g0, g1, g2, g3, dens_i, table,
    vec, weight_i, weight_log, away, row,
):
    side_i(pos, table, row)
    row[...] = row[...] / (NTOT * dens_i[...])
    weight_i[...] = 1.0 / (dens_i[...] * jnp.sqrt(row[...]))
    weight_log[0:1, :] = weight_i[:, :QB]
    weight_log[1:2, :] = jnp.log(row[:, :QB])
    weight_log[2:, :] = jnp.zeros((6, QB), F32)
    for g, ref in enumerate((g0, g1, g2, g3)):
        for n in range(4):
            at = (4 * g + n) * QB
            for h in range(2):
                both = ref[n, QB + 2 * h * KV : QB + 2 * (h + 1) * KV, :].astype(F32)
                lo = at + h * 128
                part = (both[:KV] + both[KV:]) * weight_i[:, lo : lo + 128]
                vec[:, lo : lo + 128] = part.astype(BF16)
    away[...] = apply_k(vec, (k0, k1, k2, k3), half(1 - pos[1]))


def own_kernel(pos, k0, k1, k2, k3, vec, own):
    y = apply_k(vec, (k0, k1, k2, k3), half(pos[1]))
    if vec.shape[0] == 2 * KV:
        y = y[:KV] + y[KV:]
    own[...] = y


def next_kernel(pos, k0, k1, k2, k3, weight_i, pieces, vec, gram, away, parts):
    for n in range(16):
        at = n * QB
        p = pieces[pos[2 + n]]
        v = p * weight_i[0:1, at : at + QB]
        hi = v.astype(BF16)
        vec[0:KV, at : at + QB] = hi
        vec[KV:, at : at + QB] = (v - hi.astype(F32)).astype(BF16)
        p1 = p.astype(BF16)
        r1 = p - p1.astype(F32)
        p2 = r1.astype(BF16)
        parts[0:KV, at : at + QB] = p1
        parts[KV : 2 * KV, at : at + QB] = p2
        parts[2 * KV :, at : at + QB] = (r1 - p2.astype(F32)).astype(BF16)
    s = dot(parts[...], parts[...], NT)
    rows = s[0:KV] + s[KV : 2 * KV] + s[2 * KV :]
    square = rows[:, 0:KV] + rows[:, KV : 2 * KV] + rows[:, 2 * KV :]
    square = jnp.concatenate([square, jnp.zeros((KV, 128 - KV), F32)], axis=1)
    gram[...] = square
    y2 = apply_k(vec, (k0, k1, k2, k3), half(1 - pos[1]))
    away[:, :CB] = y2[0:KV] + y2[KV:]
    away[:, CB:] = square


def core_sum_kernel(pos, own, away, *refs):
    outs = refs[-4:]
    x = pos[0]
    total = own[...] + away[:, :CB]
    for t in range(4):
        for d in range(4):

            @pl.when((x + d) % 4 == t)
            def _(t=t, d=d):
                outs[d][:KV, :QB] = total[:, t * QB : (t + 1) * QB]

    if away.shape[1] > CB:
        gram = refs[0][...] + away[:, CB:]
        for ref in outs:
            ref[:, QB:] = gram
    else:
        for ref in outs:
            ref[KV:, :] = refs[0][...]


def core_add_kernel(own, away, gram, out):
    out[:, :CB] = own[...] + away[:, :CB]
    out[:, CB:] = gram[...] + away[:, CB:]


def eliminate(gram, y):
    row = lax.broadcasted_iota(jnp.int32, (KV, 1), 0)
    pivots = jnp.zeros((KV, 1), F32)
    for k in range(KV):
        pivot = gram[k : k + 1, k : k + 1]
        ratio = jnp.where(row > k, gram[:, k : k + 1] * (1.0 / pivot), 0.0)
        pivots = jnp.where(row == k, pivot, pivots)
        gram, y = gram - ratio * gram[k : k + 1, :], y - ratio * y[k : k + 1, :]
    return y * (1.0 / jnp.sqrt(pivots))


def project_first_kernel(pos, weight_log, q0, q1, q2, q3, out, weight_own, log_degree):
    y = (q0[:KV] + q1[:KV]) + (q2[:KV] + q3[:KV])
    p = y * weight_log[0:1, :]
    for n in range(16):
        out[n] = p
    for d, ref in enumerate((q0, q1, q2, q3)):
        at = pl.ds(pl.multiple_of((pos[0] + d) % 4 * QB, QB), QB)
        weight_own[:, at] = ref[KV : KV + 1, :]
        log_degree[:, at] = ref[KV + 1 : KV + 2, :]


def project_kernel(weight_log, q0, q1, q2, q3, out):
    total = (q0[...] + q1[...]) + (q2[...] + q3[...])
    p = eliminate(total[:, QB:], total[:, :QB]) * weight_log[0:1, :]
    for n in range(16):
        out[n] = p


def last_kernel(weight_own, q0, q1, q2, q3, proj, grams):
    total = (q0[...] + q1[...]) + (q2[...] + q3[...])
    y = eliminate(total[:, CB:], total[:, :CB])
    p = y * weight_own[...]
    proj[...] = p
    gram = lax.dot_general(p, p, NT, precision=lax.Precision.HIGHEST, preferred_element_type=F32)
    gram = jnp.concatenate([gram, jnp.zeros((KV, 128 - KV), F32)], axis=1)
    for n in range(32):
        grams[n] = gram


def finish_kernel(proj, grams, out):
    gram = grams[0]
    for n in range(1, 32):
        gram = gram + grams[n]
    out[...] = eliminate(gram, proj[...]) * math.sqrt(NTOT)


def device_number(x, z, y, c):
    return (((x % 4) * 4 + z % 4) * 4 + y % 4) * 2 + c % 2


def shift(v, source):
    pairs = [
        (device_number(*source(x, z, y, c)), device_number(x, z, y, c))
        for x in range(4)
        for z in range(4)
        for y in range(4)
        for c in range(2)
    ]
    return lax.ppermute(v, ("x", "z", "y", "c"), pairs)


def from_line(v, d, second=False):
    def source(x, z, y, c):
        along_y = (c == 0) != second
        return (x, z, y + d, c) if along_y else (x, z + d, y, c)

    return shift(v, source)


def from_x(v, d):
    return shift(v, lambda x, z, y, c: (x + d, z, y, c))


def from_core(v):
    return shift(v, lambda x, z, y, c: (x, z, y, c + 1))


def body(frames, width_class, start):
    x, z, y, c = (lax.axis_index(a) for a in ("x", "z", "y", "c"))
    second, first = jnp.arange(16, dtype=jnp.int32) // 4, jnp.arange(16, dtype=jnp.int32) % 4
    piece_y = (y + jnp.where(c == 0, first, second)) % 4
    piece_z = (z + jnp.where(c == 0, second, first)) % 4
    pos = jnp.concatenate([jnp.stack([x, c]), piece_y * 4 + piece_z]).astype(jnp.int32)

    classes = width_class.reshape(8, 128)
    piece, cls = call(
        pack_kernel,
        "pack",
        [sds((PROWS, F), BF16), sds((16, 128), BF16)],
        (pos, *(pltpu.with_memory_space_constraint(a, pltpu.HBM) for a in (frames, classes, start))),
        scratch=[
            pltpu.VMEM((KV, QB), F32),
            pltpu.VMEM((8, 128), jnp.int32),
            pltpu.SemaphoreType.DMA((3,)),
        ],
        far=(1, 2, 3),
    )
    line = [piece] + [from_line(piece, d) for d in (1, 2, 3)]
    aug_j, coef_j = call(
        side_kernel,
        "side",
        [sds((NJ, 2 * F), BF16), sds((1, NJ))],
        (pos, frames, cls, from_core(frames), from_core(cls)),
        flops=NJ * 4000,
    )
    line = call(stack_kernel, "stack", sds((4, PROWS, F), BF16), (*line, coef_j))
    groups = [line] + [from_line(line, d, True) for d in (1, 2, 3)]
    ks, sums = [None] * 4, ()
    for g in GROUPS:
        ks[g], sums = call(
            functools.partial(rows_kernel, g),
            f"rows{g}",
            [vmem((4 * QB, NJ), BF16), sds((128, 1, QB) if g == LAST_GROUP else (1, NJ))],
            (pos, groups[g], aug_j, coef_j) + (() if g == 0 else (sums,)),
            flops=4 * QB * NJ * 1024,
            scratch=[pltpu.VMEM((1, NJ), F32)],
        )

    def tile():
        return [keep(k) for k in ks]

    everyone = ("y", "z", "x", "c")
    dens_i, table = call(
        degree_kernel,
        "degree",
        [sds((1, NI)), sds((128, 1, QB))],
        (pos, *tile(), lax.all_to_all(sums, everyone, 0, 0)),
        scratch=[pltpu.VMEM((1, NJ), F32)],
    )
    vec, weight_i, weight_log, away = call(
        first_kernel,
        "first",
        [sds((KV, NI), BF16), sds((1, NI)), sds((8, QB)), sds((KV, CB))],
        (pos, *tile(), *groups, dens_i, lax.all_to_all(table, everyone, 0, 0)),
        scratch=[pltpu.VMEM((1, NI), F32)],
    )
    flops = 2 * NI * CB * 256

    def own_half(iteration):
        return call(own_kernel, f"own{iteration}", sds((KV, CB)), (pos, *tile(), vec), flops=flops)

    for iteration in range(1, ITERS):
        shape = (KV + 8, QB) if iteration == 1 else (KV, QB + 128)
        quarters = call(
            core_sum_kernel,
            f"core_sum{iteration}",
            [sds(shape)] * 4,
            (pos, own_half(iteration), from_core(away), weight_log if iteration == 1 else square),
        )
        quarters = [quarters[0]] + [from_x(quarters[4 - d], d) for d in (1, 2, 3)]
        if iteration == 1:
            pieces, weight_own, log_degree = call(
                project_first_kernel,
                "project1",
                [sds((16, KV, QB)), sds((1, CB)), sds((1, CB))],
                (pos, weight_log, *quarters),
            )
        else:
            pieces = call(
                project_kernel,
                f"project{iteration}",
                sds((16, KV, QB)),
                (weight_log, *quarters),
            )
        pieces = lax.all_to_all(pieces, ("y", "z"), 0, 0)
        vec, square, away = call(
            next_kernel,
            f"next{iteration}",
            [sds((2 * KV, NI), BF16), sds((KV, 128)), sds((KV, CB + 128))],
            (pos, *tile(), weight_i, pieces),
            scratch=[pltpu.VMEM((3 * KV, NI), BF16)],
        )
    total = call(
        core_add_kernel,
        "core_add",
        sds((KV, CB + 128)),
        (own_half(ITERS), from_core(away), square),
    )
    totals = [total] + [from_x(total, d) for d in (1, 2, 3)]
    proj, grams = call(
        last_kernel, "last", [sds((KV, CB)), sds((32, KV, 128))], (weight_own, *totals)
    )
    grams = lax.all_to_all(grams, ("z", "y", "c"), 0, 0)
    embedding = call(finish_kernel, "finish", sds((KV, CB)), (proj, grams))
    return embedding, log_degree.reshape(CB)


def solution(mesh):
    grid = Mesh(mesh.devices.reshape(4, 4, 4, 2), ("x", "z", "y", "c"))
    col = ("z", "y", "c")
    in_specs = (P(col, None), P(col), P(None, col))
    out_specs = (P(None, col), P(col))
    return jax.shard_map(body, mesh=grid, in_specs=in_specs, out_specs=out_specs, check_vma=False)
```

time: 169 us -> 149 us (0.88); the launches traced: 166 us -> 148 us
  starting transfers between devices: 63.6 us -> 25.8 us
  blocking collectives: 37.1 us -> 68.7 us
  waiting for transfers between devices: 23.9 us -> 16.5 us
  Pallas kernels: 37.6 us -> 35.6 us
    ppermute x39 -> x20, starting transfers between devices: 63.6 us -> 25.8 us  [shift(): return lax.ppermute(v, ('x', 'z', 'y', 'c'), pairs)]
    all_to_all x0 -> x2, blocking collectives: none -> 34.6 us  [the longest x1 20.3 us: body(): lax.all_to_all(sums, everyone, 0, 0)]
    ppermute x39 -> x20, waiting for transfers between devices: 23.9 us -> 16.5 us  [shift(): return lax.ppermute(v, ('x', 'z', 'y', 'c'), pairs)]
    all_to_all x2, blocking collectives: 23.2 us -> 20.6 us  [body(): pieces = lax.all_to_all(pieces, ('y', 'z'), 0, 0)]
    pallas_call x17 -> x21, Pallas kernels: 37.6 us -> 35.6 us  [call(): pl.pallas_call(kernel, out_shape=outs, in_specs=[spec(n, a) for n, a in e...]
  transfers between devices with their start and end apart: 39 -> 20, of which waited for: 21 -> 12; matrix products, arithmetic and copies ran while one was open for 0% -> 0% of each run, Pallas kernels for 2% -> 11%
where the time goes in v2:
time: 149 us; the launch traced here: 148 us
  blocking collectives  68.7 us (46%)
  Pallas kernels  35.6 us (24%)
  starting transfers between devices  25.8 us (17%)
  waiting for transfers between devices  16.5 us (11%)
    pallas_call x21, Pallas kernels, call(): pl.pallas_call(kernel, out_shape=outs, in_specs=[spec(n, a) for n, a in e...  35.6 us
    ppermute x20, starting transfers between devices, shift(): return lax.ppermute(v, ('x', 'z', 'y', 'c'), pairs)  25.8 us
    all_to_all x2, blocking collectives, body(): pieces = lax.all_to_all(pieces, ('y', 'z'), 0, 0)  20.6 us
    all_to_all x1, blocking collectives, body(): lax.all_to_all(sums, everyone, 0, 0)  20.3 us
    ppermute x20, waiting for transfers between devices, shift(): return lax.ppermute(v, ('x', 'z', 'y', 'c'), pairs)  16.5 us
    all_to_all x1, blocking collectives, body(): lax.all_to_all(table, everyone, 0, 0)  14.3 us
    all_to_all x1, blocking collectives, body(): grams = lax.all_to_all(grams, ('z', 'y', 'c'), 0, 0)  13.5 us
  transfers between devices with their start and end apart: 20, of which 12 were waited for; matrix products, arithmetic and copies ran while one was open for 0% of the time, Pallas kernels for 11%

profile of v2, /device:TPU:1, one launch (start us, length us, event | category | flops | bytes accessed | tf_op | source)
XLA Modules:
  0.0 148.4 jit_solution(1154279931865688651)
XLA Ops:
  0.6 1.5 %collective-permute-start.3 = (bf16[1024,128]{1,0:T(8,128)(2,1)}, bf16[1024,128]{1,0:T(8,128)(2,1)S(1)}, u32[]{:S(2)}, u32[]{:S(2)}) collective-permute-start(bf16[1024,128]{1,0:T(8,128)(2,1)} %mine.1), channel_id=1, source_target_pairs={{1,0},{0,1},{3,2},{2,3},{5,4},{4,5},{7,6},{6,7},{9,8},{8,9},{11,10... | collective-permute-start | bytes 786440 | tf_op jit(solution)/shard_map/ppermute | solution.py:334
  2.2 1.4 pack.1
  3.7 1.8 %collective-permute-start.2 = (bf16[336,128]{1,0:T(8,128)(2,1)S(1)}, bf16[336,128]{1,0:T(8,128)(2,1)S(1)}, u32[]{:S(2)}, u32[]{:S(2)}) collective-permute-start(bf16[336,128]{1,0:T(8,128)(2,1)S(1)} %get-tuple-element.39.a), channel_id=1, source_target_pairs={{6,0},{25,1},{0,2},{27,3},{2,4},{29,5},{4,6},{31,7},{14,8},{1,9},{... | collective-permute-start | bytes 258056 | tf_op jit(solution)/shard_map/ppermute | solution.py:334
  5.4 3.3 %collective-permute-start.1 = (bf16[336,128]{1,0:T(8,128)(2,1)S(1)}, bf16[336,128]{1,0:T(8,128)(2,1)S(1)}, u32[]{:S(2)}, u32[]{:S(2)}) collective-permute-start(bf16[336,128]{1,0:T(8,128)(2,1)S(1)} %get-tuple-element.39.a), channel_id=1, source_target_pairs={{4,0},{17,1},{6,2},{19,3},{0,4},{21,5},{2,6},{23,7},{12,8},{25,9},... | collective-permute-start | bytes 258056 | tf_op jit(solution)/shard_map/ppermute | solution.py:334
  12.7 2.8 %collective-permute-start.5 = (bf16[4,336,128]{2,1,0:T(8,128)(2,1)S(1)}, bf16[4,336,128]{2,1,0:T(8,128)(2,1)S(1)}, u32[]{:S(2)}, u32[]{:S(2)}) collective-permute-start(bf16[4,336,128]{2,1,0:T(8,128)(2,1)S(1)} %stack.9.pieces.g0), channel_id=1, source_target_pairs={{8,0},{3,1},{10,2},{5,3},{12,4},{7,5},{14,6},{1,7},{16,8},{11,9},{... | collective-permute-start | bytes 1032200 | tf_op jit(solution)/shard_map/ppermute | solution.py:334
  15.5 1.6 %collective-permute-start.6 = (bf16[4,336,128]{2,1,0:T(8,128)(2,1)S(1)}, bf16[4,336,128]{2,1,0:T(8,128)(2,1)S(1)}, u32[]{:S(2)}, u32[]{:S(2)}) collective-permute-start(bf16[4,336,128]{2,1,0:T(8,128)(2,1)S(1)} %stack.9.pieces.g0), channel_id=1, source_target_pairs={{16,0},{5,1},{18,2},{7,3},{20,4},{1,5},{22,6},{3,7},{24,8},{13,9},... | collective-permute-start | bytes 1032200 | tf_op jit(solution)/shard_map/ppermute | solution.py:334
  17.1 2.8 %rows0.1 = (bf16[1024,2048]{1,0:T(8,128)(2,1)S(1)}, f32[1,2048]{1,0:T(1,128)S(1)}) custom-call(s32[18]{0:T(128)S(1)} %pad_add_fusion.pos, bf16[4,336,128]{2,1,0:T(8,128)(2,1)S(1)} %stack.9.pieces.g0, bf16[2048,256]{1,0:T(8,128)(2,1)S(1)} %get-tuple-element.42.aug_j, f32[1,2048]{1,0:T(1,128)S(1)} %get-tuple-element.41.ready.coef_j), custom_call_target="tpu_custom_call" | custom-call | flops 2147483648 | tf_op jit(solution)/shard_map/rows0/pallas_call | solution.py:45
  20.0 3.4 %collective-permute-done.5.pieces.g1 = bf16[4,336,128]{2,1,0:T(8,128)(2,1)S(1)} collective-permute-done((bf16[4,336,128]{2,1,0:T(8,128)(2,1)S(1)}, bf16[4,336,128]{2,1,0:T(8,128)(2,1)S(1)}, u32[]{:S(2)}, u32[]{:S(2)}) %collective-permute-start.5) | collective-permute-done | bytes 344096 | tf_op jit(solution)/shard_map/ppermute | solution.py:334
  23.4 2.8 %rows1.1 = (bf16[1024,2048]{1,0:T(8,128)(2,1)S(1)}, f32[1,2048]{1,0:T(1,128)S(1)}) custom-call(s32[18]{0:T(128)S(1)} %pad_add_fusion.pos, bf16[4,336,128]{2,1,0:T(8,128)(2,1)S(1)} %collective-permute-done.5.pieces.g1, bf16[2048,256]{1,0:T(8,128)(2,1)S(1)} %get-tuple-element.42.aug_j, f32[1,2048]{1,0:T(1,128)S(1)} %get-tuple-element.41.ready.coef_j, ...), custom_call_target="tpu_custom_call" | custom-call | flops 2147483648 | tf_op jit(solution)/shard_map/rows1/pallas_call | solution.py:45
  26.8 2.9 %rows3.1 = (bf16[1024,2048]{1,0:T(8,128)(2,1)S(1)}, f32[1,2048]{1,0:T(1,128)S(1)}) custom-call(s32[18]{0:T(128)S(1)} %pad_add_fusion.pos, bf16[4,336,128]{2,1,0:T(8,128)(2,1)S(1)} %collective-permute-done.7.pieces.g3, bf16[2048,256]{1,0:T(8,128)(2,1)S(1)} %get-tuple-element.42.aug_j, f32[1,2048]{1,0:T(1,128)S(1)} %get-tuple-element.41.ready.coef_j, ...), custom_call_target="tpu_custom_call" | custom-call | flops 2147483648 | tf_op jit(solution)/shard_map/rows3/pallas_call | solution.py:45
  29.7 2.9 %rows2.1 = (bf16[1024,2048]{1,0:T(8,128)(2,1)S(1)}, f32[128,1,256]{2,1,0:T(1,128)S(1)}) custom-call(s32[18]{0:T(128)S(1)} %pad_add_fusion.pos, bf16[4,336,128]{2,1,0:T(8,128)(2,1)S(1)} %collective-permute-done.6.pieces.g2, bf16[2048,256]{1,0:T(8,128)(2,1)S(1)} %get-tuple-element.42.aug_j, f32[1,2048]{1,0:T(1,128)S(1)} %get-tuple-element.41.ready.coef_j, ...), custom_call_target="tpu_custom_call" | custom-call | flops 2147483648 | tf_op jit(solution)/shard_map/rows2/pallas_call | solution.py:45
  32.6 20.3 %all_to_all.25.table = f32[128,1,256]{2,1,0:T(1,128)S(1)} all-to-all(f32[128,1,256]{2,1,0:T(1,128)S(1)} %get-tuple-element.50), channel_id=1, replica_groups=mesh['x'=4,'z'=4,'y'=4,'c'=2] {'y','z','x','c'}, dimensions={0} | all-to-all | bytes 262144 | tf_op jit(solution)/shard_map/all_to_all | solution.py:402
  52.9 2.9 %degree.1 = (f32[1,4096]{1,0:T(1,128)S(1)}, f32[128,1,256]{2,1,0:T(1,128)S(1)}) custom-call(s32[18]{0:T(128)S(1)} %pad_add_fusion.pos, bf16[1024,2048]{1,0:T(8,128)(2,1)S(1)} %get-tuple-element.43.k0, bf16[1024,2048]{1,0:T(8,128)(2,1)S(1)} %get-tuple-element.45.k1, bf16[1024,2048]{1,0:T(8,128)(2,1)S(1)} %get-tuple-element.48.k2, ...), custom_call_target="tpu_custom_call" | custom-call | tf_op jit(solution)/shard_map/degree/pallas_call | solution.py:45
  55.8 14.3 %all_to_all.26.table = f32[128,1,256]{2,1,0:T(1,128)S(1)} all-to-all(f32[128,1,256]{2,1,0:T(1,128)S(1)} %get-tuple-element.52), channel_id=1, replica_groups=mesh['x'=4,'z'=4,'y'=4,'c'=2] {'y','z','x','c'}, dimensions={0} | all-to-all | bytes 262144 | tf_op jit(solution)/shard_map/all_to_all | solution.py:409
  70.0 1.8 %first.1 = (bf16[16,4096]{1,0:T(8,128)(2,1)S(1)}, f32[1,4096]{1,0:T(1,128)S(1)}, f32[8,256]{1,0:T(8,128)S(1)}, f32[16,1024]{1,0:T(8,128)S(1)}) custom-call(s32[18]{0:T(128)S(1)} %pad_add_fusion.pos, bf16[1024,2048]{1,0:T(8,128)(2,1)S(1)} %get-tuple-element.43.k0, bf16[1024,2048]{1,0:T(8,128)(2,1)S(1)} %get-tuple-element.45.k1, ...), custom_call_target="tpu_custom_call" | custom-call | tf_op jit(solution)/shard_map/first/pallas_call | solution.py:45
  72.5 1.7 %own1.1.own = f32[16,1024]{1,0:T(8,128)S(1)} custom-call(s32[18]{0:T(128)S(1)} %pad_add_fusion.pos, bf16[1024,2048]{1,0:T(8,128)(2,1)S(1)} %get-tuple-element.43.k0, bf16[1024,2048]{1,0:T(8,128)(2,1)S(1)} %get-tuple-element.45.k1, bf16[1024,2048]{1,0:T(8,128)(2,1)S(1)} %get-tuple-element.48.k2, bf16[1024,2048]{1,0:T(8,128)(2,1)S(1)} %get-tuple-element.49.k3, ...), custom_call_target="tpu_custom_call" | custom-call | flops 2147483648 | tf_op jit(solution)/shard_map/own1/pallas_call | solution.py:45
  77.6 2.3 %collective-permute-done.10.q2 = f32[24,256]{1,0:T(8,128)S(1)} collective-permute-done((f32[24,256]{1,0:T(8,128)S(1)}, f32[24,256]{1,0:T(8,128)S(1)}, u32[]{:S(2)}, u32[]{:S(2)}) %collective-permute-start.10) | collective-permute-done | bytes 24608 | tf_op jit(solution)/shard_map/ppermute | solution.py:334
  82.3 10.0 %all_to_all.27.pieces = f32[16,16,256]{2,1,0:T(8,128)S(1)} all-to-all(f32[16,16,256]{2,1,0:T(8,128)S(1)} %get-tuple-element.62), channel_id=1, replica_groups=mesh['x'=4,'z'=4,'y'=4,'c'=2] {'y','z'}, dimensions={0} | all-to-all | bytes 524288 | tf_op jit(solution)/shard_map/all_to_all | solution.py:440
  92.3 2.0 %next1.1 = (bf16[32,4096]{1,0:T(8,128)(2,1)S(1)}, f32[16,128]{1,0:T(8,128)S(1)}, f32[16,1152]{1,0:T(8,128)S(1)}) custom-call(s32[18]{0:T(128)S(1)} %pad_add_fusion.pos, bf16[1024,2048]{1,0:T(8,128)(2,1)S(1)} %get-tuple-element.43.k0, bf16[1024,2048]{1,0:T(8,128)(2,1)S(1)} %get-tuple-element.45.k1, bf16[1024,2048]{1,0:T(8,128)(2,1)S(1)} %get-tuple-element.48.k2, ...), custom_call_target="tpu_custom_call" | custom-call | tf_op jit(solution)/shard_map/next1/pallas_call | solution.py:45
  94.3 3.2 %collective-permute-start.12 = (f32[16,1152]{1,0:T(8,128)S(1)}, f32[16,1152]{1,0:T(8,128)S(1)}, u32[]{:S(2)}, u32[]{:S(2)}) collective-permute-start(f32[16,1152]{1,0:T(8,128)S(1)} %get-tuple-element.64), channel_id=1, source_target_pairs={{1,0},{0,1},{3,2},{2,3},{5,4},{4,5},{7,6},{6,7},{9,8},{8,9},{11,10... | collective-permute-start | bytes 221192 | tf_op jit(solution)/shard_map/ppermute | solution.py:334
  97.5 2.0 %own2.1.own = f32[16,1024]{1,0:T(8,128)S(1)} custom-call(s32[18]{0:T(128)S(1)} %pad_add_fusion.pos, bf16[1024,2048]{1,0:T(8,128)(2,1)S(1)} %get-tuple-element.43.k0, bf16[1024,2048]{1,0:T(8,128)(2,1)S(1)} %get-tuple-element.45.k1, bf16[1024,2048]{1,0:T(8,128)(2,1)S(1)} %get-tuple-element.48.k2, bf16[1024,2048]{1,0:T(8,128)(2,1)S(1)} %get-tuple-element.49.k3, ...), custom_call_target="tpu_custom_call" | custom-call | flops 2147483648 | tf_op jit(solution)/shard_map/own2/pallas_call | solution.py:45
  102.8 2.1 %collective-permute-done.14.q2 = f32[16,384]{1,0:T(8,128)S(1)} collective-permute-done((f32[16,384]{1,0:T(8,128)S(1)}, f32[16,384]{1,0:T(8,128)S(1)}, u32[]{:S(2)}, u32[]{:S(2)}) %collective-permute-start.14) | collective-permute-done | bytes 24608 | tf_op jit(solution)/shard_map/ppermute | solution.py:334
  106.9 10.5 %all_to_all.28.pieces = f32[16,16,256]{2,1,0:T(8,128)S(1)} all-to-all(f32[16,16,256]{2,1,0:T(8,128)S(1)} %project2.1), channel_id=1, replica_groups=mesh['x'=4,'z'=4,'y'=4,'c'=2] {'y','z'}, dimensions={0} | all-to-all | bytes 524288 | tf_op jit(solution)/shard_map/all_to_all | solution.py:440
  117.4 2.0 %next2.1 = (bf16[32,4096]{1,0:T(8,128)(2,1)S(1)}, f32[16,128]{1,0:T(8,128)S(1)}, f32[16,1152]{1,0:T(8,128)S(1)}) custom-call(s32[18]{0:T(128)S(1)} %pad_add_fusion.pos, bf16[1024,2048]{1,0:T(8,128)(2,1)S(1)} %get-tuple-element.43.k0, bf16[1024,2048]{1,0:T(8,128)(2,1)S(1)} %get-tuple-element.45.k1, bf16[1024,2048]{1,0:T(8,128)(2,1)S(1)} %get-tuple-element.48.k2, ...), custom_call_target="tpu_custom_call" | custom-call | tf_op jit(solution)/shard_map/next2/pallas_call | solution.py:45
  119.4 2.9 %collective-permute-start.16 = (f32[16,1152]{1,0:T(8,128)S(1)}, f32[16,1152]{1,0:T(8,128)S(1)}, u32[]{:S(2)}, u32[]{:S(2)}) collective-permute-start(f32[16,1152]{1,0:T(8,128)S(1)} %get-tuple-element.71), channel_id=1, source_target_pairs={{1,0},{0,1},{3,2},{2,3},{5,4},{4,5},{7,6},{6,7},{9,8},{8,9},{11,10... | collective-permute-start | bytes 221192 | tf_op jit(solution)/shard_map/ppermute | solution.py:334
  122.3 2.0 %own3.1.own = f32[16,1024]{1,0:T(8,128)S(1)} custom-call(s32[18]{0:T(128)S(1)} %pad_add_fusion.pos, bf16[1024,2048]{1,0:T(8,128)(2,1)S(1)} %get-tuple-element.43.k0, bf16[1024,2048]{1,0:T(8,128)(2,1)S(1)} %get-tuple-element.45.k1, bf16[1024,2048]{1,0:T(8,128)(2,1)S(1)} %get-tuple-element.48.k2, bf16[1024,2048]{1,0:T(8,128)(2,1)S(1)} %get-tuple-element.49.k3, ...), custom_call_target="tpu_custom_call" | custom-call | flops 2147483648 | tf_op jit(solution)/shard_map/own3/pallas_call | solution.py:45
  124.6 2.3 %collective-permute-start.18 = (f32[16,1152]{1,0:T(8,128)S(1)}, f32[16,1152]{1,0:T(8,128)S(1)}, u32[]{:S(2)}, u32[]{:S(2)}) collective-permute-start(f32[16,1152]{1,0:T(8,128)S(1)} %core_add.1.q0), channel_id=1, source_target_pairs={{64,0},{65,1},{66,2},{67,3},{68,4},{69,5},{70,6},{71,7},{72,8},{73... | collective-permute-start | bytes 221192 | tf_op jit(solution)/shard_map/ppermute | solution.py:334
  127.5 1.9 %collective-permute-done.19.q3 = f32[16,1152]{1,0:T(8,128)S(1)} collective-permute-done((f32[16,1152]{1,0:T(8,128)S(1)}, f32[16,1152]{1,0:T(8,128)S(1)}, u32[]{:S(2)}, u32[]{:S(2)}) %collective-permute-start.19) | collective-permute-done | bytes 73760 | tf_op jit(solution)/shard_map/ppermute | solution.py:334
  129.5 1.5 %collective-permute-done.18.q2 = f32[16,1152]{1,0:T(8,128)S(1)} collective-permute-done((f32[16,1152]{1,0:T(8,128)S(1)}, f32[16,1152]{1,0:T(8,128)S(1)}, u32[]{:S(2)}, u32[]{:S(2)}) %collective-permute-start.18) | collective-permute-done | bytes 73760 | tf_op jit(solution)/shard_map/ppermute | solution.py:334
  131.3 1.6 %last.1 = (f32[16,1024]{1,0:T(8,128)S(1)}, f32[32,16,128]{2,1,0:T(8,128)S(1)}) custom-call(f32[1,1024]{1,0:T(1,128)S(1)} %get-tuple-element.60.weight_own, f32[16,1152]{1,0:T(8,128)S(1)} %core_add.1.q0, f32[16,1152]{1,0:T(8,128)S(1)} %collective-permute-done.17.q1, f32[16,1152]{1,0:T(8,128)S(1)} %collective-permute-done.18.q2, ...), custom_call_target="tpu_custom_call" | custom-call | tf_op jit(solution)/shard_map/last/pallas_call | solution.py:45
  132.9 13.5 %all_to_all.29.grams = f32[32,16,128]{2,1,0:T(8,128)S(1)} all-to-all(f32[32,16,128]{2,1,0:T(8,128)S(1)} %get-tuple-element.74), channel_id=1, replica_groups=mesh['x'=4,'z'=4,'y'=4,'c'=2] {'z','y','c'}, dimensions={0} | all-to-all | bytes 524288 | tf_op jit(solution)/shard_map/all_to_all | solution.py:458
  146.4 2.0 %finish.1 = f32[16,1024]{1,0:T(8,128)} custom-call(f32[16,1024]{1,0:T(8,128)S(1)} %get-tuple-element.73.proj, f32[32,16,128]{2,1,0:T(8,128)S(1)} %all_to_all.29.grams), custom_call_target="tpu_custom_call" | custom-call | tf_op jit(solution)/shard_map/finish/pallas_call | solution.py:45
  (38 shorter events, 17.6 us)
Async XLA Ops:
  0.6 10.0 %collective-permute-start.3 = (bf16[1024,128]{1,0:T(8,128)(2,1)}, bf16[1024,128]{1,0:T(8,128)(2,1)S(1)}, u32[]{:S(2)}, u32[]{:S(2)}) collective-permute-start(bf16[1024,128]{1,0:T(8,128)(2,1)} %mine.1), channel_id=1, source_target_pairs={{1,0},{0,1},{3,2},{2,3},{5,4},{4,5},{7,6},{6,7},{9,8},{8,9},{11,10... | collective-permute-start | bytes 786440 | tf_op jit(solution)/shard_map/ppermute | solution.py:334
  3.7 9.0 %collective-permute-start.2 = (bf16[336,128]{1,0:T(8,128)(2,1)S(1)}, bf16[336,128]{1,0:T(8,128)(2,1)S(1)}, u32[]{:S(2)}, u32[]{:S(2)}) collective-permute-start(bf16[336,128]{1,0:T(8,128)(2,1)S(1)} %get-tuple-element.39.a), channel_id=1, source_target_pairs={{6,0},{25,1},{0,2},{27,3},{2,4},{29,5},{4,6},{31,7},{14,8},{1,9},{... | collective-permute-start | bytes 258056 | tf_op jit(solution)/shard_map/ppermute | solution.py:334
  5.4 7.2 %collective-permute-start.1 = (bf16[336,128]{1,0:T(8,128)(2,1)S(1)}, bf16[336,128]{1,0:T(8,128)(2,1)S(1)}, u32[]{:S(2)}, u32[]{:S(2)}) collective-permute-start(bf16[336,128]{1,0:T(8,128)(2,1)S(1)} %get-tuple-element.39.a), channel_id=1, source_target_pairs={{4,0},{17,1},{6,2},{19,3},{0,4},{21,5},{2,6},{23,7},{12,8},{25,9},... | collective-permute-start | bytes 258056 | tf_op jit(solution)/shard_map/ppermute | solution.py:334
  8.7 3.9 %collective-permute-start = (bf16[336,128]{1,0:T(8,128)(2,1)S(1)}, bf16[336,128]{1,0:T(8,128)(2,1)S(1)}, u32[]{:S(2)}, u32[]{:S(2)}) collective-permute-start(bf16[336,128]{1,0:T(8,128)(2,1)S(1)} %get-tuple-element.39.a), channel_id=1, source_target_pairs={{2,0},{9,1},{4,2},{11,3},{6,4},{13,5},{0,6},{15,7},{10,8},{17,9},{... | collective-permute-start | bytes 258056 | tf_op jit(solution)/shard_map/ppermute | solution.py:334
  9.5 1.2 collective-permute-start.4
  10.6 1.0 copy-start
  12.7 10.7 %collective-permute-start.5 = (bf16[4,336,128]{2,1,0:T(8,128)(2,1)S(1)}, bf16[4,336,128]{2,1,0:T(8,128)(2,1)S(1)}, u32[]{:S(2)}, u32[]{:S(2)}) collective-permute-start(bf16[4,336,128]{2,1,0:T(8,128)(2,1)S(1)} %stack.9.pieces.g0), channel_id=1, source_target_pairs={{8,0},{3,1},{10,2},{5,3},{12,4},{7,5},{14,6},{1,7},{16,8},{11,9},{... | collective-permute-start | bytes 1032200 | tf_op jit(solution)/shard_map/ppermute | solution.py:334
  15.5 11.3 %collective-permute-start.7 = (bf16[4,336,128]{2,1,0:T(8,128)(2,1)S(1)}, bf16[4,336,128]{2,1,0:T(8,128)(2,1)S(1)}, u32[]{:S(2)}, u32[]{:S(2)}) collective-permute-start(bf16[4,336,128]{2,1,0:T(8,128)(2,1)S(1)} %stack.9.pieces.g0), channel_id=1, source_target_pairs={{24,0},{7,1},{26,2},{1,3},{28,4},{3,5},{30,6},{5,7},{0,8},{15,9},{... | collective-permute-start | bytes 1032200 | tf_op jit(solution)/shard_map/ppermute | solution.py:334
  15.5 14.1 %collective-permute-start.6 = (bf16[4,336,128]{2,1,0:T(8,128)(2,1)S(1)}, bf16[4,336,128]{2,1,0:T(8,128)(2,1)S(1)}, u32[]{:S(2)}, u32[]{:S(2)}) collective-permute-start(bf16[4,336,128]{2,1,0:T(8,128)(2,1)S(1)} %stack.9.pieces.g0), channel_id=1, source_target_pairs={{16,0},{5,1},{18,2},{7,3},{20,4},{1,5},{22,6},{3,7},{24,8},{13,9},... | collective-permute-start | bytes 1032200 | tf_op jit(solution)/shard_map/ppermute | solution.py:334
  71.8 2.4 %collective-permute-start.8 = (f32[16,1024]{1,0:T(8,128)S(1)}, f32[16,1024]{1,0:T(8,128)S(1)}, u32[]{:S(2)}, u32[]{:S(2)}) collective-permute-start(f32[16,1024]{1,0:T(8,128)S(1)} %get-tuple-element.55), channel_id=1, source_target_pairs={{1,0},{0,1},{3,2},{2,3},{5,4},{4,5},{7,6},{6,7},{9,8},{8,9},{11,10... | collective-permute-start | bytes 196616 | tf_op jit(solution)/shard_map/ppermute | solution.py:334
  74.9 2.7 %collective-permute-start.9 = (f32[24,256]{1,0:T(8,128)S(1)}, f32[24,256]{1,0:T(8,128)S(1)}, u32[]{:S(2)}, u32[]{:S(2)}) collective-permute-start(f32[24,256]{1,0:T(8,128)S(1)} %get-tuple-element.57), channel_id=1, source_target_pairs={{32,0},{33,1},{34,2},{35,3},{36,4},{37,5},{38,6},{39,7},{40,8},{41... | collective-permute-start | bytes 73736 | tf_op jit(solution)/shard_map/ppermute | solution.py:334
  75.8 4.2 %collective-permute-start.10 = (f32[24,256]{1,0:T(8,128)S(1)}, f32[24,256]{1,0:T(8,128)S(1)}, u32[]{:S(2)}, u32[]{:S(2)}) collective-permute-start(f32[24,256]{1,0:T(8,128)S(1)} %get-tuple-element.58), channel_id=1, source_target_pairs={{64,0},{65,1},{66,2},{67,3},{68,4},{69,5},{70,6},{71,7},{72,8},{73... | collective-permute-start | bytes 73736 | tf_op jit(solution)/shard_map/ppermute | solution.py:334
  77.1 4.1 %collective-permute-start.11 = (f32[24,256]{1,0:T(8,128)S(1)}, f32[24,256]{1,0:T(8,128)S(1)}, u32[]{:S(2)}, u32[]{:S(2)}) collective-permute-start(f32[24,256]{1,0:T(8,128)S(1)} %get-tuple-element.59), channel_id=1, source_target_pairs={{96,0},{97,1},{98,2},{99,3},{100,4},{101,5},{102,6},{103,7},{104,8... | collective-permute-start | bytes 73736 | tf_op jit(solution)/shard_map/ppermute | solution.py:334
  94.3 5.2 %collective-permute-start.12 = (f32[16,1152]{1,0:T(8,128)S(1)}, f32[16,1152]{1,0:T(8,128)S(1)}, u32[]{:S(2)}, u32[]{:S(2)}) collective-permute-start(f32[16,1152]{1,0:T(8,128)S(1)} %get-tuple-element.64), channel_id=1, source_target_pairs={{1,0},{0,1},{3,2},{2,3},{5,4},{4,5},{7,6},{6,7},{9,8},{8,9},{11,10... | collective-permute-start | bytes 221192 | tf_op jit(solution)/shard_map/ppermute | solution.py:334
  100.1 2.7 %collective-permute-start.13 = (f32[16,384]{1,0:T(8,128)S(1)}, f32[16,384]{1,0:T(8,128)S(1)}, u32[]{:S(2)}, u32[]{:S(2)}) collective-permute-start(f32[16,384]{1,0:T(8,128)S(1)} %get-tuple-element.67), channel_id=1, source_target_pairs={{32,0},{33,1},{34,2},{35,3},{36,4},{37,5},{38,6},{39,7},{40,8},{41... | collective-permute-start | bytes 73736 | tf_op jit(solution)/shard_map/ppermute | solution.py:334
  100.7 4.2 %collective-permute-start.14 = (f32[16,384]{1,0:T(8,128)S(1)}, f32[16,384]{1,0:T(8,128)S(1)}, u32[]{:S(2)}, u32[]{:S(2)}) collective-permute-start(f32[16,384]{1,0:T(8,128)S(1)} %get-tuple-element.68), channel_id=1, source_target_pairs={{64,0},{65,1},{66,2},{67,3},{68,4},{69,5},{70,6},{71,7},{72,8},{73... | collective-permute-start | bytes 73736 | tf_op jit(solution)/shard_map/ppermute | solution.py:334
  101.4 4.2 %collective-permute-start.15 = (f32[16,384]{1,0:T(8,128)S(1)}, f32[16,384]{1,0:T(8,128)S(1)}, u32[]{:S(2)}, u32[]{:S(2)}) collective-permute-start(f32[16,384]{1,0:T(8,128)S(1)} %get-tuple-element.69), channel_id=1, source_target_pairs={{96,0},{97,1},{98,2},{99,3},{100,4},{101,5},{102,6},{103,7},{104,8... | collective-permute-start | bytes 73736 | tf_op jit(solution)/shard_map/ppermute | solution.py:334
  119.4 4.8 %collective-permute-start.16 = (f32[16,1152]{1,0:T(8,128)S(1)}, f32[16,1152]{1,0:T(8,128)S(1)}, u32[]{:S(2)}, u32[]{:S(2)}) collective-permute-start(f32[16,1152]{1,0:T(8,128)S(1)} %get-tuple-element.71), channel_id=1, source_target_pairs={{1,0},{0,1},{3,2},{2,3},{5,4},{4,5},{7,6},{6,7},{9,8},{8,9},{11,10... | collective-permute-start | bytes 221192 | tf_op jit(solution)/shard_map/ppermute | solution.py:334
  124.3 5.2 %collective-permute-start.19 = (f32[16,1152]{1,0:T(8,128)S(1)}, f32[16,1152]{1,0:T(8,128)S(1)}, u32[]{:S(2)}, u32[]{:S(2)}) collective-permute-start(f32[16,1152]{1,0:T(8,128)S(1)} %core_add.1.q0), channel_id=1, source_target_pairs={{96,0},{97,1},{98,2},{99,3},{100,4},{101,5},{102,6},{103,7},{104,8... | collective-permute-start | bytes 221192 | tf_op jit(solution)/shard_map/ppermute | solution.py:334
  124.6 6.4 %collective-permute-start.18 = (f32[16,1152]{1,0:T(8,128)S(1)}, f32[16,1152]{1,0:T(8,128)S(1)}, u32[]{:S(2)}, u32[]{:S(2)}) collective-permute-start(f32[16,1152]{1,0:T(8,128)S(1)} %core_add.1.q0), channel_id=1, source_target_pairs={{64,0},{65,1},{66,2},{67,3},{68,4},{69,5},{70,6},{71,7},{72,8},{73... | collective-permute-start | bytes 221192 | tf_op jit(solution)/shard_map/ppermute | solution.py:334
  127.0 4.3 %collective-permute-start.17 = (f32[16,1152]{1,0:T(8,128)S(1)}, f32[16,1152]{1,0:T(8,128)S(1)}, u32[]{:S(2)}, u32[]{:S(2)}) collective-permute-start(f32[16,1152]{1,0:T(8,128)S(1)} %core_add.1.q0), channel_id=1, source_target_pairs={{32,0},{33,1},{34,2},{35,3},{36,4},{37,5},{38,6},{39,7},{40,8},{41... | collective-permute-start | bytes 221192 | tf_op jit(solution)/shard_map/ppermute | solution.py:334

commit v3 on v2

--- a/solution.py
+++ b/solution.py
@@ -66,12 +66,13 @@
     return pltpu.with_memory_space_constraint(a, VM)
 
 
-def pack_kernel(pos, frames, classes, start, piece, cls_out, quarter, own_classes, sems):
+def pack_kernel(pos, frames, classes, start, piece, cls_out, mine, quarter, own_classes, sems):
     at = pl.multiple_of(pos[0] * QB, QB)
     copies = (
         pltpu.make_async_copy(frames.at[pl.ds(at, QB), :], piece.at[0:QB, :], sems.at[0]),
         pltpu.make_async_copy(start.at[:, pl.ds(at, QB)], quarter, sems.at[1]),
         pltpu.make_async_copy(classes, own_classes, sems.at[2]),
+        pltpu.make_async_copy(frames, mine, sems.at[3]),
     )
     for copy in copies:
         copy.start()
@@ -141,9 +142,8 @@
 
 
 def rows_kernel(group, pos, pieces, aug_j, coef_j, *refs):
-    k_ref, out, sum_j = refs[-3:]
+    k_ref, out = refs[-2:]
     x = pos[0]
-    sum_j[...] = jnp.zeros_like(sum_j) if group == 0 else refs[0][...]
     augs, coefs = [], []
     row = lax.broadcasted_iota(jnp.int32, (16, 128), 0)
     ones = jnp.ones((16, 128), BF16)
@@ -153,19 +153,18 @@
         for h in range(2):
             one_row = jnp.where(row == 2 * x + h, cls, 0.0).astype(BF16)
             coefs.append(inverse_width(dot(one_row, ones, TN)[:, :1]))
-    aug_i = jnp.concatenate(augs, axis=0)
-    coef_i = jnp.concatenate(coefs, axis=0)
     half = 512
-    ones_row = jnp.ones((8, half), BF16)
-    for lo in range(0, 4 * QB, half):
-        m = dot(aug_i[lo : lo + half], aug_j[...], NT)
-        kb = jnp.exp2(m * coef_i[lo : lo + half] * coef_j[...]).astype(BF16)
-        k_ref[lo : lo + half, :] = kb
-        sum_j[...] += dot(ones_row, kb, NN)[0:1]
+    total = jnp.zeros((8, NJ), F32) if group == 0 else refs[0][...]
+    for n in range(2):
+        aug_i = jnp.concatenate(augs[2 * n : 2 * n + 2], axis=0)
+        coef_i = jnp.concatenate(coefs[4 * n : 4 * n + 4], axis=0)
+        e = jnp.exp2(dot(aug_i, aug_j[...], NT) * coef_i * coef_j[...])
+        k_ref[n * half : (n + 1) * half, :] = e.astype(BF16)
+        total = total + jnp.sum(e.reshape(half // 8, 8, NJ), axis=0)
     if group == LAST_GROUP:
-        spread(sum_j, out)
+        spread(jnp.sum(total, axis=0, keepdims=True), out)
     else:
-        out[...] = sum_j[...]
+        out[...] = total
 
 
 def side_i(pos, table, row):
@@ -183,12 +182,11 @@
     return (terms[0] + terms[1]) + (terms[2] + terms[3])
 
 
-def degree_kernel(pos, k0, k1, k2, k3, table, dens_i, out, sum_j):
+def degree_kernel(pos, k0, k1, k2, k3, table, dens_i, out):
     side_i(pos, table, dens_i)
     dens_i[...] = dens_i[...] * (1.0 / NTOT)
     inverse = jnp.broadcast_to(1.0 / dens_i[...], (8, NI)).astype(BF16)
-    sum_j[...] = apply_k(inverse, (k0, k1, k2, k3))[0:1]
-    spread(sum_j, out)
+    spread(apply_k(inverse, (k0, k1, k2, k3))[0:1], out)
 
 
 def half(c):
@@ -254,7 +252,7 @@
     for t in range(4):
         for d in range(4):
 
-            @pl.when((x + d) % 4 == t)
+            @pl.when((x ^ d) == t)
             def _(t=t, d=d):
                 outs[d][:KV, :QB] = total[:, t * QB : (t + 1) * QB]
 
@@ -289,7 +287,7 @@
     for n in range(16):
         out[n] = p
     for d, ref in enumerate((q0, q1, q2, q3)):
-        at = pl.ds(pl.multiple_of((pos[0] + d) % 4 * QB, QB), QB)
+        at = pl.ds(pl.multiple_of((pos[0] ^ d) * QB, QB), QB)
         weight_own[:, at] = ref[KV : KV + 1, :]
         log_degree[:, at] = ref[KV + 1 : KV + 2, :]
 
@@ -307,20 +305,30 @@
     p = y * weight_own[...]
     proj[...] = p
     gram = lax.dot_general(p, p, NT, precision=lax.Precision.HIGHEST, preferred_element_type=F32)
-    gram = jnp.concatenate([gram, jnp.zeros((KV, 128 - KV), F32)], axis=1)
+    gram = jnp.concatenate([gram[:8], gram[8:], jnp.zeros((8, 128 - 2 * KV), F32)], axis=1)
     for n in range(32):
         grams[n] = gram
 
 
 def finish_kernel(proj, grams, out):
-    gram = grams[0]
-    for n in range(1, 32):
-        gram = gram + grams[n]
-    out[...] = eliminate(gram, proj[...]) * math.sqrt(NTOT)
+    terms = [grams[n] for n in range(32)]
+    while len(terms) > 1:
+        terms = [a + b for a, b in zip(terms[::2], terms[1::2])]
+    wide = terms[0]
+    gram = jnp.concatenate([wide[:, :KV], wide[:, KV : 2 * KV]], axis=0)
+    gram = jnp.concatenate([gram, jnp.zeros((KV, 128 - KV), F32)], axis=1)
+    lane = lax.broadcasted_iota(jnp.int32, (KV, 128), 1)
+    row = lax.broadcasted_iota(jnp.int32, (KV, 128), 0)
+    factor = eliminate(gram, jnp.where(lane == row, math.sqrt(NTOT), 0.0))
+    p = proj[...]
+    terms = [factor[:, k : k + 1] * p[k : k + 1, :] for k in range(KV)]
+    while len(terms) > 1:
+        terms = [a + b for a, b in zip(terms[::2], terms[1::2])]
+    out[...] = terms[0]
 
 
 def device_number(x, z, y, c):
-    return (((x % 4) * 4 + z % 4) * 4 + y % 4) * 2 + c % 2
+    return ((x * 4 + z) * 4 + y) * 2 + c
 
 
 def shift(v, source):
@@ -337,36 +345,36 @@
 def from_line(v, d, second=False):
     def source(x, z, y, c):
         along_y = (c == 0) != second
-        return (x, z, y + d, c) if along_y else (x, z + d, y, c)
+        return (x, z, y ^ d, c) if along_y else (x, z ^ d, y, c)
 
     return shift(v, source)
 
 
 def from_x(v, d):
-    return shift(v, lambda x, z, y, c: (x + d, z, y, c))
+    return shift(v, lambda x, z, y, c: (x ^ d, z, y, c))
 
 
 def from_core(v):
-    return shift(v, lambda x, z, y, c: (x, z, y, c + 1))
+    return shift(v, lambda x, z, y, c: (x, z, y, 1 - c))
 
 
 def body(frames, width_class, start):
     x, z, y, c = (lax.axis_index(a) for a in ("x", "z", "y", "c"))
     second, first = jnp.arange(16, dtype=jnp.int32) // 4, jnp.arange(16, dtype=jnp.int32) % 4
-    piece_y = (y + jnp.where(c == 0, first, second)) % 4
-    piece_z = (z + jnp.where(c == 0, second, first)) % 4
+    piece_y = y ^ jnp.where(c == 0, first, second)
+    piece_z = z ^ jnp.where(c == 0, second, first)
     pos = jnp.concatenate([jnp.stack([x, c]), piece_y * 4 + piece_z]).astype(jnp.int32)
 
     classes = width_class.reshape(8, 128)
-    piece, cls = call(
+    piece, cls, mine = call(
         pack_kernel,
         "pack",
-        [sds((PROWS, F), BF16), sds((16, 128), BF16)],
+        [sds((PROWS, F), BF16), sds((16, 128), BF16), vmem((CB, F), BF16)],
         (pos, *(pltpu.with_memory_space_constraint(a, pltpu.HBM) for a in (frames, classes, start))),
         scratch=[
             pltpu.VMEM((KV, QB), F32),
             pltpu.VMEM((8, 128), jnp.int32),
-            pltpu.SemaphoreType.DMA((3,)),
+            pltpu.SemaphoreType.DMA((4,)),
         ],
         far=(1, 2, 3),
     )
@@ -375,7 +383,7 @@
         side_kernel,
         "side",
         [sds((NJ, 2 * F), BF16), sds((1, NJ))],
-        (pos, frames, cls, from_core(frames), from_core(cls)),
+        (pos, keep(mine), cls, from_core(frames), from_core(cls)),
         flops=NJ * 4000,
     )
     line = call(stack_kernel, "stack", sds((4, PROWS, F), BF16), (*line, coef_j))
@@ -385,10 +393,9 @@
         ks[g], sums = call(
             functools.partial(rows_kernel, g),
             f"rows{g}",
-            [vmem((4 * QB, NJ), BF16), sds((128, 1, QB) if g == LAST_GROUP else (1, NJ))],
+            [vmem((4 * QB, NJ), BF16), sds((128, 1, QB) if g == LAST_GROUP else (8, NJ))],
             (pos, groups[g], aug_j, coef_j) + (() if g == 0 else (sums,)),
             flops=4 * QB * NJ * 1024,
-            scratch=[pltpu.VMEM((1, NJ), F32)],
         )
 
     def tile():
@@ -400,7 +407,6 @@
         "degree",
         [sds((1, NI)), sds((128, 1, QB))],
         (pos, *tile(), lax.all_to_all(sums, everyone, 0, 0)),
-        scratch=[pltpu.VMEM((1, NJ), F32)],
     )
     vec, weight_i, weight_log, away = call(
         first_kernel,
@@ -422,7 +428,7 @@
             [sds(shape)] * 4,
             (pos, own_half(iteration), from_core(away), weight_log if iteration == 1 else square),
         )
-        quarters = [quarters[0]] + [from_x(quarters[4 - d], d) for d in (1, 2, 3)]
+        quarters = [quarters[0]] + [from_x(quarters[d], d) for d in (1, 2, 3)]
         if iteration == 1:
             pieces, weight_own, log_degree = call(
                 project_first_kernel,
@@ -453,7 +459,7 @@
     )
     totals = [total] + [from_x(total, d) for d in (1, 2, 3)]
     proj, grams = call(
-        last_kernel, "last", [sds((KV, CB)), sds((32, KV, 128))], (weight_own, *totals)
+        last_kernel, "last", [sds((KV, CB)), sds((32, 8, 128))], (weight_own, *totals)
     )
     grams = lax.all_to_all(grams, ("z", "y", "c"), 0, 0)
     embedding = call(finish_kernel, "finish", sds((KV, CB)), (proj, grams))

time: 149 us -> 146 us (0.980)
  starting transfers between devices: 25.8 us -> 28.4 us
  waiting for transfers between devices: 16.5 us -> 14.2 us
  Pallas kernels: 35.6 us -> 33.8 us
    ppermute x20, starting transfers between devices: 25.8 us -> 28.4 us  [shift(): return lax.ppermute(v, ('x', 'z', 'y', 'c'), pairs)]
    ppermute x20, waiting for transfers between devices: 16.5 us -> 14.2 us  [shift(): return lax.ppermute(v, ('x', 'z', 'y', 'c'), pairs)]
    pallas_call x21, Pallas kernels: 35.6 us -> 33.8 us  [call(): pl.pallas_call(kernel, out_shape=outs, in_specs=[spec(n, a) for n, a in e...]
  transfers between devices with their start and end apart: 20 -> 20, of which waited for: 12 -> 11; matrix products, arithmetic and copies ran while one was open for 0% -> 0% of each run, Pallas kernels for 11% -> 10%
where the time goes in v3:
time: 146 us; the launch traced here: 145 us
  blocking collectives  68.2 us (47%)
  Pallas kernels  33.8 us (23%)
  starting transfers between devices  28.4 us (19%)
  waiting for transfers between devices  14.2 us (10%)
    pallas_call x21, Pallas kernels, call(): pl.pallas_call(kernel, out_shape=outs, in_specs=[spec(n, a) for n, a in e...  33.8 us
    ppermute x20, starting transfers between devices, shift(): return lax.ppermute(v, ('x', 'z', 'y', 'c'), pairs)  28.4 us
    all_to_all x2, blocking collectives, body(): pieces = lax.all_to_all(pieces, ('y', 'z'), 0, 0)  21.1 us
    all_to_all x1, blocking collectives, body(): lax.all_to_all(sums, everyone, 0, 0)  20.6 us
    all_to_all x1, blocking collectives, body(): lax.all_to_all(table, everyone, 0, 0)  14.3 us
    ppermute x20, waiting for transfers between devices, shift(): return lax.ppermute(v, ('x', 'z', 'y', 'c'), pairs)  14.2 us
    all_to_all x1, blocking collectives, body(): grams = lax.all_to_all(grams, ('z', 'y', 'c'), 0, 0)  12.3 us
  transfers between devices with their start and end apart: 20, of which 11 were waited for; matrix products, arithmetic and copies ran while one was open for 0% of the time, Pallas kernels for 10%

profile of v3, /device:TPU:1, one launch (start us, length us, event | category | flops | bytes accessed | tf_op | source)
XLA Modules:
  0.0 145.5 jit_solution(6929148241608719501)
XLA Ops:
  0.6 1.5 %collective-permute-start.3 = (bf16[1024,128]{1,0:T(8,128)(2,1)}, bf16[1024,128]{1,0:T(8,128)(2,1)S(1)}, u32[]{:S(2)}, u32[]{:S(2)}) collective-permute-start(bf16[1024,128]{1,0:T(8,128)(2,1)} %frames.1), channel_id=1, source_target_pairs={{1,0},{0,1},{3,2},{2,3},{5,4},{4,5},{7,6},{6,7},{9,8},{8,9},{11,10... | collective-permute-start | bytes 786440 | tf_op jit(solution)/shard_map/ppermute | solution.py:342
  2.2 1.6 %pack.1 = (bf16[336,128]{1,0:T(8,128)(2,1)S(1)}, bf16[16,128]{1,0:T(8,128)(2,1)S(1)}, bf16[1024,128]{1,0:T(8,128)(2,1)S(1)}) custom-call(s32[18]{0:T(128)S(1)} %pad_add_fusion.pos, bf16[1024,128]{1,0:T(8,128)(2,1)} %frames.1, s32[8,128]{1,0:T(8,128)} %bitcast.4, f32[16,1024]{1,0:T(8,128)} %start.1), custom_call_target="tpu_custom_call" | custom-call | tf_op jit(solution)/shard_map/pack/pallas_call | solution.py:45
  3.8 3.9 %collective-permute-start.2 = (bf16[336,128]{1,0:T(8,128)(2,1)S(1)}, bf16[336,128]{1,0:T(8,128)(2,1)S(1)}, u32[]{:S(2)}, u32[]{:S(2)}) collective-permute-start(bf16[336,128]{1,0:T(8,128)(2,1)S(1)} %get-tuple-element.40.a), channel_id=1, source_target_pairs={{6,0},{25,1},{4,2},{27,3},{2,4},{29,5},{0,6},{31,7},{14,8},{17,9},... | collective-permute-start | bytes 258056 | tf_op jit(solution)/shard_map/ppermute | solution.py:342
  10.6 2.0 %collective-permute-done.1.c = bf16[336,128]{1,0:T(8,128)(2,1)S(1)} collective-permute-done((bf16[336,128]{1,0:T(8,128)(2,1)S(1)}, bf16[336,128]{1,0:T(8,128)(2,1)S(1)}, u32[]{:S(2)}, u32[]{:S(2)}) %collective-permute-start.1) | collective-permute-done | bytes 86048 | tf_op jit(solution)/shard_map/ppermute | solution.py:342
  14.0 1.9 %collective-permute-start.7 = (bf16[4,336,128]{2,1,0:T(8,128)(2,1)S(1)}, bf16[4,336,128]{2,1,0:T(8,128)(2,1)S(1)}, u32[]{:S(2)}, u32[]{:S(2)}) collective-permute-start(bf16[4,336,128]{2,1,0:T(8,128)(2,1)S(1)} %stack.9.pieces.g0), channel_id=1, source_target_pairs={{24,0},{7,1},{26,2},{5,3},{28,4},{3,5},{30,6},{1,7},{16,8},{15,9},... | collective-permute-start | bytes 1032200 | tf_op jit(solution)/shard_map/ppermute | solution.py:342
  16.6 2.3 %rows0.1 = (bf16[1024,2048]{1,0:T(8,128)(2,1)S(1)}, f32[8,2048]{1,0:T(8,128)S(1)}) custom-call(s32[18]{0:T(128)S(1)} %pad_add_fusion.pos, bf16[4,336,128]{2,1,0:T(8,128)(2,1)S(1)} %stack.9.pieces.g0, bf16[2048,256]{1,0:T(8,128)(2,1)S(1)} %get-tuple-element.44.aug_j, f32[1,2048]{1,0:T(1,128)S(1)} %get-tuple-element.43.ready.coef_j), custom_call_target="tpu_custom_call" | custom-call | flops 2147483648 | tf_op jit(solution)/shard_map/rows0/pallas_call | solution.py:45
  19.2 2.3 %rows1.1 = (bf16[1024,2048]{1,0:T(8,128)(2,1)S(1)}, f32[8,2048]{1,0:T(8,128)S(1)}) custom-call(s32[18]{0:T(128)S(1)} %pad_add_fusion.pos, bf16[4,336,128]{2,1,0:T(8,128)(2,1)S(1)} %collective-permute-done.5.pieces.g1, bf16[2048,256]{1,0:T(8,128)(2,1)S(1)} %get-tuple-element.44.aug_j, f32[1,2048]{1,0:T(1,128)S(1)} %get-tuple-element.43.ready.coef_j, ...), custom_call_target="tpu_custom_call" | custom-call | flops 2147483648 | tf_op jit(solution)/shard_map/rows1/pallas_call | solution.py:45
  21.5 2.3 %collective-permute-done.7.pieces.g3 = bf16[4,336,128]{2,1,0:T(8,128)(2,1)S(1)} collective-permute-done((bf16[4,336,128]{2,1,0:T(8,128)(2,1)S(1)}, bf16[4,336,128]{2,1,0:T(8,128)(2,1)S(1)}, u32[]{:S(2)}, u32[]{:S(2)}) %collective-permute-start.7) | collective-permute-done | bytes 344096 | tf_op jit(solution)/shard_map/ppermute | solution.py:342
  23.8 2.3 %rows3.1 = (bf16[1024,2048]{1,0:T(8,128)(2,1)S(1)}, f32[8,2048]{1,0:T(8,128)S(1)}) custom-call(s32[18]{0:T(128)S(1)} %pad_add_fusion.pos, bf16[4,336,128]{2,1,0:T(8,128)(2,1)S(1)} %collective-permute-done.7.pieces.g3, bf16[2048,256]{1,0:T(8,128)(2,1)S(1)} %get-tuple-element.44.aug_j, f32[1,2048]{1,0:T(1,128)S(1)} %get-tuple-element.43.ready.coef_j, ...), custom_call_target="tpu_custom_call" | custom-call | flops 2147483648 | tf_op jit(solution)/shard_map/rows3/pallas_call | solution.py:45
  26.1 2.4 %rows2.1 = (bf16[1024,2048]{1,0:T(8,128)(2,1)S(1)}, f32[128,1,256]{2,1,0:T(1,128)S(1)}) custom-call(s32[18]{0:T(128)S(1)} %pad_add_fusion.pos, bf16[4,336,128]{2,1,0:T(8,128)(2,1)S(1)} %collective-permute-done.6.pieces.g2, bf16[2048,256]{1,0:T(8,128)(2,1)S(1)} %get-tuple-element.44.aug_j, f32[1,2048]{1,0:T(1,128)S(1)} %get-tuple-element.43.ready.coef_j, ...), custom_call_target="tpu_custom_call" | custom-call | flops 2147483648 | tf_op jit(solution)/shard_map/rows2/pallas_call | solution.py:45
  28.5 20.6 %all_to_all.25.table = f32[128,1,256]{2,1,0:T(1,128)S(1)} all-to-all(f32[128,1,256]{2,1,0:T(1,128)S(1)} %get-tuple-element.52), channel_id=1, replica_groups=mesh['x'=4,'z'=4,'y'=4,'c'=2] {'y','z','x','c'}, dimensions={0} | all-to-all | bytes 262144 | tf_op jit(solution)/shard_map/all_to_all | solution.py:409
  49.1 2.8 %degree.1 = (f32[1,4096]{1,0:T(1,128)S(1)}, f32[128,1,256]{2,1,0:T(1,128)S(1)}) custom-call(s32[18]{0:T(128)S(1)} %pad_add_fusion.pos, bf16[1024,2048]{1,0:T(8,128)(2,1)S(1)} %get-tuple-element.45.k0, bf16[1024,2048]{1,0:T(8,128)(2,1)S(1)} %get-tuple-element.47.k1, bf16[1024,2048]{1,0:T(8,128)(2,1)S(1)} %get-tuple-element.50.k2, ...), custom_call_target="tpu_custom_call" | custom-call | tf_op jit(solution)/shard_map/degree/pallas_call | solution.py:45
  51.9 14.3 %all_to_all.26.table = f32[128,1,256]{2,1,0:T(1,128)S(1)} all-to-all(f32[128,1,256]{2,1,0:T(1,128)S(1)} %get-tuple-element.54), channel_id=1, replica_groups=mesh['x'=4,'z'=4,'y'=4,'c'=2] {'y','z','x','c'}, dimensions={0} | all-to-all | bytes 262144 | tf_op jit(solution)/shard_map/all_to_all | solution.py:415
  66.2 1.8 %first.1 = (bf16[16,4096]{1,0:T(8,128)(2,1)S(1)}, f32[1,4096]{1,0:T(1,128)S(1)}, f32[8,256]{1,0:T(8,128)S(1)}, f32[16,1024]{1,0:T(8,128)S(1)}) custom-call(s32[18]{0:T(128)S(1)} %pad_add_fusion.pos, bf16[1024,2048]{1,0:T(8,128)(2,1)S(1)} %get-tuple-element.45.k0, bf16[1024,2048]{1,0:T(8,128)(2,1)S(1)} %get-tuple-element.47.k1, ...), custom_call_target="tpu_custom_call" | custom-call | tf_op jit(solution)/shard_map/first/pallas_call | solution.py:45
  68.7 1.7 %own1.1.own = f32[16,1024]{1,0:T(8,128)S(1)} custom-call(s32[18]{0:T(128)S(1)} %pad_add_fusion.pos, bf16[1024,2048]{1,0:T(8,128)(2,1)S(1)} %get-tuple-element.45.k0, bf16[1024,2048]{1,0:T(8,128)(2,1)S(1)} %get-tuple-element.47.k1, bf16[1024,2048]{1,0:T(8,128)(2,1)S(1)} %get-tuple-element.50.k2, bf16[1024,2048]{1,0:T(8,128)(2,1)S(1)} %get-tuple-element.51.k3, ...), custom_call_target="tpu_custom_call" | custom-call | flops 2147483648 | tf_op jit(solution)/shard_map/own1/pallas_call | solution.py:45
  71.4 1.7 %collective-permute-start.10 = (f32[24,256]{1,0:T(8,128)S(1)}, f32[24,256]{1,0:T(8,128)S(1)}, u32[]{:S(2)}, u32[]{:S(2)}) collective-permute-start(f32[24,256]{1,0:T(8,128)S(1)} %get-tuple-element.60), channel_id=1, source_target_pairs={{64,0},{65,1},{66,2},{67,3},{68,4},{69,5},{70,6},{71,7},{72,8},{73... | collective-permute-start | bytes 73736 | tf_op jit(solution)/shard_map/ppermute | solution.py:342
  73.1 1.8 %collective-permute-start.11 = (f32[24,256]{1,0:T(8,128)S(1)}, f32[24,256]{1,0:T(8,128)S(1)}, u32[]{:S(2)}, u32[]{:S(2)}) collective-permute-start(f32[24,256]{1,0:T(8,128)S(1)} %get-tuple-element.61), channel_id=1, source_target_pairs={{96,0},{97,1},{98,2},{99,3},{100,4},{101,5},{102,6},{103,7},{104,8... | collective-permute-start | bytes 73736 | tf_op jit(solution)/shard_map/ppermute | solution.py:342
  78.2 10.5 %all_to_all.27.pieces = f32[16,16,256]{2,1,0:T(8,128)S(1)} all-to-all(f32[16,16,256]{2,1,0:T(8,128)S(1)} %get-tuple-element.64), channel_id=1, replica_groups=mesh['x'=4,'z'=4,'y'=4,'c'=2] {'y','z'}, dimensions={0} | all-to-all | bytes 524288 | tf_op jit(solution)/shard_map/all_to_all | solution.py:446
  88.7 2.0 %next1.1 = (bf16[32,4096]{1,0:T(8,128)(2,1)S(1)}, f32[16,128]{1,0:T(8,128)S(1)}, f32[16,1152]{1,0:T(8,128)S(1)}) custom-call(s32[18]{0:T(128)S(1)} %pad_add_fusion.pos, bf16[1024,2048]{1,0:T(8,128)(2,1)S(1)} %get-tuple-element.45.k0, bf16[1024,2048]{1,0:T(8,128)(2,1)S(1)} %get-tuple-element.47.k1, bf16[1024,2048]{1,0:T(8,128)(2,1)S(1)} %get-tuple-element.50.k2, ...), custom_call_target="tpu_custom_call" | custom-call | tf_op jit(solution)/shard_map/next1/pallas_call | solution.py:45
  90.7 3.1 %collective-permute-start.12 = (f32[16,1152]{1,0:T(8,128)S(1)}, f32[16,1152]{1,0:T(8,128)S(1)}, u32[]{:S(2)}, u32[]{:S(2)}) collective-permute-start(f32[16,1152]{1,0:T(8,128)S(1)} %get-tuple-element.66), channel_id=1, source_target_pairs={{1,0},{0,1},{3,2},{2,3},{5,4},{4,5},{7,6},{6,7},{9,8},{8,9},{11,10... | collective-permute-start | bytes 221192 | tf_op jit(solution)/shard_map/ppermute | solution.py:342
  93.8 2.0 %own2.1.own = f32[16,1024]{1,0:T(8,128)S(1)} custom-call(s32[18]{0:T(128)S(1)} %pad_add_fusion.pos, bf16[1024,2048]{1,0:T(8,128)(2,1)S(1)} %get-tuple-element.45.k0, bf16[1024,2048]{1,0:T(8,128)(2,1)S(1)} %get-tuple-element.47.k1, bf16[1024,2048]{1,0:T(8,128)(2,1)S(1)} %get-tuple-element.50.k2, bf16[1024,2048]{1,0:T(8,128)(2,1)S(1)} %get-tuple-element.51.k3, ...), custom_call_target="tpu_custom_call" | custom-call | flops 2147483648 | tf_op jit(solution)/shard_map/own2/pallas_call | solution.py:45
  96.5 2.7 %collective-permute-start.14 = (f32[16,384]{1,0:T(8,128)S(1)}, f32[16,384]{1,0:T(8,128)S(1)}, u32[]{:S(2)}, u32[]{:S(2)}) collective-permute-start(f32[16,384]{1,0:T(8,128)S(1)} %get-tuple-element.70), channel_id=1, source_target_pairs={{64,0},{65,1},{66,2},{67,3},{68,4},{69,5},{70,6},{71,7},{72,8},{73... | collective-permute-start | bytes 73736 | tf_op jit(solution)/shard_map/ppermute | solution.py:342
  100.9 2.3 %collective-permute-done.15.q3 = f32[16,384]{1,0:T(8,128)S(1)} collective-permute-done((f32[16,384]{1,0:T(8,128)S(1)}, f32[16,384]{1,0:T(8,128)S(1)}, u32[]{:S(2)}, u32[]{:S(2)}) %collective-permute-start.15) | collective-permute-done | bytes 24608 | tf_op jit(solution)/shard_map/ppermute | solution.py:342
  104.5 10.5 %all_to_all.28.pieces = f32[16,16,256]{2,1,0:T(8,128)S(1)} all-to-all(f32[16,16,256]{2,1,0:T(8,128)S(1)} %project2.1), channel_id=1, replica_groups=mesh['x'=4,'z'=4,'y'=4,'c'=2] {'y','z'}, dimensions={0} | all-to-all | bytes 524288 | tf_op jit(solution)/shard_map/all_to_all | solution.py:446
  115.1 2.0 %next2.1 = (bf16[32,4096]{1,0:T(8,128)(2,1)S(1)}, f32[16,128]{1,0:T(8,128)S(1)}, f32[16,1152]{1,0:T(8,128)S(1)}) custom-call(s32[18]{0:T(128)S(1)} %pad_add_fusion.pos, bf16[1024,2048]{1,0:T(8,128)(2,1)S(1)} %get-tuple-element.45.k0, bf16[1024,2048]{1,0:T(8,128)(2,1)S(1)} %get-tuple-element.47.k1, bf16[1024,2048]{1,0:T(8,128)(2,1)S(1)} %get-tuple-element.50.k2, ...), custom_call_target="tpu_custom_call" | custom-call | tf_op jit(solution)/shard_map/next2/pallas_call | solution.py:45
  117.0 3.3 %collective-permute-start.16 = (f32[16,1152]{1,0:T(8,128)S(1)}, f32[16,1152]{1,0:T(8,128)S(1)}, u32[]{:S(2)}, u32[]{:S(2)}) collective-permute-start(f32[16,1152]{1,0:T(8,128)S(1)} %get-tuple-element.73), channel_id=1, source_target_pairs={{1,0},{0,1},{3,2},{2,3},{5,4},{4,5},{7,6},{6,7},{9,8},{8,9},{11,10... | collective-permute-start | bytes 221192 | tf_op jit(solution)/shard_map/ppermute | solution.py:342
  120.3 2.0 %own3.1.own = f32[16,1024]{1,0:T(8,128)S(1)} custom-call(s32[18]{0:T(128)S(1)} %pad_add_fusion.pos, bf16[1024,2048]{1,0:T(8,128)(2,1)S(1)} %get-tuple-element.45.k0, bf16[1024,2048]{1,0:T(8,128)(2,1)S(1)} %get-tuple-element.47.k1, bf16[1024,2048]{1,0:T(8,128)(2,1)S(1)} %get-tuple-element.50.k2, bf16[1024,2048]{1,0:T(8,128)(2,1)S(1)} %get-tuple-element.51.k3, ...), custom_call_target="tpu_custom_call" | custom-call | flops 2147483648 | tf_op jit(solution)/shard_map/own3/pallas_call | solution.py:45
  123.5 2.1 %collective-permute-start.17 = (f32[16,1152]{1,0:T(8,128)S(1)}, f32[16,1152]{1,0:T(8,128)S(1)}, u32[]{:S(2)}, u32[]{:S(2)}) collective-permute-start(f32[16,1152]{1,0:T(8,128)S(1)} %core_add.1.q0), channel_id=1, source_target_pairs={{32,0},{33,1},{34,2},{35,3},{36,4},{37,5},{38,6},{39,7},{40,8},{41... | collective-permute-start | bytes 221192 | tf_op jit(solution)/shard_map/ppermute | solution.py:342
  125.7 1.8 %collective-permute-done.19.q3 = f32[16,1152]{1,0:T(8,128)S(1)} collective-permute-done((f32[16,1152]{1,0:T(8,128)S(1)}, f32[16,1152]{1,0:T(8,128)S(1)}, u32[]{:S(2)}, u32[]{:S(2)}) %collective-permute-start.19) | collective-permute-done | bytes 73760 | tf_op jit(solution)/shard_map/ppermute | solution.py:342
  129.4 1.6 %last.1 = (f32[16,1024]{1,0:T(8,128)S(1)}, f32[32,8,128]{2,1,0:T(8,128)S(1)}) custom-call(f32[1,1024]{1,0:T(1,128)S(1)} %get-tuple-element.62.weight_own, f32[16,1152]{1,0:T(8,128)S(1)} %core_add.1.q0, f32[16,1152]{1,0:T(8,128)S(1)} %collective-permute-done.17.q1, f32[16,1152]{1,0:T(8,128)S(1)} %collective-permute-done.18.q2, ...), custom_call_target="tpu_custom_call" | custom-call | tf_op jit(solution)/shard_map/last/pallas_call | solution.py:45
  131.0 12.3 %all_to_all.29.grams = f32[32,8,128]{2,1,0:T(8,128)S(1)} all-to-all(f32[32,8,128]{2,1,0:T(8,128)S(1)} %get-tuple-element.76), channel_id=1, replica_groups=mesh['x'=4,'z'=4,'y'=4,'c'=2] {'z','y','c'}, dimensions={0} | all-to-all | bytes 262144 | tf_op jit(solution)/shard_map/all_to_all | solution.py:464
  143.3 2.2 %finish.1 = f32[16,1024]{1,0:T(8,128)} custom-call(f32[16,1024]{1,0:T(8,128)S(1)} %get-tuple-element.75.proj, f32[32,8,128]{2,1,0:T(8,128)S(1)} %all_to_all.29.grams), custom_call_target="tpu_custom_call" | custom-call | tf_op jit(solution)/shard_map/finish/pallas_call | solution.py:45
  (36 shorter events, 16.9 us)
Async XLA Ops:
  0.6 9.0 %collective-permute-start.3 = (bf16[1024,128]{1,0:T(8,128)(2,1)}, bf16[1024,128]{1,0:T(8,128)(2,1)S(1)}, u32[]{:S(2)}, u32[]{:S(2)}) collective-permute-start(bf16[1024,128]{1,0:T(8,128)(2,1)} %frames.1), channel_id=1, source_target_pairs={{1,0},{0,1},{3,2},{2,3},{5,4},{4,5},{7,6},{6,7},{9,8},{8,9},{11,10... | collective-permute-start | bytes 786440 | tf_op jit(solution)/shard_map/ppermute | solution.py:342
  3.8 6.8 %collective-permute-start.2 = (bf16[336,128]{1,0:T(8,128)(2,1)S(1)}, bf16[336,128]{1,0:T(8,128)(2,1)S(1)}, u32[]{:S(2)}, u32[]{:S(2)}) collective-permute-start(bf16[336,128]{1,0:T(8,128)(2,1)S(1)} %get-tuple-element.40.a), channel_id=1, source_target_pairs={{6,0},{25,1},{4,2},{27,3},{2,4},{29,5},{0,6},{31,7},{14,8},{17,9},... | collective-permute-start | bytes 258056 | tf_op jit(solution)/shard_map/ppermute | solution.py:342
  7.8 4.9 %collective-permute-start.1 = (bf16[336,128]{1,0:T(8,128)(2,1)S(1)}, bf16[336,128]{1,0:T(8,128)(2,1)S(1)}, u32[]{:S(2)}, u32[]{:S(2)}) collective-permute-start(bf16[336,128]{1,0:T(8,128)(2,1)S(1)} %get-tuple-element.40.a), channel_id=1, source_target_pairs={{4,0},{17,1},{6,2},{19,3},{0,4},{21,5},{2,6},{23,7},{12,8},{25,9},... | collective-permute-start | bytes 258056 | tf_op jit(solution)/shard_map/ppermute | solution.py:342
  7.8 4.9 %collective-permute-start = (bf16[336,128]{1,0:T(8,128)(2,1)S(1)}, bf16[336,128]{1,0:T(8,128)(2,1)S(1)}, u32[]{:S(2)}, u32[]{:S(2)}) collective-permute-start(bf16[336,128]{1,0:T(8,128)(2,1)S(1)} %get-tuple-element.40.a), channel_id=1, source_target_pairs={{2,0},{9,1},{0,2},{11,3},{6,4},{13,5},{4,6},{15,7},{10,8},{1,9},{8... | collective-permute-start | bytes 258056 | tf_op jit(solution)/shard_map/ppermute | solution.py:342
  8.4 1.2 collective-permute-start.4
  12.7 6.5 %collective-permute-start.5 = (bf16[4,336,128]{2,1,0:T(8,128)(2,1)S(1)}, bf16[4,336,128]{2,1,0:T(8,128)(2,1)S(1)}, u32[]{:S(2)}, u32[]{:S(2)}) collective-permute-start(bf16[4,336,128]{2,1,0:T(8,128)(2,1)S(1)} %stack.9.pieces.g0), channel_id=1, source_target_pairs={{8,0},{3,1},{10,2},{1,3},{12,4},{7,5},{14,6},{5,7},{0,8},{11,9},{2... | collective-permute-start | bytes 1032200 | tf_op jit(solution)/shard_map/ppermute | solution.py:342
  14.0 9.8 %collective-permute-start.7 = (bf16[4,336,128]{2,1,0:T(8,128)(2,1)S(1)}, bf16[4,336,128]{2,1,0:T(8,128)(2,1)S(1)}, u32[]{:S(2)}, u32[]{:S(2)}) collective-permute-start(bf16[4,336,128]{2,1,0:T(8,128)(2,1)S(1)} %stack.9.pieces.g0), channel_id=1, source_target_pairs={{24,0},{7,1},{26,2},{5,3},{28,4},{3,5},{30,6},{1,7},{16,8},{15,9},... | collective-permute-start | bytes 1032200 | tf_op jit(solution)/shard_map/ppermute | solution.py:342
  15.9 10.2 %collective-permute-start.6 = (bf16[4,336,128]{2,1,0:T(8,128)(2,1)S(1)}, bf16[4,336,128]{2,1,0:T(8,128)(2,1)S(1)}, u32[]{:S(2)}, u32[]{:S(2)}) collective-permute-start(bf16[4,336,128]{2,1,0:T(8,128)(2,1)S(1)} %stack.9.pieces.g0), channel_id=1, source_target_pairs={{16,0},{5,1},{18,2},{7,3},{20,4},{1,5},{22,6},{3,7},{24,8},{13,9},... | collective-permute-start | bytes 1032200 | tf_op jit(solution)/shard_map/ppermute | solution.py:342
  68.0 2.4 %collective-permute-start.8 = (f32[16,1024]{1,0:T(8,128)S(1)}, f32[16,1024]{1,0:T(8,128)S(1)}, u32[]{:S(2)}, u32[]{:S(2)}) collective-permute-start(f32[16,1024]{1,0:T(8,128)S(1)} %get-tuple-element.57), channel_id=1, source_target_pairs={{1,0},{0,1},{3,2},{2,3},{5,4},{4,5},{7,6},{6,7},{9,8},{8,9},{11,10... | collective-permute-start | bytes 196616 | tf_op jit(solution)/shard_map/ppermute | solution.py:342
  71.0 3.9 %collective-permute-start.9 = (f32[24,256]{1,0:T(8,128)S(1)}, f32[24,256]{1,0:T(8,128)S(1)}, u32[]{:S(2)}, u32[]{:S(2)}) collective-permute-start(f32[24,256]{1,0:T(8,128)S(1)} %get-tuple-element.59), channel_id=1, source_target_pairs={{32,0},{33,1},{34,2},{35,3},{36,4},{37,5},{38,6},{39,7},{40,8},{41... | collective-permute-start | bytes 73736 | tf_op jit(solution)/shard_map/ppermute | solution.py:342
  71.4 4.2 %collective-permute-start.10 = (f32[24,256]{1,0:T(8,128)S(1)}, f32[24,256]{1,0:T(8,128)S(1)}, u32[]{:S(2)}, u32[]{:S(2)}) collective-permute-start(f32[24,256]{1,0:T(8,128)S(1)} %get-tuple-element.60), channel_id=1, source_target_pairs={{64,0},{65,1},{66,2},{67,3},{68,4},{69,5},{70,6},{71,7},{72,8},{73... | collective-permute-start | bytes 73736 | tf_op jit(solution)/shard_map/ppermute | solution.py:342
  73.1 3.9 %collective-permute-start.11 = (f32[24,256]{1,0:T(8,128)S(1)}, f32[24,256]{1,0:T(8,128)S(1)}, u32[]{:S(2)}, u32[]{:S(2)}) collective-permute-start(f32[24,256]{1,0:T(8,128)S(1)} %get-tuple-element.61), channel_id=1, source_target_pairs={{96,0},{97,1},{98,2},{99,3},{100,4},{101,5},{102,6},{103,7},{104,8... | collective-permute-start | bytes 73736 | tf_op jit(solution)/shard_map/ppermute | solution.py:342
  90.7 5.1 %collective-permute-start.12 = (f32[16,1152]{1,0:T(8,128)S(1)}, f32[16,1152]{1,0:T(8,128)S(1)}, u32[]{:S(2)}, u32[]{:S(2)}) collective-permute-start(f32[16,1152]{1,0:T(8,128)S(1)} %get-tuple-element.66), channel_id=1, source_target_pairs={{1,0},{0,1},{3,2},{2,3},{5,4},{4,5},{7,6},{6,7},{9,8},{8,9},{11,10... | collective-permute-start | bytes 221192 | tf_op jit(solution)/shard_map/ppermute | solution.py:342
  96.4 3.9 %collective-permute-start.13 = (f32[16,384]{1,0:T(8,128)S(1)}, f32[16,384]{1,0:T(8,128)S(1)}, u32[]{:S(2)}, u32[]{:S(2)}) collective-permute-start(f32[16,384]{1,0:T(8,128)S(1)} %get-tuple-element.69), channel_id=1, source_target_pairs={{32,0},{33,1},{34,2},{35,3},{36,4},{37,5},{38,6},{39,7},{40,8},{41... | collective-permute-start | bytes 73736 | tf_op jit(solution)/shard_map/ppermute | solution.py:342
  96.5 4.4 %collective-permute-start.14 = (f32[16,384]{1,0:T(8,128)S(1)}, f32[16,384]{1,0:T(8,128)S(1)}, u32[]{:S(2)}, u32[]{:S(2)}) collective-permute-start(f32[16,384]{1,0:T(8,128)S(1)} %get-tuple-element.70), channel_id=1, source_target_pairs={{64,0},{65,1},{66,2},{67,3},{68,4},{69,5},{70,6},{71,7},{72,8},{73... | collective-permute-start | bytes 73736 | tf_op jit(solution)/shard_map/ppermute | solution.py:342
  99.3 3.9 %collective-permute-start.15 = (f32[16,384]{1,0:T(8,128)S(1)}, f32[16,384]{1,0:T(8,128)S(1)}, u32[]{:S(2)}, u32[]{:S(2)}) collective-permute-start(f32[16,384]{1,0:T(8,128)S(1)} %get-tuple-element.71), channel_id=1, source_target_pairs={{96,0},{97,1},{98,2},{99,3},{100,4},{101,5},{102,6},{103,7},{104,8... | collective-permute-start | bytes 73736 | tf_op jit(solution)/shard_map/ppermute | solution.py:342
  117.0 5.3 %collective-permute-start.16 = (f32[16,1152]{1,0:T(8,128)S(1)}, f32[16,1152]{1,0:T(8,128)S(1)}, u32[]{:S(2)}, u32[]{:S(2)}) collective-permute-start(f32[16,1152]{1,0:T(8,128)S(1)} %get-tuple-element.73), channel_id=1, source_target_pairs={{1,0},{0,1},{3,2},{2,3},{5,4},{4,5},{7,6},{6,7},{9,8},{8,9},{11,10... | collective-permute-start | bytes 221192 | tf_op jit(solution)/shard_map/ppermute | solution.py:342
  122.4 5.2 %collective-permute-start.19 = (f32[16,1152]{1,0:T(8,128)S(1)}, f32[16,1152]{1,0:T(8,128)S(1)}, u32[]{:S(2)}, u32[]{:S(2)}) collective-permute-start(f32[16,1152]{1,0:T(8,128)S(1)} %core_add.1.q0), channel_id=1, source_target_pairs={{96,0},{97,1},{98,2},{99,3},{100,4},{101,5},{102,6},{103,7},{104,8... | collective-permute-start | bytes 221192 | tf_op jit(solution)/shard_map/ppermute | solution.py:342
  123.5 5.1 %collective-permute-start.18 = (f32[16,1152]{1,0:T(8,128)S(1)}, f32[16,1152]{1,0:T(8,128)S(1)}, u32[]{:S(2)}, u32[]{:S(2)}) collective-permute-start(f32[16,1152]{1,0:T(8,128)S(1)} %core_add.1.q0), channel_id=1, source_target_pairs={{64,0},{65,1},{66,2},{67,3},{68,4},{69,5},{70,6},{71,7},{72,8},{73... | collective-permute-start | bytes 221192 | tf_op jit(solution)/shard_map/ppermute | solution.py:342
  123.5 5.8 %collective-permute-start.17 = (f32[16,1152]{1,0:T(8,128)S(1)}, f32[16,1152]{1,0:T(8,128)S(1)}, u32[]{:S(2)}, u32[]{:S(2)}) collective-permute-start(f32[16,1152]{1,0:T(8,128)S(1)} %core_add.1.q0), channel_id=1, source_target_pairs={{32,0},{33,1},{34,2},{35,3},{36,4},{37,5},{38,6},{39,7},{40,8},{41... | collective-permute-start | bytes 221192 | tf_op jit(solution)/shard_map/ppermute | solution.py:342

commit v4 on v3

--- a/solution.py
+++ b/solution.py
@@ -67,6 +67,7 @@
 
 
 def pack_kernel(pos, frames, classes, start, piece, cls_out, mine, quarter, own_classes, sems):
+    x = pos[0]
     at = pl.multiple_of(pos[0] * QB, QB)
     copies = (
         pltpu.make_async_copy(frames.at[pl.ds(at, QB), :], piece.at[0:QB, :], sems.at[0]),
@@ -78,10 +79,20 @@
         copy.start()
     for copy in copies:
         copy.wait()
-    cls = own_classes[...].astype(F32)
-    cls = jnp.concatenate([cls, jnp.zeros_like(cls)], axis=0).astype(BF16)
-    piece[CLS:PROWS, :] = cls
-    cls_out[...] = cls
+    cls_out[...] = own_classes[...]
+    wide = piece[0:QB, :].astype(F32)
+    square = wide * wide
+    upper = square.astype(BF16)
+    lower = (square - upper.astype(F32)).astype(BF16)
+    ones = jnp.ones((8, F), BF16)
+    half = -0.5 * (dot(ones, upper, NT) + dot(ones, lower, NT))[0:1]
+    p1 = half.astype(BF16).astype(F32)
+    p2 = (half - p1).astype(BF16).astype(F32)
+    extra = [p[:, h * 128 : (h + 1) * 128] for p in (p1, p2, half - p1 - p2) for h in range(2)]
+    extra.append(own_classes[pl.ds(2 * x, 1), :].astype(F32))
+    extra.append(own_classes[pl.ds(2 * x + 1, 1), :].astype(F32))
+    extra.append(jnp.ones((8, 128), F32))
+    piece[CLS:PROWS, :] = jnp.concatenate(extra, axis=0).astype(BF16)
     high = quarter[...].astype(BF16)
     low = (quarter[...] - high.astype(F32)).astype(BF16)
     for h in range(2):
@@ -90,24 +101,21 @@
         piece[at + KV : at + 2 * KV, :] = low[:, h * 128 : (h + 1) * 128]
 
 
-def stack_kernel(a, b, c, d, ready, out):
+def stack_kernel(a, b, d, c, ready, out):
     del ready
     for n, ref in enumerate((a, b, c, d)):
         out[n] = ref[...]
 
 
-def augment(rows, own_first):
+def augment(rows):
     wide = rows.astype(F32)
     half = -0.5 * jnp.sum(wide * wide, axis=1, keepdims=True)
     p1 = half.astype(BF16).astype(F32)
     p2 = (half - p1).astype(BF16).astype(F32)
-    p3 = half - p1 - p2
     lane = lax.broadcasted_iota(jnp.int32, (rows.shape[0], 128), 1)
-    first = 0 if own_first else 3
-    ones = jnp.logical_and(lane >= 3 - first, lane < 6 - first)
-    extra = jnp.where(ones, 1.0, 0.0)
-    for n, part in enumerate((p1, p2, p3)):
-        extra = jnp.where(lane == first + n, part, extra)
+    extra = jnp.where(lane < 3, 1.0, 0.0)
+    for n, part in enumerate((p1, p2, half - p1 - p2)):
+        extra = jnp.where(lane == 3 + n, part, extra)
     return jnp.concatenate([rows, extra.astype(BF16)], axis=1)
 
 
@@ -115,56 +123,55 @@
     return jnp.exp2(cls * (-math.log2(width_growth))) * (1.0 / base_width)
 
 
-def side_kernel(pos, mine, mine_cls, other, other_cls, aug_j, coef_j):
-    c = pos[1]
-
-    def side(blocks):
-        for n, (rows, cls) in enumerate(blocks):
-            aug_j[n * CB : (n + 1) * CB, :] = augment(rows[...], False)
-            coef = inverse_width(cls[...].astype(F32)) * (2.0 * math.log2(math.e))
-            for r in range(8):
-                lo = n * CB + r * 128
-                coef_j[:, lo : lo + 128] = coef[r : r + 1, :]
-
-    @pl.when(c == 0)
-    def _():
-        side(((mine, mine_cls), (other, other_cls)))
-
-    @pl.when(c != 0)
-    def _():
-        side(((other, other_cls), (mine, mine_cls)))
-
-
-def spread(sum_j, out):
-    for n in range(128):
-        lo = n % 2 * CB + n // 2 % 4 * QB
-        out[n] = sum_j[:, lo : lo + QB]
-
-
-def rows_kernel(group, pos, pieces, aug_j, coef_j, *refs):
+def side_kernel(rows, cls, aug_j, coef_j):
+    aug_j[...] = augment(rows[...])
+    coef = inverse_width(cls[...].astype(F32)) * (2.0 * math.log2(math.e))
+    for r in range(8):
+        coef_j[:, r * 128 : (r + 1) * 128] = coef[r : r + 1, :]
+
+
+def spread(row, c, out):
+    for quarter in range(4):
+        lo = quarter * QB
+        own, other = row[:, lo : lo + QB], row[:, CB + lo : CB + lo + QB]
+        for core in range(2):
+            value = jnp.where(c == core, own, other)
+            for n in range(16):
+                out[8 * n + 2 * quarter + core] = value
+
+
+def rows_kernel(group, pos, pieces, aug_own, coef_own, aug_other, coef_other, *refs):
     k_ref, out = refs[-2:]
-    x = pos[0]
-    augs, coefs = [], []
     row = lax.broadcasted_iota(jnp.int32, (16, 128), 0)
-    ones = jnp.ones((16, 128), BF16)
-    for n in range(4):
-        augs.append(augment(pieces[n, 0:QB, :], True))
-        cls = pieces[n, CLS:PROWS, :].astype(F32)
-        for h in range(2):
-            one_row = jnp.where(row == 2 * x + h, cls, 0.0).astype(BF16)
-            coefs.append(inverse_width(dot(one_row, ones, TN)[:, :1]))
+    lane = lax.broadcasted_iota(jnp.int32, (16, 128), 1)
+    picks = []
+    for h in range(2):
+        parts = jnp.logical_and(lane < 3, row == 2 * lane + h)
+        ones = jnp.logical_and(jnp.logical_and(lane >= 3, lane < 6), row == 8)
+        cls = jnp.logical_and(lane == 8, row == 6 + h)
+        pick = jnp.logical_or(jnp.logical_or(parts, ones), cls)
+        picks.append(jnp.where(pick, 1.0, 0.0).astype(BF16))
     half = 512
-    total = jnp.zeros((8, NJ), F32) if group == 0 else refs[0][...]
+    sides = ((0, aug_own, coef_own), (CB, aug_other, coef_other))
+    totals = [jnp.zeros((8, CB), F32) if group == 0 else refs[0][:, lo : lo + CB] for lo, _, _ in sides]
     for n in range(2):
-        aug_i = jnp.concatenate(augs[2 * n : 2 * n + 2], axis=0)
-        coef_i = jnp.concatenate(coefs[4 * n : 4 * n + 4], axis=0)
-        e = jnp.exp2(dot(aug_i, aug_j[...], NT) * coef_i * coef_j[...])
-        k_ref[n * half : (n + 1) * half, :] = e.astype(BF16)
-        total = total + jnp.sum(e.reshape(half // 8, 8, NJ), axis=0)
+        columns = [
+            dot(pieces[m, CLS:PROWS, :], pick, TN) for m in (2 * n, 2 * n + 1) for pick in picks
+        ]
+        columns = jnp.concatenate(columns, axis=0)
+        rows = jnp.concatenate([pieces[2 * n, 0:QB, :], pieces[2 * n + 1, 0:QB, :]], axis=0)
+        aug_i = jnp.concatenate([rows, columns.astype(BF16)], axis=1)
+        coef_i = inverse_width(columns[:, 8:9])
+        for s, (lo, aug, coef) in enumerate(sides):
+            e = jnp.exp2(dot(aug_i, aug[...], NT) * coef_i * coef[...])
+            k_ref[n * half : (n + 1) * half, lo : lo + CB] = e.astype(BF16)
+            totals[s] = totals[s] + jnp.sum(e.reshape(half // 8, 8, CB), axis=0)
     if group == LAST_GROUP:
-        spread(jnp.sum(total, axis=0, keepdims=True), out)
+        total = jnp.concatenate(totals, axis=1)
+        spread(jnp.sum(total, axis=0, keepdims=True), pos[1], out)
     else:
-        out[...] = total
+        for total, (lo, _, _) in zip(totals, sides):
+            out[:, lo : lo + CB] = total
 
 
 def side_i(pos, table, row):
@@ -186,11 +193,10 @@
     side_i(pos, table, dens_i)
     dens_i[...] = dens_i[...] * (1.0 / NTOT)
     inverse = jnp.broadcast_to(1.0 / dens_i[...], (8, NI)).astype(BF16)
-    spread(apply_k(inverse, (k0, k1, k2, k3))[0:1], out)
-
-
-def half(c):
-    return pl.ds(pl.multiple_of(c * CB, CB), CB)
+    spread(apply_k(inverse, (k0, k1, k2, k3))[0:1], pos[1], out)
+
+
+OWN, AWAY = slice(0, CB), slice(CB, NJ)
 
 
 def first_kernel(
@@ -211,11 +217,11 @@
                 lo = at + h * 128
                 part = (both[:KV] + both[KV:]) * weight_i[:, lo : lo + 128]
                 vec[:, lo : lo + 128] = part.astype(BF16)
-    away[...] = apply_k(vec, (k0, k1, k2, k3), half(1 - pos[1]))
-
-
-def own_kernel(pos, k0, k1, k2, k3, vec, own):
-    y = apply_k(vec, (k0, k1, k2, k3), half(pos[1]))
+    away[...] = apply_k(vec, (k0, k1, k2, k3), AWAY)
+
+
+def own_kernel(k0, k1, k2, k3, vec, own):
+    y = apply_k(vec, (k0, k1, k2, k3), OWN)
     if vec.shape[0] == 2 * KV:
         y = y[:KV] + y[KV:]
     own[...] = y
@@ -240,7 +246,7 @@
     square = rows[:, 0:KV] + rows[:, KV : 2 * KV] + rows[:, 2 * KV :]
     square = jnp.concatenate([square, jnp.zeros((KV, 128 - KV), F32)], axis=1)
     gram[...] = square
-    y2 = apply_k(vec, (k0, k1, k2, k3), half(1 - pos[1]))
+    y2 = apply_k(vec, (k0, k1, k2, k3), AWAY)
     away[:, :CB] = y2[0:KV] + y2[KV:]
     away[:, CB:] = square
 
@@ -286,7 +292,7 @@
     p = y * weight_log[0:1, :]
     for n in range(16):
         out[n] = p
-    for d, ref in enumerate((q0, q1, q2, q3)):
+    for d, ref in zip((0, 2, 1, 3), (q0, q1, q2, q3)):
         at = pl.ds(pl.multiple_of((pos[0] ^ d) * QB, QB), QB)
         weight_own[:, at] = ref[KV : KV + 1, :]
         log_degree[:, at] = ref[KV + 1 : KV + 2, :]
@@ -369,7 +375,7 @@
     piece, cls, mine = call(
         pack_kernel,
         "pack",
-        [sds((PROWS, F), BF16), sds((16, 128), BF16), vmem((CB, F), BF16)],
+        [sds((PROWS, F), BF16), sds((8, 128), jnp.int32), vmem((CB, F), BF16)],
         (pos, *(pltpu.with_memory_space_constraint(a, pltpu.HBM) for a in (frames, classes, start))),
         scratch=[
             pltpu.VMEM((KV, QB), F32),
@@ -378,15 +384,15 @@
         ],
         far=(1, 2, 3),
     )
-    line = [piece] + [from_line(piece, d) for d in (1, 2, 3)]
-    aug_j, coef_j = call(
-        side_kernel,
-        "side",
-        [sds((NJ, 2 * F), BF16), sds((1, NJ))],
-        (pos, keep(mine), cls, from_core(frames), from_core(cls)),
-        flops=NJ * 4000,
-    )
-    line = call(stack_kernel, "stack", sds((4, PROWS, F), BF16), (*line, coef_j))
+    line = [piece] + [from_line(piece, d) for d in (1, 3, 2)]
+    shapes = [sds((CB, 2 * F), BF16), sds((1, CB))]
+    own_side = call(side_kernel, "own_side", shapes, (keep(mine), cls), flops=CB * 4000)
+    sides = own_side + call(
+        side_kernel, "other_side", shapes, (from_core(frames), from_core(classes)), flops=CB * 4000
+    )
+    line = call(
+        stack_kernel, "stack", sds((4, PROWS, F), BF16), (*line, own_side[1])
+    )
     groups = [line] + [from_line(line, d, True) for d in (1, 2, 3)]
     ks, sums = [None] * 4, ()
     for g in GROUPS:
@@ -394,7 +400,7 @@
             functools.partial(rows_kernel, g),
             f"rows{g}",
             [vmem((4 * QB, NJ), BF16), sds((128, 1, QB) if g == LAST_GROUP else (8, NJ))],
-            (pos, groups[g], aug_j, coef_j) + (() if g == 0 else (sums,)),
+            (pos, groups[g], *sides) + (() if g == 0 else (sums,)),
             flops=4 * QB * NJ * 1024,
         )
 
@@ -418,7 +424,7 @@
     flops = 2 * NI * CB * 256
 
     def own_half(iteration):
-        return call(own_kernel, f"own{iteration}", sds((KV, CB)), (pos, *tile(), vec), flops=flops)
+        return call(own_kernel, f"own{iteration}", sds((KV, CB)), (*tile(), vec), flops=flops)
 
     for iteration in range(1, ITERS):
         shape = (KV + 8, QB) if iteration == 1 else (KV, QB + 128)
@@ -428,7 +434,7 @@
             [sds(shape)] * 4,
             (pos, own_half(iteration), from_core(away), weight_log if iteration == 1 else square),
         )
-        quarters = [quarters[0]] + [from_x(quarters[d], d) for d in (1, 2, 3)]
+        quarters = [quarters[0]] + [from_x(quarters[d], d) for d in (2, 1, 3)]
         if iteration == 1:
             pieces, weight_own, log_degree = call(
                 project_first_kernel,
@@ -457,7 +463,7 @@
         sds((KV, CB + 128)),
         (own_half(ITERS), from_core(away), square),
     )
-    totals = [total] + [from_x(total, d) for d in (1, 2, 3)]
+    totals = [total] + [from_x(total, d) for d in (1, 3, 2)]
     proj, grams = call(
         last_kernel, "last", [sds((KV, CB)), sds((32, 8, 128))], (weight_own, *totals)
     )

time: 146 us -> 142 us (0.973)
  waiting for transfers between devices: 14.2 us -> 17.5 us
  blocking collectives: 68.2 us -> 65.2 us
  Pallas kernels: 33.8 us -> 31.8 us
  starting transfers between devices: 28.4 us -> 26.6 us
    ppermute x20, waiting for transfers between devices: 14.2 us -> 17.5 us  [shift(): return lax.ppermute(v, ('x', 'z', 'y', 'c'), pairs)]
    all_to_all x1, blocking collectives: 20.6 us -> 18.1 us  [body(): lax.all_to_all(sums, everyone, 0, 0)]
    pallas_call x21 -> x22, Pallas kernels: 33.8 us -> 31.8 us  [call(): pl.pallas_call(kernel, out_shape=outs, in_specs=[spec(n, a) for n, a in e...]
    ppermute x20, starting transfers between devices: 28.4 us -> 26.6 us  [shift(): return lax.ppermute(v, ('x', 'z', 'y', 'c'), pairs)]
  transfers between devices with their start and end apart: 20 -> 20, of which waited for: 11 -> 9; matrix products, arithmetic and copies ran while one was open for 0% -> 0% of each run, Pallas kernels for 10% -> 9%
where the time goes in v4:
time: 142 us
  blocking collectives  65.2 us (46%)
  Pallas kernels  31.8 us (22%)
  starting transfers between devices  26.6 us (19%)
  waiting for transfers between devices  17.5 us (12%)
    pallas_call x22, Pallas kernels, call(): pl.pallas_call(kernel, out_shape=outs, in_specs=[spec(n, a) for n, a in e...  31.8 us
    ppermute x20, starting transfers between devices, shift(): return lax.ppermute(v, ('x', 'z', 'y', 'c'), pairs)  26.6 us
    all_to_all x2, blocking collectives, body(): pieces = lax.all_to_all(pieces, ('y', 'z'), 0, 0)  21.1 us
    all_to_all x1, blocking collectives, body(): lax.all_to_all(sums, everyone, 0, 0)  18.1 us
    ppermute x20, waiting for transfers between devices, shift(): return lax.ppermute(v, ('x', 'z', 'y', 'c'), pairs)  17.5 us
    all_to_all x1, blocking collectives, body(): lax.all_to_all(table, everyone, 0, 0)  14.3 us
    all_to_all x1, blocking collectives, body(): grams = lax.all_to_all(grams, ('z', 'y', 'c'), 0, 0)  11.8 us
  transfers between devices with their start and end apart: 20, of which 9 were waited for; matrix products, arithmetic and copies ran while one was open for 0% of the time, Pallas kernels for 9%

profile of v4, /device:TPU:1, one launch (start us, length us, event | category | flops | bytes accessed | tf_op | source)
XLA Modules:
  0.0 142.1 jit_solution(1699644465081854456)
XLA Ops:
  0.6 1.5 %collective-permute-start.3 = (bf16[1024,128]{1,0:T(8,128)(2,1)}, bf16[1024,128]{1,0:T(8,128)(2,1)S(1)}, u32[]{:S(2)}, u32[]{:S(2)}) collective-permute-start(bf16[1024,128]{1,0:T(8,128)(2,1)} %frames.1), channel_id=1, source_target_pairs={{1,0},{0,1},{3,2},{2,3},{5,4},{4,5},{7,6},{6,7},{9,8},{8,9},{11,10... | collective-permute-start | bytes 786440 | tf_op jit(solution)/shard_map/ppermute | solution.py:348
  2.2 1.8 %pack.1 = (bf16[336,128]{1,0:T(8,128)(2,1)S(1)}, s32[8,128]{1,0:T(8,128)S(1)}, bf16[1024,128]{1,0:T(8,128)(2,1)S(1)}) custom-call(s32[18]{0:T(128)S(1)} %pad_add_fusion.pos, bf16[1024,128]{1,0:T(8,128)(2,1)} %frames.1, s32[8,128]{1,0:T(8,128)} %bitcast.4, f32[16,1024]{1,0:T(8,128)} %start.1), custom_call_target="tpu_custom_call" | custom-call | tf_op jit(solution)/shard_map/pack/pallas_call | solution.py:45
  4.0 3.8 %collective-permute-start.2 = (bf16[336,128]{1,0:T(8,128)(2,1)S(1)}, bf16[336,128]{1,0:T(8,128)(2,1)S(1)}, u32[]{:S(2)}, u32[]{:S(2)}) collective-permute-start(bf16[336,128]{1,0:T(8,128)(2,1)S(1)} %get-tuple-element.42.a), channel_id=1, source_target_pairs={{4,0},{17,1},{6,2},{19,3},{0,4},{21,5},{2,6},{23,7},{12,8},{25,9},... | collective-permute-start | bytes 258056 | tf_op jit(solution)/shard_map/ppermute | solution.py:348
  9.7 2.9 %collective-permute-done.1.d = bf16[336,128]{1,0:T(8,128)(2,1)S(1)} collective-permute-done((bf16[336,128]{1,0:T(8,128)(2,1)S(1)}, bf16[336,128]{1,0:T(8,128)(2,1)S(1)}, u32[]{:S(2)}, u32[]{:S(2)}) %collective-permute-start.1) | collective-permute-done | bytes 86048 | tf_op jit(solution)/shard_map/ppermute | solution.py:348
  13.7 1.4 collective-permute-start.4
  15.1 1.7 %collective-permute-start.7 = (bf16[4,336,128]{2,1,0:T(8,128)(2,1)S(1)}, bf16[4,336,128]{2,1,0:T(8,128)(2,1)S(1)}, u32[]{:S(2)}, u32[]{:S(2)}) collective-permute-start(bf16[4,336,128]{2,1,0:T(8,128)(2,1)S(1)} %stack.9.pieces.g0), channel_id=1, source_target_pairs={{24,0},{7,1},{26,2},{5,3},{28,4},{3,5},{30,6},{1,7},{16,8},{15,9},... | collective-permute-start | bytes 1032200 | tf_op jit(solution)/shard_map/ppermute | solution.py:348
  17.2 2.3 %rows0.1 = (bf16[1024,2048]{1,0:T(8,128)(2,1)S(1)}, f32[8,2048]{1,0:T(8,128)S(1)}) custom-call(s32[18]{0:T(128)S(1)} %pad_add_fusion.pos, bf16[4,336,128]{2,1,0:T(8,128)(2,1)S(1)} %stack.9.pieces.g0, bf16[1024,256]{1,0:T(8,128)(2,1)S(1)} %get-tuple-element.46.aug_own, f32[1,1024]{1,0:T(1,128)S(1)} %get-tuple-element.45.ready.coef_own, ...), custom_call_target="tpu_custom_call" | custom-call | flops 2147483648 | tf_op jit(solution)/shard_map/rows0/pallas_call | solution.py:45
  19.5 2.3 %rows1.1 = (bf16[1024,2048]{1,0:T(8,128)(2,1)S(1)}, f32[8,2048]{1,0:T(8,128)S(1)}) custom-call(s32[18]{0:T(128)S(1)} %pad_add_fusion.pos, bf16[4,336,128]{2,1,0:T(8,128)(2,1)S(1)} %collective-permute-done.5.pieces.g1, bf16[1024,256]{1,0:T(8,128)(2,1)S(1)} %get-tuple-element.46.aug_own, f32[1,1024]{1,0:T(1,128)S(1)} %get-tuple-element.45.ready.coef_own, ...), custom_call_target="tpu_custom_call" | custom-call | flops 2147483648 | tf_op jit(solution)/shard_map/rows1/pallas_call | solution.py:45
  21.8 4.6 %collective-permute-done.7.pieces.g3 = bf16[4,336,128]{2,1,0:T(8,128)(2,1)S(1)} collective-permute-done((bf16[4,336,128]{2,1,0:T(8,128)(2,1)S(1)}, bf16[4,336,128]{2,1,0:T(8,128)(2,1)S(1)}, u32[]{:S(2)}, u32[]{:S(2)}) %collective-permute-start.7) | collective-permute-done | bytes 344096 | tf_op jit(solution)/shard_map/ppermute | solution.py:348
  26.4 2.3 %rows3.1 = (bf16[1024,2048]{1,0:T(8,128)(2,1)S(1)}, f32[8,2048]{1,0:T(8,128)S(1)}) custom-call(s32[18]{0:T(128)S(1)} %pad_add_fusion.pos, bf16[4,336,128]{2,1,0:T(8,128)(2,1)S(1)} %collective-permute-done.7.pieces.g3, bf16[1024,256]{1,0:T(8,128)(2,1)S(1)} %get-tuple-element.46.aug_own, f32[1,1024]{1,0:T(1,128)S(1)} %get-tuple-element.45.ready.coef_own, ...), custom_call_target="tpu_custom_call" | custom-call | flops 2147483648 | tf_op jit(solution)/shard_map/rows3/pallas_call | solution.py:45
  28.7 2.4 %rows2.1 = (bf16[1024,2048]{1,0:T(8,128)(2,1)S(1)}, f32[128,1,256]{2,1,0:T(1,128)S(1)}) custom-call(s32[18]{0:T(128)S(1)} %pad_add_fusion.pos, bf16[4,336,128]{2,1,0:T(8,128)(2,1)S(1)} %collective-permute-done.6.pieces.g2, bf16[1024,256]{1,0:T(8,128)(2,1)S(1)} %get-tuple-element.46.aug_own, f32[1,1024]{1,0:T(1,128)S(1)} %get-tuple-element.45.ready.coef_own, ...), custom_call_target="tpu_custom_call" | custom-call | flops 2147483648 | tf_op jit(solution)/shard_map/rows2/pallas_call | solution.py:45
  31.1 18.1 %all_to_all.25.table = f32[128,1,256]{2,1,0:T(1,128)S(1)} all-to-all(f32[128,1,256]{2,1,0:T(1,128)S(1)} %get-tuple-element.56), channel_id=1, replica_groups=mesh['x'=4,'z'=4,'y'=4,'c'=2] {'y','z','x','c'}, dimensions={0} | all-to-all | bytes 262144 | tf_op jit(solution)/shard_map/all_to_all | solution.py:415
  49.2 2.8 %degree.1 = (f32[1,4096]{1,0:T(1,128)S(1)}, f32[128,1,256]{2,1,0:T(1,128)S(1)}) custom-call(s32[18]{0:T(128)S(1)} %pad_add_fusion.pos, bf16[1024,2048]{1,0:T(8,128)(2,1)S(1)} %get-tuple-element.49.k0, bf16[1024,2048]{1,0:T(8,128)(2,1)S(1)} %get-tuple-element.51.k1, bf16[1024,2048]{1,0:T(8,128)(2,1)S(1)} %get-tuple-element.54.k2, ...), custom_call_target="tpu_custom_call" | custom-call | tf_op jit(solution)/shard_map/degree/pallas_call | solution.py:45
  52.0 14.3 %all_to_all.26.table = f32[128,1,256]{2,1,0:T(1,128)S(1)} all-to-all(f32[128,1,256]{2,1,0:T(1,128)S(1)} %get-tuple-element.58), channel_id=1, replica_groups=mesh['x'=4,'z'=4,'y'=4,'c'=2] {'y','z','x','c'}, dimensions={0} | all-to-all | bytes 262144 | tf_op jit(solution)/shard_map/all_to_all | solution.py:421
  66.3 1.8 %first.1 = (bf16[16,4096]{1,0:T(8,128)(2,1)S(1)}, f32[1,4096]{1,0:T(1,128)S(1)}, f32[8,256]{1,0:T(8,128)S(1)}, f32[16,1024]{1,0:T(8,128)S(1)}) custom-call(s32[18]{0:T(128)S(1)} %pad_add_fusion.pos, bf16[1024,2048]{1,0:T(8,128)(2,1)S(1)} %get-tuple-element.49.k0, bf16[1024,2048]{1,0:T(8,128)(2,1)S(1)} %get-tuple-element.51.k1, ...), custom_call_target="tpu_custom_call" | custom-call | tf_op jit(solution)/shard_map/first/pallas_call | solution.py:45
  72.1 1.8 %collective-permute-start.11 = (f32[24,256]{1,0:T(8,128)S(1)}, f32[24,256]{1,0:T(8,128)S(1)}, u32[]{:S(2)}, u32[]{:S(2)}) collective-permute-start(f32[24,256]{1,0:T(8,128)S(1)} %get-tuple-element.65), channel_id=1, source_target_pairs={{96,0},{97,1},{98,2},{99,3},{100,4},{101,5},{102,6},{103,7},{104,8... | collective-permute-start | bytes 73736 | tf_op jit(solution)/shard_map/ppermute | solution.py:348
  77.1 10.5 %all_to_all.27.pieces = f32[16,16,256]{2,1,0:T(8,128)S(1)} all-to-all(f32[16,16,256]{2,1,0:T(8,128)S(1)} %get-tuple-element.68), channel_id=1, replica_groups=mesh['x'=4,'z'=4,'y'=4,'c'=2] {'y','z'}, dimensions={0} | all-to-all | bytes 524288 | tf_op jit(solution)/shard_map/all_to_all | solution.py:452
  87.7 2.0 %next1.1 = (bf16[32,4096]{1,0:T(8,128)(2,1)S(1)}, f32[16,128]{1,0:T(8,128)S(1)}, f32[16,1152]{1,0:T(8,128)S(1)}) custom-call(s32[18]{0:T(128)S(1)} %pad_add_fusion.pos, bf16[1024,2048]{1,0:T(8,128)(2,1)S(1)} %get-tuple-element.49.k0, bf16[1024,2048]{1,0:T(8,128)(2,1)S(1)} %get-tuple-element.51.k1, bf16[1024,2048]{1,0:T(8,128)(2,1)S(1)} %get-tuple-element.54.k2, ...), custom_call_target="tpu_custom_call" | custom-call | tf_op jit(solution)/shard_map/next1/pallas_call | solution.py:45
  89.6 3.2 %collective-permute-start.12 = (f32[16,1152]{1,0:T(8,128)S(1)}, f32[16,1152]{1,0:T(8,128)S(1)}, u32[]{:S(2)}, u32[]{:S(2)}) collective-permute-start(f32[16,1152]{1,0:T(8,128)S(1)} %get-tuple-element.70), channel_id=1, source_target_pairs={{1,0},{0,1},{3,2},{2,3},{5,4},{4,5},{7,6},{6,7},{9,8},{8,9},{11,10... | collective-permute-start | bytes 221192 | tf_op jit(solution)/shard_map/ppermute | solution.py:348
  92.8 1.4 %own2.1.own = f32[16,1024]{1,0:T(8,128)S(1)} custom-call(bf16[1024,2048]{1,0:T(8,128)(2,1)S(1)} %get-tuple-element.49.k0, bf16[1024,2048]{1,0:T(8,128)(2,1)S(1)} %get-tuple-element.51.k1, bf16[1024,2048]{1,0:T(8,128)(2,1)S(1)} %get-tuple-element.54.k2, bf16[1024,2048]{1,0:T(8,128)(2,1)S(1)} %get-tuple-element.55.k3, bf16[32,4096]{1,0:T(8,128)(2,1)S(1)} %get-tuple-element.69.vec), custom_call_target="tpu_custom_call" | custom-call | flops 2147483648 | tf_op jit(solution)/shard_map/own2/pallas_call | solution.py:45
  99.1 1.8 %collective-permute-done.15.q3 = f32[16,384]{1,0:T(8,128)S(1)} collective-permute-done((f32[16,384]{1,0:T(8,128)S(1)}, f32[16,384]{1,0:T(8,128)S(1)}, u32[]{:S(2)}, u32[]{:S(2)}) %collective-permute-start.15) | collective-permute-done | bytes 24608 | tf_op jit(solution)/shard_map/ppermute | solution.py:348
  100.9 1.4 project2.1
  102.3 10.5 %all_to_all.28.pieces = f32[16,16,256]{2,1,0:T(8,128)S(1)} all-to-all(f32[16,16,256]{2,1,0:T(8,128)S(1)} %project2.1), channel_id=1, replica_groups=mesh['x'=4,'z'=4,'y'=4,'c'=2] {'y','z'}, dimensions={0} | all-to-all | bytes 524288 | tf_op jit(solution)/shard_map/all_to_all | solution.py:452
  112.9 2.0 %next2.1 = (bf16[32,4096]{1,0:T(8,128)(2,1)S(1)}, f32[16,128]{1,0:T(8,128)S(1)}, f32[16,1152]{1,0:T(8,128)S(1)}) custom-call(s32[18]{0:T(128)S(1)} %pad_add_fusion.pos, bf16[1024,2048]{1,0:T(8,128)(2,1)S(1)} %get-tuple-element.49.k0, bf16[1024,2048]{1,0:T(8,128)(2,1)S(1)} %get-tuple-element.51.k1, bf16[1024,2048]{1,0:T(8,128)(2,1)S(1)} %get-tuple-element.54.k2, ...), custom_call_target="tpu_custom_call" | custom-call | tf_op jit(solution)/shard_map/next2/pallas_call | solution.py:45
  114.8 3.1 %collective-permute-start.16 = (f32[16,1152]{1,0:T(8,128)S(1)}, f32[16,1152]{1,0:T(8,128)S(1)}, u32[]{:S(2)}, u32[]{:S(2)}) collective-permute-start(f32[16,1152]{1,0:T(8,128)S(1)} %get-tuple-element.77), channel_id=1, source_target_pairs={{1,0},{0,1},{3,2},{2,3},{5,4},{4,5},{7,6},{6,7},{9,8},{8,9},{11,10... | collective-permute-start | bytes 221192 | tf_op jit(solution)/shard_map/ppermute | solution.py:348
  118.0 1.4 %own3.1.own = f32[16,1024]{1,0:T(8,128)S(1)} custom-call(bf16[1024,2048]{1,0:T(8,128)(2,1)S(1)} %get-tuple-element.49.k0, bf16[1024,2048]{1,0:T(8,128)(2,1)S(1)} %get-tuple-element.51.k1, bf16[1024,2048]{1,0:T(8,128)(2,1)S(1)} %get-tuple-element.54.k2, bf16[1024,2048]{1,0:T(8,128)(2,1)S(1)} %get-tuple-element.55.k3, bf16[32,4096]{1,0:T(8,128)(2,1)S(1)} %get-tuple-element.76.vec), custom_call_target="tpu_custom_call" | custom-call | flops 2147483648 | tf_op jit(solution)/shard_map/own3/pallas_call | solution.py:45
  119.5 1.5 %collective-permute-start.18 = (f32[16,1152]{1,0:T(8,128)S(1)}, f32[16,1152]{1,0:T(8,128)S(1)}, u32[]{:S(2)}, u32[]{:S(2)}) collective-permute-start(f32[16,1152]{1,0:T(8,128)S(1)} %core_add.1.q0), channel_id=1, source_target_pairs={{96,0},{97,1},{98,2},{99,3},{100,4},{101,5},{102,6},{103,7},{104,8... | collective-permute-start | bytes 221192 | tf_op jit(solution)/shard_map/ppermute | solution.py:348
  122.2 2.8 %collective-permute-done.19.q3 = f32[16,1152]{1,0:T(8,128)S(1)} collective-permute-done((f32[16,1152]{1,0:T(8,128)S(1)}, f32[16,1152]{1,0:T(8,128)S(1)}, u32[]{:S(2)}, u32[]{:S(2)}) %collective-permute-start.19) | collective-permute-done | bytes 73760 | tf_op jit(solution)/shard_map/ppermute | solution.py:348
  125.0 1.4 %collective-permute-done.18.q2 = f32[16,1152]{1,0:T(8,128)S(1)} collective-permute-done((f32[16,1152]{1,0:T(8,128)S(1)}, f32[16,1152]{1,0:T(8,128)S(1)}, u32[]{:S(2)}, u32[]{:S(2)}) %collective-permute-start.18) | collective-permute-done | bytes 73760 | tf_op jit(solution)/shard_map/ppermute | solution.py:348
  126.4 1.6 %last.1 = (f32[16,1024]{1,0:T(8,128)S(1)}, f32[32,8,128]{2,1,0:T(8,128)S(1)}) custom-call(f32[1,1024]{1,0:T(1,128)S(1)} %get-tuple-element.66.weight_own, f32[16,1152]{1,0:T(8,128)S(1)} %core_add.1.q0, f32[16,1152]{1,0:T(8,128)S(1)} %collective-permute-done.17.q1, f32[16,1152]{1,0:T(8,128)S(1)} %collective-permute-done.18.q2, ...), custom_call_target="tpu_custom_call" | custom-call | tf_op jit(solution)/shard_map/last/pallas_call | solution.py:45
  128.0 11.8 %all_to_all.29.grams = f32[32,8,128]{2,1,0:T(8,128)S(1)} all-to-all(f32[32,8,128]{2,1,0:T(8,128)S(1)} %get-tuple-element.80), channel_id=1, replica_groups=mesh['x'=4,'z'=4,'y'=4,'c'=2] {'z','y','c'}, dimensions={0} | all-to-all | bytes 262144 | tf_op jit(solution)/shard_map/all_to_all | solution.py:470
  139.9 2.2 %finish.1 = f32[16,1024]{1,0:T(8,128)} custom-call(f32[16,1024]{1,0:T(8,128)S(1)} %get-tuple-element.79.proj, f32[32,8,128]{2,1,0:T(8,128)S(1)} %all_to_all.29.grams), custom_call_target="tpu_custom_call" | custom-call | tf_op jit(solution)/shard_map/finish/pallas_call | solution.py:45
  (37 shorter events, 16.8 us)
Async XLA Ops:
  0.6 16.2 %collective-permute-start.3 = (bf16[1024,128]{1,0:T(8,128)(2,1)}, bf16[1024,128]{1,0:T(8,128)(2,1)S(1)}, u32[]{:S(2)}, u32[]{:S(2)}) collective-permute-start(bf16[1024,128]{1,0:T(8,128)(2,1)} %frames.1), channel_id=1, source_target_pairs={{1,0},{0,1},{3,2},{2,3},{5,4},{4,5},{7,6},{6,7},{9,8},{8,9},{11,10... | collective-permute-start | bytes 786440 | tf_op jit(solution)/shard_map/ppermute | solution.py:348
  4.0 5.7 %collective-permute-start.2 = (bf16[336,128]{1,0:T(8,128)(2,1)S(1)}, bf16[336,128]{1,0:T(8,128)(2,1)S(1)}, u32[]{:S(2)}, u32[]{:S(2)}) collective-permute-start(bf16[336,128]{1,0:T(8,128)(2,1)S(1)} %get-tuple-element.42.a), channel_id=1, source_target_pairs={{4,0},{17,1},{6,2},{19,3},{0,4},{21,5},{2,6},{23,7},{12,8},{25,9},... | collective-permute-start | bytes 258056 | tf_op jit(solution)/shard_map/ppermute | solution.py:348
  7.8 4.8 %collective-permute-start.1 = (bf16[336,128]{1,0:T(8,128)(2,1)S(1)}, bf16[336,128]{1,0:T(8,128)(2,1)S(1)}, u32[]{:S(2)}, u32[]{:S(2)}) collective-permute-start(bf16[336,128]{1,0:T(8,128)(2,1)S(1)} %get-tuple-element.42.a), channel_id=1, source_target_pairs={{6,0},{25,1},{4,2},{27,3},{2,4},{29,5},{0,6},{31,7},{14,8},{17,9},... | collective-permute-start | bytes 258056 | tf_op jit(solution)/shard_map/ppermute | solution.py:348
  8.2 4.4 %collective-permute-start = (bf16[336,128]{1,0:T(8,128)(2,1)S(1)}, bf16[336,128]{1,0:T(8,128)(2,1)S(1)}, u32[]{:S(2)}, u32[]{:S(2)}) collective-permute-start(bf16[336,128]{1,0:T(8,128)(2,1)S(1)} %get-tuple-element.42.a), channel_id=1, source_target_pairs={{2,0},{9,1},{0,2},{11,3},{6,4},{13,5},{4,6},{15,7},{10,8},{1,9},{8... | collective-permute-start | bytes 258056 | tf_op jit(solution)/shard_map/ppermute | solution.py:348
  12.6 6.8 %collective-permute-start.5 = (bf16[4,336,128]{2,1,0:T(8,128)(2,1)S(1)}, bf16[4,336,128]{2,1,0:T(8,128)(2,1)S(1)}, u32[]{:S(2)}, u32[]{:S(2)}) collective-permute-start(bf16[4,336,128]{2,1,0:T(8,128)(2,1)S(1)} %stack.9.pieces.g0), channel_id=1, source_target_pairs={{8,0},{3,1},{10,2},{1,3},{12,4},{7,5},{14,6},{5,7},{0,8},{11,9},{2... | collective-permute-start | bytes 1032200 | tf_op jit(solution)/shard_map/ppermute | solution.py:348
  13.7 3.2 %collective-permute-start.4 = (s32[8,128]{1,0:T(8,128)}, s32[8,128]{1,0:T(8,128)S(1)}, u32[]{:S(2)}, u32[]{:S(2)}) collective-permute-start(s32[8,128]{1,0:T(8,128)} %bitcast.5), channel_id=1, source_target_pairs={{1,0},{0,1},{3,2},{2,3},{5,4},{4,5},{7,6},{6,7},{9,8},{8,9},{11,10... | collective-permute-start | bytes 12296 | tf_op jit(solution)/shard_map/ppermute | solution.py:348
  15.1 11.3 %collective-permute-start.7 = (bf16[4,336,128]{2,1,0:T(8,128)(2,1)S(1)}, bf16[4,336,128]{2,1,0:T(8,128)(2,1)S(1)}, u32[]{:S(2)}, u32[]{:S(2)}) collective-permute-start(bf16[4,336,128]{2,1,0:T(8,128)(2,1)S(1)} %stack.9.pieces.g0), channel_id=1, source_target_pairs={{24,0},{7,1},{26,2},{5,3},{28,4},{3,5},{30,6},{1,7},{16,8},{15,9},... | collective-permute-start | bytes 1032200 | tf_op jit(solution)/shard_map/ppermute | solution.py:348
  16.9 11.9 %collective-permute-start.6 = (bf16[4,336,128]{2,1,0:T(8,128)(2,1)S(1)}, bf16[4,336,128]{2,1,0:T(8,128)(2,1)S(1)}, u32[]{:S(2)}, u32[]{:S(2)}) collective-permute-start(bf16[4,336,128]{2,1,0:T(8,128)(2,1)S(1)} %stack.9.pieces.g0), channel_id=1, source_target_pairs={{16,0},{5,1},{18,2},{7,3},{20,4},{1,5},{22,6},{3,7},{24,8},{13,9},... | collective-permute-start | bytes 1032200 | tf_op jit(solution)/shard_map/ppermute | solution.py:348
  68.0 1.9 %collective-permute-start.8 = (f32[16,1024]{1,0:T(8,128)S(1)}, f32[16,1024]{1,0:T(8,128)S(1)}, u32[]{:S(2)}, u32[]{:S(2)}) collective-permute-start(f32[16,1024]{1,0:T(8,128)S(1)} %get-tuple-element.61), channel_id=1, source_target_pairs={{1,0},{0,1},{3,2},{2,3},{5,4},{4,5},{7,6},{6,7},{9,8},{8,9},{11,10... | collective-permute-start | bytes 196616 | tf_op jit(solution)/shard_map/ppermute | solution.py:348
  70.6 4.3 %collective-permute-start.9 = (f32[24,256]{1,0:T(8,128)S(1)}, f32[24,256]{1,0:T(8,128)S(1)}, u32[]{:S(2)}, u32[]{:S(2)}) collective-permute-start(f32[24,256]{1,0:T(8,128)S(1)} %get-tuple-element.63), channel_id=1, source_target_pairs={{64,0},{65,1},{66,2},{67,3},{68,4},{69,5},{70,6},{71,7},{72,8},{73... | collective-permute-start | bytes 73736 | tf_op jit(solution)/shard_map/ppermute | solution.py:348
  71.4 3.4 %collective-permute-start.10 = (f32[24,256]{1,0:T(8,128)S(1)}, f32[24,256]{1,0:T(8,128)S(1)}, u32[]{:S(2)}, u32[]{:S(2)}) collective-permute-start(f32[24,256]{1,0:T(8,128)S(1)} %get-tuple-element.64), channel_id=1, source_target_pairs={{32,0},{33,1},{34,2},{35,3},{36,4},{37,5},{38,6},{39,7},{40,8},{41... | collective-permute-start | bytes 73736 | tf_op jit(solution)/shard_map/ppermute | solution.py:348
  72.1 3.9 %collective-permute-start.11 = (f32[24,256]{1,0:T(8,128)S(1)}, f32[24,256]{1,0:T(8,128)S(1)}, u32[]{:S(2)}, u32[]{:S(2)}) collective-permute-start(f32[24,256]{1,0:T(8,128)S(1)} %get-tuple-element.65), channel_id=1, source_target_pairs={{96,0},{97,1},{98,2},{99,3},{100,4},{101,5},{102,6},{103,7},{104,8... | collective-permute-start | bytes 73736 | tf_op jit(solution)/shard_map/ppermute | solution.py:348
  89.6 4.6 %collective-permute-start.12 = (f32[16,1152]{1,0:T(8,128)S(1)}, f32[16,1152]{1,0:T(8,128)S(1)}, u32[]{:S(2)}, u32[]{:S(2)}) collective-permute-start(f32[16,1152]{1,0:T(8,128)S(1)} %get-tuple-element.70), channel_id=1, source_target_pairs={{1,0},{0,1},{3,2},{2,3},{5,4},{4,5},{7,6},{6,7},{9,8},{8,9},{11,10... | collective-permute-start | bytes 221192 | tf_op jit(solution)/shard_map/ppermute | solution.py:348
  94.9 4.3 %collective-permute-start.13 = (f32[16,384]{1,0:T(8,128)S(1)}, f32[16,384]{1,0:T(8,128)S(1)}, u32[]{:S(2)}, u32[]{:S(2)}) collective-permute-start(f32[16,384]{1,0:T(8,128)S(1)} %get-tuple-element.73), channel_id=1, source_target_pairs={{64,0},{65,1},{66,2},{67,3},{68,4},{69,5},{70,6},{71,7},{72,8},{73... | collective-permute-start | bytes 73736 | tf_op jit(solution)/shard_map/ppermute | solution.py:348
  95.9 3.2 %collective-permute-start.14 = (f32[16,384]{1,0:T(8,128)S(1)}, f32[16,384]{1,0:T(8,128)S(1)}, u32[]{:S(2)}, u32[]{:S(2)}) collective-permute-start(f32[16,384]{1,0:T(8,128)S(1)} %get-tuple-element.74), channel_id=1, source_target_pairs={{32,0},{33,1},{34,2},{35,3},{36,4},{37,5},{38,6},{39,7},{40,8},{41... | collective-permute-start | bytes 73736 | tf_op jit(solution)/shard_map/ppermute | solution.py:348
  97.1 3.9 %collective-permute-start.15 = (f32[16,384]{1,0:T(8,128)S(1)}, f32[16,384]{1,0:T(8,128)S(1)}, u32[]{:S(2)}, u32[]{:S(2)}) collective-permute-start(f32[16,384]{1,0:T(8,128)S(1)} %get-tuple-element.75), channel_id=1, source_target_pairs={{96,0},{97,1},{98,2},{99,3},{100,4},{101,5},{102,6},{103,7},{104,8... | collective-permute-start | bytes 73736 | tf_op jit(solution)/shard_map/ppermute | solution.py:348
  114.8 4.6 %collective-permute-start.16 = (f32[16,1152]{1,0:T(8,128)S(1)}, f32[16,1152]{1,0:T(8,128)S(1)}, u32[]{:S(2)}, u32[]{:S(2)}) collective-permute-start(f32[16,1152]{1,0:T(8,128)S(1)} %get-tuple-element.77), channel_id=1, source_target_pairs={{1,0},{0,1},{3,2},{2,3},{5,4},{4,5},{7,6},{6,7},{9,8},{8,9},{11,10... | collective-permute-start | bytes 221192 | tf_op jit(solution)/shard_map/ppermute | solution.py:348
  119.4 5.5 %collective-permute-start.19 = (f32[16,1152]{1,0:T(8,128)S(1)}, f32[16,1152]{1,0:T(8,128)S(1)}, u32[]{:S(2)}, u32[]{:S(2)}) collective-permute-start(f32[16,1152]{1,0:T(8,128)S(1)} %core_add.1.q0), channel_id=1, source_target_pairs={{64,0},{65,1},{66,2},{67,3},{68,4},{69,5},{70,6},{71,7},{72,8},{73... | collective-permute-start | bytes 221192 | tf_op jit(solution)/shard_map/ppermute | solution.py:348
  119.5 6.9 %collective-permute-start.18 = (f32[16,1152]{1,0:T(8,128)S(1)}, f32[16,1152]{1,0:T(8,128)S(1)}, u32[]{:S(2)}, u32[]{:S(2)}) collective-permute-start(f32[16,1152]{1,0:T(8,128)S(1)} %core_add.1.q0), channel_id=1, source_target_pairs={{96,0},{97,1},{98,2},{99,3},{100,4},{101,5},{102,6},{103,7},{104,8... | collective-permute-start | bytes 221192 | tf_op jit(solution)/shard_map/ppermute | solution.py:348
  121.0 5.4 %collective-permute-start.17 = (f32[16,1152]{1,0:T(8,128)S(1)}, f32[16,1152]{1,0:T(8,128)S(1)}, u32[]{:S(2)}, u32[]{:S(2)}) collective-permute-start(f32[16,1152]{1,0:T(8,128)S(1)} %core_add.1.q0), channel_id=1, source_target_pairs={{32,0},{33,1},{34,2},{35,3},{36,4},{37,5},{38,6},{39,7},{40,8},{41... | collective-permute-start | bytes 221192 | tf_op jit(solution)/shard_map/ppermute | solution.py:348

commit v5 on v4

--- a/solution.py
+++ b/solution.py
@@ -18,8 +18,6 @@
 NI = 16 * QB
 KV = 16
 NTOT = 32768
-GROUPS = (0, 1, 3, 2)
-LAST_GROUP = GROUPS[-1]
 CLS = QB + 4 * KV
 PROWS = CLS + 16
 base_width = 2.8
@@ -66,20 +64,21 @@
     return pltpu.with_memory_space_constraint(a, VM)
 
 
-def pack_kernel(pos, frames, classes, start, piece, cls_out, mine, quarter, own_classes, sems):
+def pack_kernel(pos, frames, classes, start, piece, mine, quarter, own_classes, sems):
     x = pos[0]
     at = pl.multiple_of(pos[0] * QB, QB)
     copies = (
         pltpu.make_async_copy(frames.at[pl.ds(at, QB), :], piece.at[0:QB, :], sems.at[0]),
         pltpu.make_async_copy(start.at[:, pl.ds(at, QB)], quarter, sems.at[1]),
         pltpu.make_async_copy(classes, own_classes, sems.at[2]),
-        pltpu.make_async_copy(frames, mine, sems.at[3]),
+        pltpu.make_async_copy(frames, mine.at[0:CB, :], sems.at[3]),
     )
     for copy in copies:
         copy.start()
     for copy in copies:
         copy.wait()
-    cls_out[...] = own_classes[...]
+    cls = own_classes[...].astype(F32)
+    mine[CB:, :] = jnp.concatenate([cls, jnp.zeros_like(cls)], axis=0).astype(BF16)
     wide = piece[0:QB, :].astype(F32)
     square = wide * wide
     upper = square.astype(BF16)
@@ -123,9 +122,9 @@
     return jnp.exp2(cls * (-math.log2(width_growth))) * (1.0 / base_width)
 
 
-def side_kernel(rows, cls, aug_j, coef_j):
-    aug_j[...] = augment(rows[...])
-    coef = inverse_width(cls[...].astype(F32)) * (2.0 * math.log2(math.e))
+def side_kernel(block, aug_j, coef_j):
+    aug_j[...] = augment(block[0:CB, :])
+    coef = inverse_width(block[CB:, :].astype(F32)) * (2.0 * math.log2(math.e))
     for r in range(8):
         coef_j[:, r * 128 : (r + 1) * 128] = coef[r : r + 1, :]
 
@@ -140,8 +139,9 @@
                 out[8 * n + 2 * quarter + core] = value
 
 
-def rows_kernel(group, pos, pieces, aug_own, coef_own, aug_other, coef_other, *refs):
-    k_ref, out = refs[-2:]
+def rows_kernel(count, first, last, pos, *refs):
+    groups, (aug_own, coef_own, aug_other, coef_other) = refs[:count], refs[count : count + 4]
+    k_refs, out = refs[-1 - count : -1], refs[-1]
     row = lax.broadcasted_iota(jnp.int32, (16, 128), 0)
     lane = lax.broadcasted_iota(jnp.int32, (16, 128), 1)
     picks = []
@@ -153,20 +153,23 @@
         picks.append(jnp.where(pick, 1.0, 0.0).astype(BF16))
     half = 512
     sides = ((0, aug_own, coef_own), (CB, aug_other, coef_other))
-    totals = [jnp.zeros((8, CB), F32) if group == 0 else refs[0][:, lo : lo + CB] for lo, _, _ in sides]
-    for n in range(2):
-        columns = [
-            dot(pieces[m, CLS:PROWS, :], pick, TN) for m in (2 * n, 2 * n + 1) for pick in picks
-        ]
-        columns = jnp.concatenate(columns, axis=0)
-        rows = jnp.concatenate([pieces[2 * n, 0:QB, :], pieces[2 * n + 1, 0:QB, :]], axis=0)
-        aug_i = jnp.concatenate([rows, columns.astype(BF16)], axis=1)
-        coef_i = inverse_width(columns[:, 8:9])
-        for s, (lo, aug, coef) in enumerate(sides):
-            e = jnp.exp2(dot(aug_i, aug[...], NT) * coef_i * coef[...])
-            k_ref[n * half : (n + 1) * half, lo : lo + CB] = e.astype(BF16)
-            totals[s] = totals[s] + jnp.sum(e.reshape(half // 8, 8, CB), axis=0)
-    if group == LAST_GROUP:
+    totals = [
+        jnp.zeros((8, CB), F32) if first else refs[count + 4][:, lo : lo + CB] for lo, _, _ in sides
+    ]
+    for pieces, k_ref in zip(groups, k_refs):
+        for n in range(2):
+            columns = [
+                dot(pieces[m, CLS:PROWS, :], pick, TN) for m in (2 * n, 2 * n + 1) for pick in picks
+            ]
+            columns = jnp.concatenate(columns, axis=0)
+            rows = jnp.concatenate([pieces[2 * n, 0:QB, :], pieces[2 * n + 1, 0:QB, :]], axis=0)
+            aug_i = jnp.concatenate([rows, columns.astype(BF16)], axis=1)
+            coef_i = inverse_width(columns[:, 8:9])
+            for s, (lo, aug, coef) in enumerate(sides):
+                e = jnp.exp2(dot(aug_i, aug[...], NT) * coef_i * coef[...])
+                k_ref[n * half : (n + 1) * half, lo : lo + CB] = e.astype(BF16)
+                totals[s] = totals[s] + jnp.sum(e.reshape(half // 8, 8, CB), axis=0)
+    if last:
         total = jnp.concatenate(totals, axis=1)
         spread(jnp.sum(total, axis=0, keepdims=True), pos[1], out)
     else:
@@ -253,15 +256,9 @@
 
 def core_sum_kernel(pos, own, away, *refs):
     outs = refs[-4:]
-    x = pos[0]
-    total = own[...] + away[:, :CB]
-    for t in range(4):
-        for d in range(4):
-
-            @pl.when((x ^ d) == t)
-            def _(t=t, d=d):
-                outs[d][:KV, :QB] = total[:, t * QB : (t + 1) * QB]
-
+    for d, out in enumerate(outs):
+        at = pl.ds(pl.multiple_of((pos[0] ^ d) * QB, QB), QB)
+        out[:KV, :QB] = own[:, at] + away[:, at]
     if away.shape[1] > CB:
         gram = refs[0][...] + away[:, CB:]
         for ref in outs:
@@ -316,7 +313,8 @@
         grams[n] = gram
 
 
-def finish_kernel(proj, grams, out):
+def finish_kernel(proj, grams, log_in, out, log_degree):
+    log_degree[...] = log_in[...]
     terms = [grams[n] for n in range(32)]
     while len(terms) > 1:
         terms = [a + b for a, b in zip(terms[::2], terms[1::2])]
@@ -372,10 +370,10 @@
     pos = jnp.concatenate([jnp.stack([x, c]), piece_y * 4 + piece_z]).astype(jnp.int32)
 
     classes = width_class.reshape(8, 128)
-    piece, cls, mine = call(
+    piece, mine = call(
         pack_kernel,
         "pack",
-        [sds((PROWS, F), BF16), sds((8, 128), jnp.int32), vmem((CB, F), BF16)],
+        [sds((PROWS, F), BF16), vmem((CB + 16, F), BF16)],
         (pos, *(pltpu.with_memory_space_constraint(a, pltpu.HBM) for a in (frames, classes, start))),
         scratch=[
             pltpu.VMEM((KV, QB), F32),
@@ -386,23 +384,27 @@
     )
     line = [piece] + [from_line(piece, d) for d in (1, 3, 2)]
     shapes = [sds((CB, 2 * F), BF16), sds((1, CB))]
-    own_side = call(side_kernel, "own_side", shapes, (keep(mine), cls), flops=CB * 4000)
+    own_side = call(side_kernel, "own_side", shapes, (keep(mine),), flops=CB * 4000)
     sides = own_side + call(
-        side_kernel, "other_side", shapes, (from_core(frames), from_core(classes)), flops=CB * 4000
+        side_kernel, "other_side", shapes, (from_core(keep(mine)),), flops=CB * 4000
     )
     line = call(
         stack_kernel, "stack", sds((4, PROWS, F), BF16), (*line, own_side[1])
     )
     groups = [line] + [from_line(line, d, True) for d in (1, 2, 3)]
     ks, sums = [None] * 4, ()
-    for g in GROUPS:
-        ks[g], sums = call(
-            functools.partial(rows_kernel, g),
-            f"rows{g}",
-            [vmem((4 * QB, NJ), BF16), sds((128, 1, QB) if g == LAST_GROUP else (8, NJ))],
-            (pos, groups[g], *sides) + (() if g == 0 else (sums,)),
-            flops=4 * QB * NJ * 1024,
+    for step in ((0,), (1,), (2,), (3,)):
+        last = step == (3,)
+        *made, total = call(
+            functools.partial(rows_kernel, len(step), step == (0,), last),
+            f"rows{step[0]}",
+            [vmem((4 * QB, NJ), BF16)] * len(step) + [sds((128, 1, QB) if last else (8, NJ))],
+            (pos, *(groups[g] for g in step), *sides, *sums),
+            flops=len(step) * 4 * QB * NJ * 1024,
         )
+        sums = (total,)
+        for g, k in zip(step, made):
+            ks[g] = k
 
     def tile():
         return [keep(k) for k in ks]
@@ -412,7 +414,7 @@
         degree_kernel,
         "degree",
         [sds((1, NI)), sds((128, 1, QB))],
-        (pos, *tile(), lax.all_to_all(sums, everyone, 0, 0)),
+        (pos, *tile(), lax.all_to_all(sums[0], everyone, 0, 0)),
     )
     vec, weight_i, weight_log, away = call(
         first_kernel,
@@ -468,7 +470,9 @@
         last_kernel, "last", [sds((KV, CB)), sds((32, 8, 128))], (weight_own, *totals)
     )
     grams = lax.all_to_all(grams, ("z", "y", "c"), 0, 0)
-    embedding = call(finish_kernel, "finish", sds((KV, CB)), (proj, grams))
+    embedding, log_degree = call(
+        finish_kernel, "finish", [sds((KV, CB)), sds((1, CB))], (proj, grams, log_degree)
+    )
     return embedding, log_degree.reshape(CB)
 
 

time: 142 us -> 140 us (0.986)
    ppermute x20 -> x19, waiting for transfers between devices: 17.5 us -> 16.6 us  [shift(): return lax.ppermute(v, ('x', 'z', 'y', 'c'), pairs)]
    ppermute x20 -> x19, starting transfers between devices: 26.6 us -> 26 us  [shift(): return lax.ppermute(v, ('x', 'z', 'y', 'c'), pairs)]
  transfers between devices with their start and end apart: 20 -> 19, of which waited for: 9 -> 10; matrix products, arithmetic and copies ran while one was open for 0% -> 0% of each run, Pallas kernels for 9% -> 8%
where the time goes in v5:
time: 140 us
  blocking collectives  65.1 us (46%)
  Pallas kernels  31.1 us (22%)
  starting transfers between devices  26 us (19%)
  waiting for transfers between devices  16.6 us (12%)
    pallas_call x22, Pallas kernels, call(): pl.pallas_call(kernel, out_shape=outs, in_specs=[spec(n, a) for n, a in e...  31.1 us
    ppermute x19, starting transfers between devices, shift(): return lax.ppermute(v, ('x', 'z', 'y', 'c'), pairs)  26 us
    all_to_all x2, blocking collectives, body(): pieces = lax.all_to_all(pieces, ('y', 'z'), 0, 0)  21.1 us
    all_to_all x1, blocking collectives, body(): lax.all_to_all(sums[0], everyone, 0, 0)  17.9 us
    ppermute x19, waiting for transfers between devices, shift(): return lax.ppermute(v, ('x', 'z', 'y', 'c'), pairs)  16.6 us
    all_to_all x1, blocking collectives, body(): lax.all_to_all(table, everyone, 0, 0)  14.3 us
    all_to_all x1, blocking collectives, body(): grams = lax.all_to_all(grams, ('z', 'y', 'c'), 0, 0)  11.8 us
  transfers between devices with their start and end apart: 19, of which 10 were waited for; matrix products, arithmetic and copies ran while one was open for 0% of the time, Pallas kernels for 8%

profile of v5, /device:TPU:1, one launch (start us, length us, event | category | flops | bytes accessed | tf_op | source)
XLA Modules:
  0.0 139.7 jit_solution(1816449525743383970)
XLA Ops:
  0.7 1.8 %pack.1 = (bf16[336,128]{1,0:T(8,128)(2,1)S(1)}, bf16[1040,128]{1,0:T(8,128)(2,1)S(1)}) custom-call(s32[18]{0:T(128)S(1)} %pad_add_fusion.pos, bf16[1024,128]{1,0:T(8,128)(2,1)} %frames.1, s32[8,128]{1,0:T(8,128)} %bitcast.4, f32[16,1024]{1,0:T(8,128)} %start.1), custom_call_target="tpu_custom_call" | custom-call | tf_op jit(solution)/shard_map/pack/pallas_call | solution.py:43
  2.5 1.5 %collective-permute-start.3 = (bf16[1040,128]{1,0:T(8,128)(2,1)S(1)}, bf16[1040,128]{1,0:T(8,128)(2,1)S(1)}, u32[]{:S(2)}, u32[]{:S(2)}) collective-permute-start(bf16[1040,128]{1,0:T(8,128)(2,1)S(1)} %get-tuple-element.44.block), channel_id=1, source_target_pairs={{1,0},{0,1},{3,2},{2,3},{5,4},{4,5},{7,6},{6,7},{9,8},{8,9},{11,10... | collective-permute-start | bytes 798728 | tf_op jit(solution)/shard_map/ppermute | solution.py:346
  4.0 3.7 %collective-permute-start.2 = (bf16[336,128]{1,0:T(8,128)(2,1)S(1)}, bf16[336,128]{1,0:T(8,128)(2,1)S(1)}, u32[]{:S(2)}, u32[]{:S(2)}) collective-permute-start(bf16[336,128]{1,0:T(8,128)(2,1)S(1)} %get-tuple-element.43.a), channel_id=1, source_target_pairs={{4,0},{17,1},{6,2},{19,3},{0,4},{21,5},{2,6},{23,7},{12,8},{25,9},... | collective-permute-start | bytes 258056 | tf_op jit(solution)/shard_map/ppermute | solution.py:346
  9.7 2.8 %collective-permute-done.1.d = bf16[336,128]{1,0:T(8,128)(2,1)S(1)} collective-permute-done((bf16[336,128]{1,0:T(8,128)(2,1)S(1)}, bf16[336,128]{1,0:T(8,128)(2,1)S(1)}, u32[]{:S(2)}, u32[]{:S(2)}) %collective-permute-start.1) | collective-permute-done | bytes 86048 | tf_op jit(solution)/shard_map/ppermute | solution.py:346
  13.7 1.9 %collective-permute-start.6 = (bf16[4,336,128]{2,1,0:T(8,128)(2,1)S(1)}, bf16[4,336,128]{2,1,0:T(8,128)(2,1)S(1)}, u32[]{:S(2)}, u32[]{:S(2)}) collective-permute-start(bf16[4,336,128]{2,1,0:T(8,128)(2,1)S(1)} %stack.9.refs_0_.g0), channel_id=1, source_target_pairs={{24,0},{7,1},{26,2},{5,3},{28,4},{3,5},{30,6},{1,7},{16,8},{15,9},... | collective-permute-start | bytes 1032200 | tf_op jit(solution)/shard_map/ppermute | solution.py:346
  16.6 2.3 %rows0.1 = (bf16[1024,2048]{1,0:T(8,128)(2,1)S(1)}, f32[8,2048]{1,0:T(8,128)S(1)}) custom-call(s32[18]{0:T(128)S(1)} %pad_add_fusion.pos, bf16[4,336,128]{2,1,0:T(8,128)(2,1)S(1)} %stack.9.refs_0_.g0, bf16[1024,256]{1,0:T(8,128)(2,1)S(1)} %get-tuple-element.46.refs_1_, f32[1,1024]{1,0:T(1,128)S(1)} %get-tuple-element.45.ready.refs_2_, ...), custom_call_target="tpu_custom_call" | custom-call | flops 2147483648 | tf_op jit(solution)/shard_map/rows0/pallas_call | solution.py:43
  19.1 2.3 %rows1.1 = (bf16[1024,2048]{1,0:T(8,128)(2,1)S(1)}, f32[8,2048]{1,0:T(8,128)S(1)}) custom-call(s32[18]{0:T(128)S(1)} %pad_add_fusion.pos, bf16[4,336,128]{2,1,0:T(8,128)(2,1)S(1)} %collective-permute-done.4.refs_0_.g1, bf16[1024,256]{1,0:T(8,128)(2,1)S(1)} %get-tuple-element.46.refs_1_, f32[1,1024]{1,0:T(1,128)S(1)} %get-tuple-element.45.ready.refs_2_, ...), custom_call_target="tpu_custom_call" | custom-call | flops 2147483648 | tf_op jit(solution)/shard_map/rows1/pallas_call | solution.py:43
  21.4 3.5 %collective-permute-done.5.refs_0_.g2 = bf16[4,336,128]{2,1,0:T(8,128)(2,1)S(1)} collective-permute-done((bf16[4,336,128]{2,1,0:T(8,128)(2,1)S(1)}, bf16[4,336,128]{2,1,0:T(8,128)(2,1)S(1)}, u32[]{:S(2)}, u32[]{:S(2)}) %collective-permute-start.5) | collective-permute-done | bytes 344096 | tf_op jit(solution)/shard_map/ppermute | solution.py:346
  24.9 2.3 %rows2.1 = (bf16[1024,2048]{1,0:T(8,128)(2,1)S(1)}, f32[8,2048]{1,0:T(8,128)S(1)}) custom-call(s32[18]{0:T(128)S(1)} %pad_add_fusion.pos, bf16[4,336,128]{2,1,0:T(8,128)(2,1)S(1)} %collective-permute-done.5.refs_0_.g2, bf16[1024,256]{1,0:T(8,128)(2,1)S(1)} %get-tuple-element.46.refs_1_, f32[1,1024]{1,0:T(1,128)S(1)} %get-tuple-element.45.ready.refs_2_, ...), custom_call_target="tpu_custom_call" | custom-call | flops 2147483648 | tf_op jit(solution)/shard_map/rows2/pallas_call | solution.py:43
  27.2 2.4 %rows3.1 = (bf16[1024,2048]{1,0:T(8,128)(2,1)S(1)}, f32[128,1,256]{2,1,0:T(1,128)S(1)}) custom-call(s32[18]{0:T(128)S(1)} %pad_add_fusion.pos, bf16[4,336,128]{2,1,0:T(8,128)(2,1)S(1)} %collective-permute-done.6.refs_0_.g3, bf16[1024,256]{1,0:T(8,128)(2,1)S(1)} %get-tuple-element.46.refs_1_, f32[1,1024]{1,0:T(1,128)S(1)} %get-tuple-element.45.ready.refs_2_, ...), custom_call_target="tpu_custom_call" | custom-call | flops 2147483648 | tf_op jit(solution)/shard_map/rows3/pallas_call | solution.py:43
  29.6 17.9 %all_to_all.25.table = f32[128,1,256]{2,1,0:T(1,128)S(1)} all-to-all(f32[128,1,256]{2,1,0:T(1,128)S(1)} %get-tuple-element.56), channel_id=1, replica_groups=mesh['x'=4,'z'=4,'y'=4,'c'=2] {'y','z','x','c'}, dimensions={0} | all-to-all | bytes 262144 | tf_op jit(solution)/shard_map/all_to_all | solution.py:417
  47.5 2.8 %degree.1 = (f32[1,4096]{1,0:T(1,128)S(1)}, f32[128,1,256]{2,1,0:T(1,128)S(1)}) custom-call(s32[18]{0:T(128)S(1)} %pad_add_fusion.pos, bf16[1024,2048]{1,0:T(8,128)(2,1)S(1)} %get-tuple-element.49.k0, bf16[1024,2048]{1,0:T(8,128)(2,1)S(1)} %get-tuple-element.51.k1, bf16[1024,2048]{1,0:T(8,128)(2,1)S(1)} %get-tuple-element.53.k2, ...), custom_call_target="tpu_custom_call" | custom-call | tf_op jit(solution)/shard_map/degree/pallas_call | solution.py:43
  50.4 14.3 %all_to_all.26.table = f32[128,1,256]{2,1,0:T(1,128)S(1)} all-to-all(f32[128,1,256]{2,1,0:T(1,128)S(1)} %get-tuple-element.58), channel_id=1, replica_groups=mesh['x'=4,'z'=4,'y'=4,'c'=2] {'y','z','x','c'}, dimensions={0} | all-to-all | bytes 262144 | tf_op jit(solution)/shard_map/all_to_all | solution.py:423
  64.6 1.8 %first.1 = (bf16[16,4096]{1,0:T(8,128)(2,1)S(1)}, f32[1,4096]{1,0:T(1,128)S(1)}, f32[8,256]{1,0:T(8,128)S(1)}, f32[16,1024]{1,0:T(8,128)S(1)}) custom-call(s32[18]{0:T(128)S(1)} %pad_add_fusion.pos, bf16[1024,2048]{1,0:T(8,128)(2,1)S(1)} %get-tuple-element.49.k0, bf16[1024,2048]{1,0:T(8,128)(2,1)S(1)} %get-tuple-element.51.k1, ...), custom_call_target="tpu_custom_call" | custom-call | tf_op jit(solution)/shard_map/first/pallas_call | solution.py:43
  67.1 1.2 own1.1.own
  70.4 1.8 %collective-permute-start.10 = (f32[24,256]{1,0:T(8,128)S(1)}, f32[24,256]{1,0:T(8,128)S(1)}, u32[]{:S(2)}, u32[]{:S(2)}) collective-permute-start(f32[24,256]{1,0:T(8,128)S(1)} %get-tuple-element.65), channel_id=1, source_target_pairs={{96,0},{97,1},{98,2},{99,3},{100,4},{101,5},{102,6},{103,7},{104,8... | collective-permute-start | bytes 73736 | tf_op jit(solution)/shard_map/ppermute | solution.py:346
  74.8 10.6 %all_to_all.27.pieces = f32[16,16,256]{2,1,0:T(8,128)S(1)} all-to-all(f32[16,16,256]{2,1,0:T(8,128)S(1)} %get-tuple-element.68), channel_id=1, replica_groups=mesh['x'=4,'z'=4,'y'=4,'c'=2] {'y','z'}, dimensions={0} | all-to-all | bytes 524288 | tf_op jit(solution)/shard_map/all_to_all | solution.py:454
  85.4 2.0 %next1.1 = (bf16[32,4096]{1,0:T(8,128)(2,1)S(1)}, f32[16,128]{1,0:T(8,128)S(1)}, f32[16,1152]{1,0:T(8,128)S(1)}) custom-call(s32[18]{0:T(128)S(1)} %pad_add_fusion.pos, bf16[1024,2048]{1,0:T(8,128)(2,1)S(1)} %get-tuple-element.49.k0, bf16[1024,2048]{1,0:T(8,128)(2,1)S(1)} %get-tuple-element.51.k1, bf16[1024,2048]{1,0:T(8,128)(2,1)S(1)} %get-tuple-element.53.k2, ...), custom_call_target="tpu_custom_call" | custom-call | tf_op jit(solution)/shard_map/next1/pallas_call | solution.py:43
  87.4 3.2 %collective-permute-start.11 = (f32[16,1152]{1,0:T(8,128)S(1)}, f32[16,1152]{1,0:T(8,128)S(1)}, u32[]{:S(2)}, u32[]{:S(2)}) collective-permute-start(f32[16,1152]{1,0:T(8,128)S(1)} %get-tuple-element.70), channel_id=1, source_target_pairs={{1,0},{0,1},{3,2},{2,3},{5,4},{4,5},{7,6},{6,7},{9,8},{8,9},{11,10... | collective-permute-start | bytes 221192 | tf_op jit(solution)/shard_map/ppermute | solution.py:346
  90.5 1.4 %own2.1.own = f32[16,1024]{1,0:T(8,128)S(1)} custom-call(bf16[1024,2048]{1,0:T(8,128)(2,1)S(1)} %get-tuple-element.49.k0, bf16[1024,2048]{1,0:T(8,128)(2,1)S(1)} %get-tuple-element.51.k1, bf16[1024,2048]{1,0:T(8,128)(2,1)S(1)} %get-tuple-element.53.k2, bf16[1024,2048]{1,0:T(8,128)(2,1)S(1)} %get-tuple-element.55.k3, bf16[32,4096]{1,0:T(8,128)(2,1)S(1)} %get-tuple-element.69.vec), custom_call_target="tpu_custom_call" | custom-call | flops 2147483648 | tf_op jit(solution)/shard_map/own2/pallas_call | solution.py:43
  96.8 1.8 %collective-permute-done.14.q3 = f32[16,384]{1,0:T(8,128)S(1)} collective-permute-done((f32[16,384]{1,0:T(8,128)S(1)}, f32[16,384]{1,0:T(8,128)S(1)}, u32[]{:S(2)}, u32[]{:S(2)}) %collective-permute-start.14) | collective-permute-done | bytes 24608 | tf_op jit(solution)/shard_map/ppermute | solution.py:346
  98.6 1.4 project2.1
  100.0 10.5 %all_to_all.28.pieces = f32[16,16,256]{2,1,0:T(8,128)S(1)} all-to-all(f32[16,16,256]{2,1,0:T(8,128)S(1)} %project2.1), channel_id=1, replica_groups=mesh['x'=4,'z'=4,'y'=4,'c'=2] {'y','z'}, dimensions={0} | all-to-all | bytes 524288 | tf_op jit(solution)/shard_map/all_to_all | solution.py:454
  110.5 2.0 %next2.1 = (bf16[32,4096]{1,0:T(8,128)(2,1)S(1)}, f32[16,128]{1,0:T(8,128)S(1)}, f32[16,1152]{1,0:T(8,128)S(1)}) custom-call(s32[18]{0:T(128)S(1)} %pad_add_fusion.pos, bf16[1024,2048]{1,0:T(8,128)(2,1)S(1)} %get-tuple-element.49.k0, bf16[1024,2048]{1,0:T(8,128)(2,1)S(1)} %get-tuple-element.51.k1, bf16[1024,2048]{1,0:T(8,128)(2,1)S(1)} %get-tuple-element.53.k2, ...), custom_call_target="tpu_custom_call" | custom-call | tf_op jit(solution)/shard_map/next2/pallas_call | solution.py:43
  112.5 3.1 %collective-permute-start.15 = (f32[16,1152]{1,0:T(8,128)S(1)}, f32[16,1152]{1,0:T(8,128)S(1)}, u32[]{:S(2)}, u32[]{:S(2)}) collective-permute-start(f32[16,1152]{1,0:T(8,128)S(1)} %get-tuple-element.77), channel_id=1, source_target_pairs={{1,0},{0,1},{3,2},{2,3},{5,4},{4,5},{7,6},{6,7},{9,8},{8,9},{11,10... | collective-permute-start | bytes 221192 | tf_op jit(solution)/shard_map/ppermute | solution.py:346
  115.6 1.4 %own3.1.own = f32[16,1024]{1,0:T(8,128)S(1)} custom-call(bf16[1024,2048]{1,0:T(8,128)(2,1)S(1)} %get-tuple-element.49.k0, bf16[1024,2048]{1,0:T(8,128)(2,1)S(1)} %get-tuple-element.51.k1, bf16[1024,2048]{1,0:T(8,128)(2,1)S(1)} %get-tuple-element.53.k2, bf16[1024,2048]{1,0:T(8,128)(2,1)S(1)} %get-tuple-element.55.k3, bf16[32,4096]{1,0:T(8,128)(2,1)S(1)} %get-tuple-element.76.vec), custom_call_target="tpu_custom_call" | custom-call | flops 2147483648 | tf_op jit(solution)/shard_map/own3/pallas_call | solution.py:43
  117.2 1.5 %collective-permute-start.17 = (f32[16,1152]{1,0:T(8,128)S(1)}, f32[16,1152]{1,0:T(8,128)S(1)}, u32[]{:S(2)}, u32[]{:S(2)}) collective-permute-start(f32[16,1152]{1,0:T(8,128)S(1)} %core_add.1.q0), channel_id=1, source_target_pairs={{96,0},{97,1},{98,2},{99,3},{100,4},{101,5},{102,6},{103,7},{104,8... | collective-permute-start | bytes 221192 | tf_op jit(solution)/shard_map/ppermute | solution.py:346
  119.8 2.8 %collective-permute-done.18.q3 = f32[16,1152]{1,0:T(8,128)S(1)} collective-permute-done((f32[16,1152]{1,0:T(8,128)S(1)}, f32[16,1152]{1,0:T(8,128)S(1)}, u32[]{:S(2)}, u32[]{:S(2)}) %collective-permute-start.18) | collective-permute-done | bytes 73760 | tf_op jit(solution)/shard_map/ppermute | solution.py:346
  122.6 1.4 %collective-permute-done.17.q2 = f32[16,1152]{1,0:T(8,128)S(1)} collective-permute-done((f32[16,1152]{1,0:T(8,128)S(1)}, f32[16,1152]{1,0:T(8,128)S(1)}, u32[]{:S(2)}, u32[]{:S(2)}) %collective-permute-start.17) | collective-permute-done | bytes 73760 | tf_op jit(solution)/shard_map/ppermute | solution.py:346
  124.0 1.6 %last.1 = (f32[16,1024]{1,0:T(8,128)S(1)}, f32[32,8,128]{2,1,0:T(8,128)S(1)}) custom-call(f32[1,1024]{1,0:T(1,128)S(1)} %get-tuple-element.66.weight_own, f32[16,1152]{1,0:T(8,128)S(1)} %core_add.1.q0, f32[16,1152]{1,0:T(8,128)S(1)} %collective-permute-done.16.q1, f32[16,1152]{1,0:T(8,128)S(1)} %collective-permute-done.17.q2, ...), custom_call_target="tpu_custom_call" | custom-call | tf_op jit(solution)/shard_map/last/pallas_call | solution.py:43
  125.7 11.8 %all_to_all.29.grams = f32[32,8,128]{2,1,0:T(8,128)S(1)} all-to-all(f32[32,8,128]{2,1,0:T(8,128)S(1)} %get-tuple-element.80), channel_id=1, replica_groups=mesh['x'=4,'z'=4,'y'=4,'c'=2] {'z','y','c'}, dimensions={0} | all-to-all | bytes 262144 | tf_op jit(solution)/shard_map/all_to_all | solution.py:472
  137.5 2.2 %finish.1 = (f32[16,1024]{1,0:T(8,128)}, f32[1,1024]{1,0:T(1,128)}) custom-call(f32[16,1024]{1,0:T(8,128)S(1)} %get-tuple-element.79.proj, f32[32,8,128]{2,1,0:T(8,128)S(1)} %all_to_all.29.grams, f32[1,1024]{1,0:T(1,128)S(1)} %get-tuple-element.81.log_in), custom_call_target="tpu_custom_call" | custom-call | tf_op jit(solution)/shard_map/finish/pallas_call | solution.py:43
  (35 shorter events, 15.9 us)
Async XLA Ops:
  2.5 13.8 %collective-permute-start.3 = (bf16[1040,128]{1,0:T(8,128)(2,1)S(1)}, bf16[1040,128]{1,0:T(8,128)(2,1)S(1)}, u32[]{:S(2)}, u32[]{:S(2)}) collective-permute-start(bf16[1040,128]{1,0:T(8,128)(2,1)S(1)} %get-tuple-element.44.block), channel_id=1, source_target_pairs={{1,0},{0,1},{3,2},{2,3},{5,4},{4,5},{7,6},{6,7},{9,8},{8,9},{11,10... | collective-permute-start | bytes 798728 | tf_op jit(solution)/shard_map/ppermute | solution.py:346
  4.0 5.7 %collective-permute-start.2 = (bf16[336,128]{1,0:T(8,128)(2,1)S(1)}, bf16[336,128]{1,0:T(8,128)(2,1)S(1)}, u32[]{:S(2)}, u32[]{:S(2)}) collective-permute-start(bf16[336,128]{1,0:T(8,128)(2,1)S(1)} %get-tuple-element.43.a), channel_id=1, source_target_pairs={{4,0},{17,1},{6,2},{19,3},{0,4},{21,5},{2,6},{23,7},{12,8},{25,9},... | collective-permute-start | bytes 258056 | tf_op jit(solution)/shard_map/ppermute | solution.py:346
  7.7 4.8 %collective-permute-start.1 = (bf16[336,128]{1,0:T(8,128)(2,1)S(1)}, bf16[336,128]{1,0:T(8,128)(2,1)S(1)}, u32[]{:S(2)}, u32[]{:S(2)}) collective-permute-start(bf16[336,128]{1,0:T(8,128)(2,1)S(1)} %get-tuple-element.43.a), channel_id=1, source_target_pairs={{6,0},{25,1},{4,2},{27,3},{2,4},{29,5},{0,6},{31,7},{14,8},{17,9},... | collective-permute-start | bytes 258056 | tf_op jit(solution)/shard_map/ppermute | solution.py:346
  8.1 4.4 %collective-permute-start = (bf16[336,128]{1,0:T(8,128)(2,1)S(1)}, bf16[336,128]{1,0:T(8,128)(2,1)S(1)}, u32[]{:S(2)}, u32[]{:S(2)}) collective-permute-start(bf16[336,128]{1,0:T(8,128)(2,1)S(1)} %get-tuple-element.43.a), channel_id=1, source_target_pairs={{2,0},{9,1},{0,2},{11,3},{6,4},{13,5},{4,6},{15,7},{10,8},{1,9},{8... | collective-permute-start | bytes 258056 | tf_op jit(solution)/shard_map/ppermute | solution.py:346
  12.6 6.5 %collective-permute-start.4 = (bf16[4,336,128]{2,1,0:T(8,128)(2,1)S(1)}, bf16[4,336,128]{2,1,0:T(8,128)(2,1)S(1)}, u32[]{:S(2)}, u32[]{:S(2)}) collective-permute-start(bf16[4,336,128]{2,1,0:T(8,128)(2,1)S(1)} %stack.9.refs_0_.g0), channel_id=1, source_target_pairs={{8,0},{3,1},{10,2},{1,3},{12,4},{7,5},{14,6},{5,7},{0,8},{11,9},{2... | collective-permute-start | bytes 1032200 | tf_op jit(solution)/shard_map/ppermute | solution.py:346
  13.7 13.5 %collective-permute-start.6 = (bf16[4,336,128]{2,1,0:T(8,128)(2,1)S(1)}, bf16[4,336,128]{2,1,0:T(8,128)(2,1)S(1)}, u32[]{:S(2)}, u32[]{:S(2)}) collective-permute-start(bf16[4,336,128]{2,1,0:T(8,128)(2,1)S(1)} %stack.9.refs_0_.g0), channel_id=1, source_target_pairs={{24,0},{7,1},{26,2},{5,3},{28,4},{3,5},{30,6},{1,7},{16,8},{15,9},... | collective-permute-start | bytes 1032200 | tf_op jit(solution)/shard_map/ppermute | solution.py:346
  15.6 9.3 %collective-permute-start.5 = (bf16[4,336,128]{2,1,0:T(8,128)(2,1)S(1)}, bf16[4,336,128]{2,1,0:T(8,128)(2,1)S(1)}, u32[]{:S(2)}, u32[]{:S(2)}) collective-permute-start(bf16[4,336,128]{2,1,0:T(8,128)(2,1)S(1)} %stack.9.refs_0_.g0), channel_id=1, source_target_pairs={{16,0},{5,1},{18,2},{7,3},{20,4},{1,5},{22,6},{3,7},{24,8},{13,9},... | collective-permute-start | bytes 1032200 | tf_op jit(solution)/shard_map/ppermute | solution.py:346
  66.4 1.9 %collective-permute-start.7 = (f32[16,1024]{1,0:T(8,128)S(1)}, f32[16,1024]{1,0:T(8,128)S(1)}, u32[]{:S(2)}, u32[]{:S(2)}) collective-permute-start(f32[16,1024]{1,0:T(8,128)S(1)} %get-tuple-element.61), channel_id=1, source_target_pairs={{1,0},{0,1},{3,2},{2,3},{5,4},{4,5},{7,6},{6,7},{9,8},{8,9},{11,10... | collective-permute-start | bytes 196616 | tf_op jit(solution)/shard_map/ppermute | solution.py:346
  68.9 4.3 %collective-permute-start.8 = (f32[24,256]{1,0:T(8,128)S(1)}, f32[24,256]{1,0:T(8,128)S(1)}, u32[]{:S(2)}, u32[]{:S(2)}) collective-permute-start(f32[24,256]{1,0:T(8,128)S(1)} %get-tuple-element.63), channel_id=1, source_target_pairs={{64,0},{65,1},{66,2},{67,3},{68,4},{69,5},{70,6},{71,7},{72,8},{73... | collective-permute-start | bytes 73736 | tf_op jit(solution)/shard_map/ppermute | solution.py:346
  69.7 3.4 %collective-permute-start.9 = (f32[24,256]{1,0:T(8,128)S(1)}, f32[24,256]{1,0:T(8,128)S(1)}, u32[]{:S(2)}, u32[]{:S(2)}) collective-permute-start(f32[24,256]{1,0:T(8,128)S(1)} %get-tuple-element.64), channel_id=1, source_target_pairs={{32,0},{33,1},{34,2},{35,3},{36,4},{37,5},{38,6},{39,7},{40,8},{41... | collective-permute-start | bytes 73736 | tf_op jit(solution)/shard_map/ppermute | solution.py:346
  70.4 3.9 %collective-permute-start.10 = (f32[24,256]{1,0:T(8,128)S(1)}, f32[24,256]{1,0:T(8,128)S(1)}, u32[]{:S(2)}, u32[]{:S(2)}) collective-permute-start(f32[24,256]{1,0:T(8,128)S(1)} %get-tuple-element.65), channel_id=1, source_target_pairs={{96,0},{97,1},{98,2},{99,3},{100,4},{101,5},{102,6},{103,7},{104,8... | collective-permute-start | bytes 73736 | tf_op jit(solution)/shard_map/ppermute | solution.py:346
  87.4 4.6 %collective-permute-start.11 = (f32[16,1152]{1,0:T(8,128)S(1)}, f32[16,1152]{1,0:T(8,128)S(1)}, u32[]{:S(2)}, u32[]{:S(2)}) collective-permute-start(f32[16,1152]{1,0:T(8,128)S(1)} %get-tuple-element.70), channel_id=1, source_target_pairs={{1,0},{0,1},{3,2},{2,3},{5,4},{4,5},{7,6},{6,7},{9,8},{8,9},{11,10... | collective-permute-start | bytes 221192 | tf_op jit(solution)/shard_map/ppermute | solution.py:346
  92.5 4.3 %collective-permute-start.12 = (f32[16,384]{1,0:T(8,128)S(1)}, f32[16,384]{1,0:T(8,128)S(1)}, u32[]{:S(2)}, u32[]{:S(2)}) collective-permute-start(f32[16,384]{1,0:T(8,128)S(1)} %get-tuple-element.73), channel_id=1, source_target_pairs={{64,0},{65,1},{66,2},{67,3},{68,4},{69,5},{70,6},{71,7},{72,8},{73... | collective-permute-start | bytes 73736 | tf_op jit(solution)/shard_map/ppermute | solution.py:346
  93.5 3.2 %collective-permute-start.13 = (f32[16,384]{1,0:T(8,128)S(1)}, f32[16,384]{1,0:T(8,128)S(1)}, u32[]{:S(2)}, u32[]{:S(2)}) collective-permute-start(f32[16,384]{1,0:T(8,128)S(1)} %get-tuple-element.74), channel_id=1, source_target_pairs={{32,0},{33,1},{34,2},{35,3},{36,4},{37,5},{38,6},{39,7},{40,8},{41... | collective-permute-start | bytes 73736 | tf_op jit(solution)/shard_map/ppermute | solution.py:346
  94.7 3.9 %collective-permute-start.14 = (f32[16,384]{1,0:T(8,128)S(1)}, f32[16,384]{1,0:T(8,128)S(1)}, u32[]{:S(2)}, u32[]{:S(2)}) collective-permute-start(f32[16,384]{1,0:T(8,128)S(1)} %get-tuple-element.75), channel_id=1, source_target_pairs={{96,0},{97,1},{98,2},{99,3},{100,4},{101,5},{102,6},{103,7},{104,8... | collective-permute-start | bytes 73736 | tf_op jit(solution)/shard_map/ppermute | solution.py:346
  112.5 4.6 %collective-permute-start.15 = (f32[16,1152]{1,0:T(8,128)S(1)}, f32[16,1152]{1,0:T(8,128)S(1)}, u32[]{:S(2)}, u32[]{:S(2)}) collective-permute-start(f32[16,1152]{1,0:T(8,128)S(1)} %get-tuple-element.77), channel_id=1, source_target_pairs={{1,0},{0,1},{3,2},{2,3},{5,4},{4,5},{7,6},{6,7},{9,8},{8,9},{11,10... | collective-permute-start | bytes 221192 | tf_op jit(solution)/shard_map/ppermute | solution.py:346
  117.1 5.5 %collective-permute-start.18 = (f32[16,1152]{1,0:T(8,128)S(1)}, f32[16,1152]{1,0:T(8,128)S(1)}, u32[]{:S(2)}, u32[]{:S(2)}) collective-permute-start(f32[16,1152]{1,0:T(8,128)S(1)} %core_add.1.q0), channel_id=1, source_target_pairs={{64,0},{65,1},{66,2},{67,3},{68,4},{69,5},{70,6},{71,7},{72,8},{73... | collective-permute-start | bytes 221192 | tf_op jit(solution)/shard_map/ppermute | solution.py:346
  117.2 6.9 %collective-permute-start.17 = (f32[16,1152]{1,0:T(8,128)S(1)}, f32[16,1152]{1,0:T(8,128)S(1)}, u32[]{:S(2)}, u32[]{:S(2)}) collective-permute-start(f32[16,1152]{1,0:T(8,128)S(1)} %core_add.1.q0), channel_id=1, source_target_pairs={{96,0},{97,1},{98,2},{99,3},{100,4},{101,5},{102,6},{103,7},{104,8... | collective-permute-start | bytes 221192 | tf_op jit(solution)/shard_map/ppermute | solution.py:346
  118.7 5.4 %collective-permute-start.16 = (f32[16,1152]{1,0:T(8,128)S(1)}, f32[16,1152]{1,0:T(8,128)S(1)}, u32[]{:S(2)}, u32[]{:S(2)}) collective-permute-start(f32[16,1152]{1,0:T(8,128)S(1)} %core_add.1.q0), channel_id=1, source_target_pairs={{32,0},{33,1},{34,2},{35,3},{36,4},{37,5},{38,6},{39,7},{40,8},{41... | collective-permute-start | bytes 221192 | tf_op jit(solution)/shard_map/ppermute | solution.py:346

commit v6 on v5

--- a/solution.py
+++ b/solution.py
@@ -274,14 +274,19 @@
 
 
 def eliminate(gram, y):
-    row = lax.broadcasted_iota(jnp.int32, (KV, 1), 0)
-    pivots = jnp.zeros((KV, 1), F32)
+    row = lax.broadcasted_iota(jnp.int32, (KV, 128), 0)
+    columns = [jnp.broadcast_to(gram[:, j : j + 1], (KV, 128)) for j in range(KV)]
+    tiles = [y[:, lo : lo + 128] for lo in range(0, y.shape[1], 128)]
+    pivots = jnp.zeros((KV, 128), F32)
     for k in range(KV):
-        pivot = gram[k : k + 1, k : k + 1]
-        ratio = jnp.where(row > k, gram[:, k : k + 1] * (1.0 / pivot), 0.0)
+        pivot = columns[k][k : k + 1, :]
+        ratio = jnp.where(row > k, columns[k] * (1.0 / pivot), 0.0)
         pivots = jnp.where(row == k, pivot, pivots)
-        gram, y = gram - ratio * gram[k : k + 1, :], y - ratio * y[k : k + 1, :]
-    return y * (1.0 / jnp.sqrt(pivots))
+        for j in range(k + 1, KV):
+            columns[j] = columns[j] - ratio * columns[j][k : k + 1, :]
+        tiles = [tile - ratio * tile[k : k + 1, :] for tile in tiles]
+    scale = 1.0 / jnp.sqrt(pivots)
+    return jnp.concatenate([tile * scale for tile in tiles], axis=1)
 
 
 def project_first_kernel(pos, weight_log, q0, q1, q2, q3, out, weight_own, log_degree):

time: 140 us -> 137 us (0.979)
  Pallas kernels: 31.1 us -> 27.9 us
    pallas_call x22, Pallas kernels: 31.1 us -> 27.9 us  [call(): pl.pallas_call(kernel, out_shape=outs, in_specs=[spec(n, a) for n, a in e...]
where the time goes in v6:
time: 137 us; the launch traced here: 136 us
  blocking collectives  65.1 us (48%)
  Pallas kernels  27.9 us (20%)
  starting transfers between devices  26 us (19%)
  waiting for transfers between devices  16.6 us (12%)
    pallas_call x22, Pallas kernels, call(): pl.pallas_call(kernel, out_shape=outs, in_specs=[spec(n, a) for n, a in e...  27.9 us
    ppermute x19, starting transfers between devices, shift(): return lax.ppermute(v, ('x', 'z', 'y', 'c'), pairs)  26 us
    all_to_all x2, blocking collectives, body(): pieces = lax.all_to_all(pieces, ('y', 'z'), 0, 0)  21.1 us
    all_to_all x1, blocking collectives, body(): lax.all_to_all(sums[0], everyone, 0, 0)  17.9 us
    ppermute x19, waiting for transfers between devices, shift(): return lax.ppermute(v, ('x', 'z', 'y', 'c'), pairs)  16.6 us
    all_to_all x1, blocking collectives, body(): lax.all_to_all(table, everyone, 0, 0)  14.3 us
    all_to_all x1, blocking collectives, body(): grams = lax.all_to_all(grams, ('z', 'y', 'c'), 0, 0)  11.8 us
  transfers between devices with their start and end apart: 19, of which 10 were waited for; matrix products, arithmetic and copies ran while one was open for 0% of the time, Pallas kernels for 8%

profile of v6, /device:TPU:1, one launch (start us, length us, event | category | flops | bytes accessed | tf_op | source)
XLA Modules:
  0.0 136.5 jit_solution(2565904132377441572)
XLA Ops:
  0.7 1.8 %pack.1 = (bf16[336,128]{1,0:T(8,128)(2,1)S(1)}, bf16[1040,128]{1,0:T(8,128)(2,1)S(1)}) custom-call(s32[18]{0:T(128)S(1)} %pad_add_fusion.pos, bf16[1024,128]{1,0:T(8,128)(2,1)} %frames.1, s32[8,128]{1,0:T(8,128)} %bitcast.4, f32[16,1024]{1,0:T(8,128)} %start.1), custom_call_target="tpu_custom_call" | custom-call | tf_op jit(solution)/shard_map/pack/pallas_call | solution.py:43
  2.5 1.5 %collective-permute-start.3 = (bf16[1040,128]{1,0:T(8,128)(2,1)S(1)}, bf16[1040,128]{1,0:T(8,128)(2,1)S(1)}, u32[]{:S(2)}, u32[]{:S(2)}) collective-permute-start(bf16[1040,128]{1,0:T(8,128)(2,1)S(1)} %get-tuple-element.44.block), channel_id=1, source_target_pairs={{1,0},{0,1},{3,2},{2,3},{5,4},{4,5},{7,6},{6,7},{9,8},{8,9},{11,10... | collective-permute-start | bytes 798728 | tf_op jit(solution)/shard_map/ppermute | solution.py:351
  4.0 3.7 %collective-permute-start.2 = (bf16[336,128]{1,0:T(8,128)(2,1)S(1)}, bf16[336,128]{1,0:T(8,128)(2,1)S(1)}, u32[]{:S(2)}, u32[]{:S(2)}) collective-permute-start(bf16[336,128]{1,0:T(8,128)(2,1)S(1)} %get-tuple-element.43.a), channel_id=1, source_target_pairs={{4,0},{17,1},{6,2},{19,3},{0,4},{21,5},{2,6},{23,7},{12,8},{25,9},... | collective-permute-start | bytes 258056 | tf_op jit(solution)/shard_map/ppermute | solution.py:351
  9.7 2.8 %collective-permute-done.1.d = bf16[336,128]{1,0:T(8,128)(2,1)S(1)} collective-permute-done((bf16[336,128]{1,0:T(8,128)(2,1)S(1)}, bf16[336,128]{1,0:T(8,128)(2,1)S(1)}, u32[]{:S(2)}, u32[]{:S(2)}) %collective-permute-start.1) | collective-permute-done | bytes 86048 | tf_op jit(solution)/shard_map/ppermute | solution.py:351
  13.7 1.9 %collective-permute-start.6 = (bf16[4,336,128]{2,1,0:T(8,128)(2,1)S(1)}, bf16[4,336,128]{2,1,0:T(8,128)(2,1)S(1)}, u32[]{:S(2)}, u32[]{:S(2)}) collective-permute-start(bf16[4,336,128]{2,1,0:T(8,128)(2,1)S(1)} %stack.9.refs_0_.g0), channel_id=1, source_target_pairs={{24,0},{7,1},{26,2},{5,3},{28,4},{3,5},{30,6},{1,7},{16,8},{15,9},... | collective-permute-start | bytes 1032200 | tf_op jit(solution)/shard_map/ppermute | solution.py:351
  16.6 2.3 %rows0.1 = (bf16[1024,2048]{1,0:T(8,128)(2,1)S(1)}, f32[8,2048]{1,0:T(8,128)S(1)}) custom-call(s32[18]{0:T(128)S(1)} %pad_add_fusion.pos, bf16[4,336,128]{2,1,0:T(8,128)(2,1)S(1)} %stack.9.refs_0_.g0, bf16[1024,256]{1,0:T(8,128)(2,1)S(1)} %get-tuple-element.46.refs_1_, f32[1,1024]{1,0:T(1,128)S(1)} %get-tuple-element.45.ready.refs_2_, ...), custom_call_target="tpu_custom_call" | custom-call | flops 2147483648 | tf_op jit(solution)/shard_map/rows0/pallas_call | solution.py:43
  19.1 2.3 %rows1.1 = (bf16[1024,2048]{1,0:T(8,128)(2,1)S(1)}, f32[8,2048]{1,0:T(8,128)S(1)}) custom-call(s32[18]{0:T(128)S(1)} %pad_add_fusion.pos, bf16[4,336,128]{2,1,0:T(8,128)(2,1)S(1)} %collective-permute-done.4.refs_0_.g1, bf16[1024,256]{1,0:T(8,128)(2,1)S(1)} %get-tuple-element.46.refs_1_, f32[1,1024]{1,0:T(1,128)S(1)} %get-tuple-element.45.ready.refs_2_, ...), custom_call_target="tpu_custom_call" | custom-call | flops 2147483648 | tf_op jit(solution)/shard_map/rows1/pallas_call | solution.py:43
  21.4 3.5 %collective-permute-done.5.refs_0_.g2 = bf16[4,336,128]{2,1,0:T(8,128)(2,1)S(1)} collective-permute-done((bf16[4,336,128]{2,1,0:T(8,128)(2,1)S(1)}, bf16[4,336,128]{2,1,0:T(8,128)(2,1)S(1)}, u32[]{:S(2)}, u32[]{:S(2)}) %collective-permute-start.5) | collective-permute-done | bytes 344096 | tf_op jit(solution)/shard_map/ppermute | solution.py:351
  24.9 2.3 %rows2.1 = (bf16[1024,2048]{1,0:T(8,128)(2,1)S(1)}, f32[8,2048]{1,0:T(8,128)S(1)}) custom-call(s32[18]{0:T(128)S(1)} %pad_add_fusion.pos, bf16[4,336,128]{2,1,0:T(8,128)(2,1)S(1)} %collective-permute-done.5.refs_0_.g2, bf16[1024,256]{1,0:T(8,128)(2,1)S(1)} %get-tuple-element.46.refs_1_, f32[1,1024]{1,0:T(1,128)S(1)} %get-tuple-element.45.ready.refs_2_, ...), custom_call_target="tpu_custom_call" | custom-call | flops 2147483648 | tf_op jit(solution)/shard_map/rows2/pallas_call | solution.py:43
  27.2 2.4 %rows3.1 = (bf16[1024,2048]{1,0:T(8,128)(2,1)S(1)}, f32[128,1,256]{2,1,0:T(1,128)S(1)}) custom-call(s32[18]{0:T(128)S(1)} %pad_add_fusion.pos, bf16[4,336,128]{2,1,0:T(8,128)(2,1)S(1)} %collective-permute-done.6.refs_0_.g3, bf16[1024,256]{1,0:T(8,128)(2,1)S(1)} %get-tuple-element.46.refs_1_, f32[1,1024]{1,0:T(1,128)S(1)} %get-tuple-element.45.ready.refs_2_, ...), custom_call_target="tpu_custom_call" | custom-call | flops 2147483648 | tf_op jit(solution)/shard_map/rows3/pallas_call | solution.py:43
  29.6 17.9 %all_to_all.25.table = f32[128,1,256]{2,1,0:T(1,128)S(1)} all-to-all(f32[128,1,256]{2,1,0:T(1,128)S(1)} %get-tuple-element.56), channel_id=1, replica_groups=mesh['x'=4,'z'=4,'y'=4,'c'=2] {'y','z','x','c'}, dimensions={0} | all-to-all | bytes 262144 | tf_op jit(solution)/shard_map/all_to_all | solution.py:422
  47.5 2.8 %degree.1 = (f32[1,4096]{1,0:T(1,128)S(1)}, f32[128,1,256]{2,1,0:T(1,128)S(1)}) custom-call(s32[18]{0:T(128)S(1)} %pad_add_fusion.pos, bf16[1024,2048]{1,0:T(8,128)(2,1)S(1)} %get-tuple-element.49.k0, bf16[1024,2048]{1,0:T(8,128)(2,1)S(1)} %get-tuple-element.51.k1, bf16[1024,2048]{1,0:T(8,128)(2,1)S(1)} %get-tuple-element.53.k2, ...), custom_call_target="tpu_custom_call" | custom-call | tf_op jit(solution)/shard_map/degree/pallas_call | solution.py:43
  50.4 14.3 %all_to_all.26.table = f32[128,1,256]{2,1,0:T(1,128)S(1)} all-to-all(f32[128,1,256]{2,1,0:T(1,128)S(1)} %get-tuple-element.58), channel_id=1, replica_groups=mesh['x'=4,'z'=4,'y'=4,'c'=2] {'y','z','x','c'}, dimensions={0} | all-to-all | bytes 262144 | tf_op jit(solution)/shard_map/all_to_all | solution.py:428
  64.6 1.8 %first.1 = (bf16[16,4096]{1,0:T(8,128)(2,1)S(1)}, f32[1,4096]{1,0:T(1,128)S(1)}, f32[8,256]{1,0:T(8,128)S(1)}, f32[16,1024]{1,0:T(8,128)S(1)}) custom-call(s32[18]{0:T(128)S(1)} %pad_add_fusion.pos, bf16[1024,2048]{1,0:T(8,128)(2,1)S(1)} %get-tuple-element.49.k0, bf16[1024,2048]{1,0:T(8,128)(2,1)S(1)} %get-tuple-element.51.k1, ...), custom_call_target="tpu_custom_call" | custom-call | tf_op jit(solution)/shard_map/first/pallas_call | solution.py:43
  67.1 1.2 own1.1.own
  70.4 1.8 %collective-permute-start.10 = (f32[24,256]{1,0:T(8,128)S(1)}, f32[24,256]{1,0:T(8,128)S(1)}, u32[]{:S(2)}, u32[]{:S(2)}) collective-permute-start(f32[24,256]{1,0:T(8,128)S(1)} %get-tuple-element.65), channel_id=1, source_target_pairs={{96,0},{97,1},{98,2},{99,3},{100,4},{101,5},{102,6},{103,7},{104,8... | collective-permute-start | bytes 73736 | tf_op jit(solution)/shard_map/ppermute | solution.py:351
  74.8 10.6 %all_to_all.27.pieces = f32[16,16,256]{2,1,0:T(8,128)S(1)} all-to-all(f32[16,16,256]{2,1,0:T(8,128)S(1)} %get-tuple-element.68), channel_id=1, replica_groups=mesh['x'=4,'z'=4,'y'=4,'c'=2] {'y','z'}, dimensions={0} | all-to-all | bytes 524288 | tf_op jit(solution)/shard_map/all_to_all | solution.py:459
  85.4 2.0 %next1.1 = (bf16[32,4096]{1,0:T(8,128)(2,1)S(1)}, f32[16,128]{1,0:T(8,128)S(1)}, f32[16,1152]{1,0:T(8,128)S(1)}) custom-call(s32[18]{0:T(128)S(1)} %pad_add_fusion.pos, bf16[1024,2048]{1,0:T(8,128)(2,1)S(1)} %get-tuple-element.49.k0, bf16[1024,2048]{1,0:T(8,128)(2,1)S(1)} %get-tuple-element.51.k1, bf16[1024,2048]{1,0:T(8,128)(2,1)S(1)} %get-tuple-element.53.k2, ...), custom_call_target="tpu_custom_call" | custom-call | tf_op jit(solution)/shard_map/next1/pallas_call | solution.py:43
  87.4 3.2 %collective-permute-start.11 = (f32[16,1152]{1,0:T(8,128)S(1)}, f32[16,1152]{1,0:T(8,128)S(1)}, u32[]{:S(2)}, u32[]{:S(2)}) collective-permute-start(f32[16,1152]{1,0:T(8,128)S(1)} %get-tuple-element.70), channel_id=1, source_target_pairs={{1,0},{0,1},{3,2},{2,3},{5,4},{4,5},{7,6},{6,7},{9,8},{8,9},{11,10... | collective-permute-start | bytes 221192 | tf_op jit(solution)/shard_map/ppermute | solution.py:351
  90.5 1.4 %own2.1.own = f32[16,1024]{1,0:T(8,128)S(1)} custom-call(bf16[1024,2048]{1,0:T(8,128)(2,1)S(1)} %get-tuple-element.49.k0, bf16[1024,2048]{1,0:T(8,128)(2,1)S(1)} %get-tuple-element.51.k1, bf16[1024,2048]{1,0:T(8,128)(2,1)S(1)} %get-tuple-element.53.k2, bf16[1024,2048]{1,0:T(8,128)(2,1)S(1)} %get-tuple-element.55.k3, bf16[32,4096]{1,0:T(8,128)(2,1)S(1)} %get-tuple-element.69.vec), custom_call_target="tpu_custom_call" | custom-call | flops 2147483648 | tf_op jit(solution)/shard_map/own2/pallas_call | solution.py:43
  93.5 1.2 collective-permute-start.13
  94.7 1.2 collective-permute-start.14
  96.8 1.8 %collective-permute-done.14.q3 = f32[16,384]{1,0:T(8,128)S(1)} collective-permute-done((f32[16,384]{1,0:T(8,128)S(1)}, f32[16,384]{1,0:T(8,128)S(1)}, u32[]{:S(2)}, u32[]{:S(2)}) %collective-permute-start.14) | collective-permute-done | bytes 24608 | tf_op jit(solution)/shard_map/ppermute | solution.py:351
  98.9 10.5 %all_to_all.28.pieces = f32[16,16,256]{2,1,0:T(8,128)S(1)} all-to-all(f32[16,16,256]{2,1,0:T(8,128)S(1)} %project2.1), channel_id=1, replica_groups=mesh['x'=4,'z'=4,'y'=4,'c'=2] {'y','z'}, dimensions={0} | all-to-all | bytes 524288 | tf_op jit(solution)/shard_map/all_to_all | solution.py:459
  109.4 2.0 %next2.1 = (bf16[32,4096]{1,0:T(8,128)(2,1)S(1)}, f32[16,128]{1,0:T(8,128)S(1)}, f32[16,1152]{1,0:T(8,128)S(1)}) custom-call(s32[18]{0:T(128)S(1)} %pad_add_fusion.pos, bf16[1024,2048]{1,0:T(8,128)(2,1)S(1)} %get-tuple-element.49.k0, bf16[1024,2048]{1,0:T(8,128)(2,1)S(1)} %get-tuple-element.51.k1, bf16[1024,2048]{1,0:T(8,128)(2,1)S(1)} %get-tuple-element.53.k2, ...), custom_call_target="tpu_custom_call" | custom-call | tf_op jit(solution)/shard_map/next2/pallas_call | solution.py:43
  111.4 3.1 %collective-permute-start.15 = (f32[16,1152]{1,0:T(8,128)S(1)}, f32[16,1152]{1,0:T(8,128)S(1)}, u32[]{:S(2)}, u32[]{:S(2)}) collective-permute-start(f32[16,1152]{1,0:T(8,128)S(1)} %get-tuple-element.77), channel_id=1, source_target_pairs={{1,0},{0,1},{3,2},{2,3},{5,4},{4,5},{7,6},{6,7},{9,8},{8,9},{11,10... | collective-permute-start | bytes 221192 | tf_op jit(solution)/shard_map/ppermute | solution.py:351
  114.6 1.4 %own3.1.own = f32[16,1024]{1,0:T(8,128)S(1)} custom-call(bf16[1024,2048]{1,0:T(8,128)(2,1)S(1)} %get-tuple-element.49.k0, bf16[1024,2048]{1,0:T(8,128)(2,1)S(1)} %get-tuple-element.51.k1, bf16[1024,2048]{1,0:T(8,128)(2,1)S(1)} %get-tuple-element.53.k2, bf16[1024,2048]{1,0:T(8,128)(2,1)S(1)} %get-tuple-element.55.k3, bf16[32,4096]{1,0:T(8,128)(2,1)S(1)} %get-tuple-element.76.vec), custom_call_target="tpu_custom_call" | custom-call | flops 2147483648 | tf_op jit(solution)/shard_map/own3/pallas_call | solution.py:43
  116.1 1.5 %collective-permute-start.17 = (f32[16,1152]{1,0:T(8,128)S(1)}, f32[16,1152]{1,0:T(8,128)S(1)}, u32[]{:S(2)}, u32[]{:S(2)}) collective-permute-start(f32[16,1152]{1,0:T(8,128)S(1)} %core_add.1.q0), channel_id=1, source_target_pairs={{96,0},{97,1},{98,2},{99,3},{100,4},{101,5},{102,6},{103,7},{104,8... | collective-permute-start | bytes 221192 | tf_op jit(solution)/shard_map/ppermute | solution.py:351
  117.6 1.2 collective-permute-start.16
  118.7 2.8 %collective-permute-done.18.q3 = f32[16,1152]{1,0:T(8,128)S(1)} collective-permute-done((f32[16,1152]{1,0:T(8,128)S(1)}, f32[16,1152]{1,0:T(8,128)S(1)}, u32[]{:S(2)}, u32[]{:S(2)}) %collective-permute-start.18) | collective-permute-done | bytes 73760 | tf_op jit(solution)/shard_map/ppermute | solution.py:351
  121.5 1.4 %collective-permute-done.17.q2 = f32[16,1152]{1,0:T(8,128)S(1)} collective-permute-done((f32[16,1152]{1,0:T(8,128)S(1)}, f32[16,1152]{1,0:T(8,128)S(1)}, u32[]{:S(2)}, u32[]{:S(2)}) %collective-permute-start.17) | collective-permute-done | bytes 73760 | tf_op jit(solution)/shard_map/ppermute | solution.py:351
  123.6 11.8 %all_to_all.29.grams = f32[32,8,128]{2,1,0:T(8,128)S(1)} all-to-all(f32[32,8,128]{2,1,0:T(8,128)S(1)} %get-tuple-element.80), channel_id=1, replica_groups=mesh['x'=4,'z'=4,'y'=4,'c'=2] {'z','y','c'}, dimensions={0} | all-to-all | bytes 262144 | tf_op jit(solution)/shard_map/all_to_all | solution.py:477
  (35 shorter events, 14.4 us)
Async XLA Ops:
  2.5 13.8 %collective-permute-start.3 = (bf16[1040,128]{1,0:T(8,128)(2,1)S(1)}, bf16[1040,128]{1,0:T(8,128)(2,1)S(1)}, u32[]{:S(2)}, u32[]{:S(2)}) collective-permute-start(bf16[1040,128]{1,0:T(8,128)(2,1)S(1)} %get-tuple-element.44.block), channel_id=1, source_target_pairs={{1,0},{0,1},{3,2},{2,3},{5,4},{4,5},{7,6},{6,7},{9,8},{8,9},{11,10... | collective-permute-start | bytes 798728 | tf_op jit(solution)/shard_map/ppermute | solution.py:351
  4.0 5.7 %collective-permute-start.2 = (bf16[336,128]{1,0:T(8,128)(2,1)S(1)}, bf16[336,128]{1,0:T(8,128)(2,1)S(1)}, u32[]{:S(2)}, u32[]{:S(2)}) collective-permute-start(bf16[336,128]{1,0:T(8,128)(2,1)S(1)} %get-tuple-element.43.a), channel_id=1, source_target_pairs={{4,0},{17,1},{6,2},{19,3},{0,4},{21,5},{2,6},{23,7},{12,8},{25,9},... | collective-permute-start | bytes 258056 | tf_op jit(solution)/shard_map/ppermute | solution.py:351
  7.7 4.8 %collective-permute-start.1 = (bf16[336,128]{1,0:T(8,128)(2,1)S(1)}, bf16[336,128]{1,0:T(8,128)(2,1)S(1)}, u32[]{:S(2)}, u32[]{:S(2)}) collective-permute-start(bf16[336,128]{1,0:T(8,128)(2,1)S(1)} %get-tuple-element.43.a), channel_id=1, source_target_pairs={{6,0},{25,1},{4,2},{27,3},{2,4},{29,5},{0,6},{31,7},{14,8},{17,9},... | collective-permute-start | bytes 258056 | tf_op jit(solution)/shard_map/ppermute | solution.py:351
  8.1 4.4 %collective-permute-start = (bf16[336,128]{1,0:T(8,128)(2,1)S(1)}, bf16[336,128]{1,0:T(8,128)(2,1)S(1)}, u32[]{:S(2)}, u32[]{:S(2)}) collective-permute-start(bf16[336,128]{1,0:T(8,128)(2,1)S(1)} %get-tuple-element.43.a), channel_id=1, source_target_pairs={{2,0},{9,1},{0,2},{11,3},{6,4},{13,5},{4,6},{15,7},{10,8},{1,9},{8... | collective-permute-start | bytes 258056 | tf_op jit(solution)/shard_map/ppermute | solution.py:351
  12.6 6.5 %collective-permute-start.4 = (bf16[4,336,128]{2,1,0:T(8,128)(2,1)S(1)}, bf16[4,336,128]{2,1,0:T(8,128)(2,1)S(1)}, u32[]{:S(2)}, u32[]{:S(2)}) collective-permute-start(bf16[4,336,128]{2,1,0:T(8,128)(2,1)S(1)} %stack.9.refs_0_.g0), channel_id=1, source_target_pairs={{8,0},{3,1},{10,2},{1,3},{12,4},{7,5},{14,6},{5,7},{0,8},{11,9},{2... | collective-permute-start | bytes 1032200 | tf_op jit(solution)/shard_map/ppermute | solution.py:351
  13.7 13.5 %collective-permute-start.6 = (bf16[4,336,128]{2,1,0:T(8,128)(2,1)S(1)}, bf16[4,336,128]{2,1,0:T(8,128)(2,1)S(1)}, u32[]{:S(2)}, u32[]{:S(2)}) collective-permute-start(bf16[4,336,128]{2,1,0:T(8,128)(2,1)S(1)} %stack.9.refs_0_.g0), channel_id=1, source_target_pairs={{24,0},{7,1},{26,2},{5,3},{28,4},{3,5},{30,6},{1,7},{16,8},{15,9},... | collective-permute-start | bytes 1032200 | tf_op jit(solution)/shard_map/ppermute | solution.py:351
  15.6 9.3 %collective-permute-start.5 = (bf16[4,336,128]{2,1,0:T(8,128)(2,1)S(1)}, bf16[4,336,128]{2,1,0:T(8,128)(2,1)S(1)}, u32[]{:S(2)}, u32[]{:S(2)}) collective-permute-start(bf16[4,336,128]{2,1,0:T(8,128)(2,1)S(1)} %stack.9.refs_0_.g0), channel_id=1, source_target_pairs={{16,0},{5,1},{18,2},{7,3},{20,4},{1,5},{22,6},{3,7},{24,8},{13,9},... | collective-permute-start | bytes 1032200 | tf_op jit(solution)/shard_map/ppermute | solution.py:351
  66.4 1.9 %collective-permute-start.7 = (f32[16,1024]{1,0:T(8,128)S(1)}, f32[16,1024]{1,0:T(8,128)S(1)}, u32[]{:S(2)}, u32[]{:S(2)}) collective-permute-start(f32[16,1024]{1,0:T(8,128)S(1)} %get-tuple-element.61), channel_id=1, source_target_pairs={{1,0},{0,1},{3,2},{2,3},{5,4},{4,5},{7,6},{6,7},{9,8},{8,9},{11,10... | collective-permute-start | bytes 196616 | tf_op jit(solution)/shard_map/ppermute | solution.py:351
  68.9 4.3 %collective-permute-start.8 = (f32[24,256]{1,0:T(8,128)S(1)}, f32[24,256]{1,0:T(8,128)S(1)}, u32[]{:S(2)}, u32[]{:S(2)}) collective-permute-start(f32[24,256]{1,0:T(8,128)S(1)} %get-tuple-element.63), channel_id=1, source_target_pairs={{64,0},{65,1},{66,2},{67,3},{68,4},{69,5},{70,6},{71,7},{72,8},{73... | collective-permute-start | bytes 73736 | tf_op jit(solution)/shard_map/ppermute | solution.py:351
  69.7 3.4 %collective-permute-start.9 = (f32[24,256]{1,0:T(8,128)S(1)}, f32[24,256]{1,0:T(8,128)S(1)}, u32[]{:S(2)}, u32[]{:S(2)}) collective-permute-start(f32[24,256]{1,0:T(8,128)S(1)} %get-tuple-element.64), channel_id=1, source_target_pairs={{32,0},{33,1},{34,2},{35,3},{36,4},{37,5},{38,6},{39,7},{40,8},{41... | collective-permute-start | bytes 73736 | tf_op jit(solution)/shard_map/ppermute | solution.py:351
  70.4 3.9 %collective-permute-start.10 = (f32[24,256]{1,0:T(8,128)S(1)}, f32[24,256]{1,0:T(8,128)S(1)}, u32[]{:S(2)}, u32[]{:S(2)}) collective-permute-start(f32[24,256]{1,0:T(8,128)S(1)} %get-tuple-element.65), channel_id=1, source_target_pairs={{96,0},{97,1},{98,2},{99,3},{100,4},{101,5},{102,6},{103,7},{104,8... | collective-permute-start | bytes 73736 | tf_op jit(solution)/shard_map/ppermute | solution.py:351
  87.4 4.6 %collective-permute-start.11 = (f32[16,1152]{1,0:T(8,128)S(1)}, f32[16,1152]{1,0:T(8,128)S(1)}, u32[]{:S(2)}, u32[]{:S(2)}) collective-permute-start(f32[16,1152]{1,0:T(8,128)S(1)} %get-tuple-element.70), channel_id=1, source_target_pairs={{1,0},{0,1},{3,2},{2,3},{5,4},{4,5},{7,6},{6,7},{9,8},{8,9},{11,10... | collective-permute-start | bytes 221192 | tf_op jit(solution)/shard_map/ppermute | solution.py:351
  92.5 4.3 %collective-permute-start.12 = (f32[16,384]{1,0:T(8,128)S(1)}, f32[16,384]{1,0:T(8,128)S(1)}, u32[]{:S(2)}, u32[]{:S(2)}) collective-permute-start(f32[16,384]{1,0:T(8,128)S(1)} %get-tuple-element.73), channel_id=1, source_target_pairs={{64,0},{65,1},{66,2},{67,3},{68,4},{69,5},{70,6},{71,7},{72,8},{73... | collective-permute-start | bytes 73736 | tf_op jit(solution)/shard_map/ppermute | solution.py:351
  93.5 3.2 %collective-permute-start.13 = (f32[16,384]{1,0:T(8,128)S(1)}, f32[16,384]{1,0:T(8,128)S(1)}, u32[]{:S(2)}, u32[]{:S(2)}) collective-permute-start(f32[16,384]{1,0:T(8,128)S(1)} %get-tuple-element.74), channel_id=1, source_target_pairs={{32,0},{33,1},{34,2},{35,3},{36,4},{37,5},{38,6},{39,7},{40,8},{41... | collective-permute-start | bytes 73736 | tf_op jit(solution)/shard_map/ppermute | solution.py:351
  94.7 3.9 %collective-permute-start.14 = (f32[16,384]{1,0:T(8,128)S(1)}, f32[16,384]{1,0:T(8,128)S(1)}, u32[]{:S(2)}, u32[]{:S(2)}) collective-permute-start(f32[16,384]{1,0:T(8,128)S(1)} %get-tuple-element.75), channel_id=1, source_target_pairs={{96,0},{97,1},{98,2},{99,3},{100,4},{101,5},{102,6},{103,7},{104,8... | collective-permute-start | bytes 73736 | tf_op jit(solution)/shard_map/ppermute | solution.py:351
  111.4 4.6 %collective-permute-start.15 = (f32[16,1152]{1,0:T(8,128)S(1)}, f32[16,1152]{1,0:T(8,128)S(1)}, u32[]{:S(2)}, u32[]{:S(2)}) collective-permute-start(f32[16,1152]{1,0:T(8,128)S(1)} %get-tuple-element.77), channel_id=1, source_target_pairs={{1,0},{0,1},{3,2},{2,3},{5,4},{4,5},{7,6},{6,7},{9,8},{8,9},{11,10... | collective-permute-start | bytes 221192 | tf_op jit(solution)/shard_map/ppermute | solution.py:351
  116.0 5.5 %collective-permute-start.18 = (f32[16,1152]{1,0:T(8,128)S(1)}, f32[16,1152]{1,0:T(8,128)S(1)}, u32[]{:S(2)}, u32[]{:S(2)}) collective-permute-start(f32[16,1152]{1,0:T(8,128)S(1)} %core_add.1.q0), channel_id=1, source_target_pairs={{64,0},{65,1},{66,2},{67,3},{68,4},{69,5},{70,6},{71,7},{72,8},{73... | collective-permute-start | bytes 221192 | tf_op jit(solution)/shard_map/ppermute | solution.py:351
  116.1 6.9 %collective-permute-start.17 = (f32[16,1152]{1,0:T(8,128)S(1)}, f32[16,1152]{1,0:T(8,128)S(1)}, u32[]{:S(2)}, u32[]{:S(2)}) collective-permute-start(f32[16,1152]{1,0:T(8,128)S(1)} %core_add.1.q0), channel_id=1, source_target_pairs={{96,0},{97,1},{98,2},{99,3},{100,4},{101,5},{102,6},{103,7},{104,8... | collective-permute-start | bytes 221192 | tf_op jit(solution)/shard_map/ppermute | solution.py:351
  117.6 5.4 %collective-permute-start.16 = (f32[16,1152]{1,0:T(8,128)S(1)}, f32[16,1152]{1,0:T(8,128)S(1)}, u32[]{:S(2)}, u32[]{:S(2)}) collective-permute-start(f32[16,1152]{1,0:T(8,128)S(1)} %core_add.1.q0), channel_id=1, source_target_pairs={{32,0},{33,1},{34,2},{35,3},{36,4},{37,5},{38,6},{39,7},{40,8},{41... | collective-permute-start | bytes 221192 | tf_op jit(solution)/shard_map/ppermute | solution.py:351

commit v7 on v6

--- a/solution.py
+++ b/solution.py
@@ -75,8 +75,8 @@
     )
     for copy in copies:
         copy.start()
-    for copy in copies:
-        copy.wait()
+    copies[2].wait()
+    copies[0].wait()
     cls = own_classes[...].astype(F32)
     mine[CB:, :] = jnp.concatenate([cls, jnp.zeros_like(cls)], axis=0).astype(BF16)
     wide = piece[0:QB, :].astype(F32)
@@ -92,12 +92,14 @@
     extra.append(own_classes[pl.ds(2 * x + 1, 1), :].astype(F32))
     extra.append(jnp.ones((8, 128), F32))
     piece[CLS:PROWS, :] = jnp.concatenate(extra, axis=0).astype(BF16)
+    copies[1].wait()
     high = quarter[...].astype(BF16)
     low = (quarter[...] - high.astype(F32)).astype(BF16)
     for h in range(2):
         at = QB + 2 * h * KV
         piece[at : at + KV, :] = high[:, h * 128 : (h + 1) * 128]
         piece[at + KV : at + 2 * KV, :] = low[:, h * 128 : (h + 1) * 128]
+    copies[3].wait()
 
 
 def stack_kernel(a, b, d, c, ready, out):
@@ -313,7 +315,7 @@
     p = y * weight_own[...]
     proj[...] = p
     gram = lax.dot_general(p, p, NT, precision=lax.Precision.HIGHEST, preferred_element_type=F32)
-    gram = jnp.concatenate([gram[:8], gram[8:], jnp.zeros((8, 128 - 2 * KV), F32)], axis=1)
+    gram = jnp.concatenate([gram[k : k + 1] for k in range(KV)], axis=1)
     for n in range(32):
         grams[n] = gram
 
@@ -324,7 +326,7 @@
     while len(terms) > 1:
         terms = [a + b for a, b in zip(terms[::2], terms[1::2])]
     wide = terms[0]
-    gram = jnp.concatenate([wide[:, :KV], wide[:, KV : 2 * KV]], axis=0)
+    gram = jnp.concatenate([wide[:, k * KV : (k + 1) * KV] for k in range(KV)], axis=0)
     gram = jnp.concatenate([gram, jnp.zeros((KV, 128 - KV), F32)], axis=1)
     lane = lax.broadcasted_iota(jnp.int32, (KV, 128), 1)
     row = lax.broadcasted_iota(jnp.int32, (KV, 128), 0)
@@ -472,7 +474,7 @@
     )
     totals = [total] + [from_x(total, d) for d in (1, 3, 2)]
     proj, grams = call(
-        last_kernel, "last", [sds((KV, CB)), sds((32, 8, 128))], (weight_own, *totals)
+        last_kernel, "last", [sds((KV, CB)), sds((32, 1, KV * KV))], (weight_own, *totals)
     )
     grams = lax.all_to_all(grams, ("z", "y", "c"), 0, 0)
     embedding, log_degree = call(

time: 137 us -> 136 us (level)
  no operation moved by 1% of the time
where the time goes in v7:
time: 136 us
  blocking collectives  64.7 us (48%)
  Pallas kernels  27.8 us (20%)
  starting transfers between devices  26 us (19%)
  waiting for transfers between devices  16.6 us (12%)
    pallas_call x22, Pallas kernels, call(): pl.pallas_call(kernel, out_shape=outs, in_specs=[spec(n, a) for n, a in e...  27.8 us
    ppermute x19, starting transfers between devices, shift(): return lax.ppermute(v, ('x', 'z', 'y', 'c'), pairs)  26 us
    all_to_all x2, blocking collectives, body(): pieces = lax.all_to_all(pieces, ('y', 'z'), 0, 0)  21.1 us
    all_to_all x1, blocking collectives, body(): lax.all_to_all(sums[0], everyone, 0, 0)  17.9 us
    ppermute x19, waiting for transfers between devices, shift(): return lax.ppermute(v, ('x', 'z', 'y', 'c'), pairs)  16.6 us
    all_to_all x1, blocking collectives, body(): lax.all_to_all(table, everyone, 0, 0)  14.3 us
    all_to_all x1, blocking collectives, body(): grams = lax.all_to_all(grams, ('z', 'y', 'c'), 0, 0)  11.5 us
  transfers between devices with their start and end apart: 19, of which 10 were waited for; matrix products, arithmetic and copies ran while one was open for 0% of the time, Pallas kernels for 8%

profile of v7, /device:TPU:1, one launch (start us, length us, event | category | flops | bytes accessed | tf_op | source)
XLA Modules:
  0.0 136.0 jit_solution(10142053139402939221)
XLA Ops:
  0.7 1.6 %pack.1 = (bf16[336,128]{1,0:T(8,128)(2,1)S(1)}, bf16[1040,128]{1,0:T(8,128)(2,1)S(1)}) custom-call(s32[18]{0:T(128)S(1)} %pad_add_fusion.pos, bf16[1024,128]{1,0:T(8,128)(2,1)} %frames.1, s32[8,128]{1,0:T(8,128)} %bitcast.4, f32[16,1024]{1,0:T(8,128)} %start.1), custom_call_target="tpu_custom_call" | custom-call | tf_op jit(solution)/shard_map/pack/pallas_call | solution.py:43
  2.4 1.5 %collective-permute-start.3 = (bf16[1040,128]{1,0:T(8,128)(2,1)S(1)}, bf16[1040,128]{1,0:T(8,128)(2,1)S(1)}, u32[]{:S(2)}, u32[]{:S(2)}) collective-permute-start(bf16[1040,128]{1,0:T(8,128)(2,1)S(1)} %get-tuple-element.44.block), channel_id=1, source_target_pairs={{1,0},{0,1},{3,2},{2,3},{5,4},{4,5},{7,6},{6,7},{9,8},{8,9},{11,10... | collective-permute-start | bytes 798728 | tf_op jit(solution)/shard_map/ppermute | solution.py:353
  3.9 3.7 %collective-permute-start.2 = (bf16[336,128]{1,0:T(8,128)(2,1)S(1)}, bf16[336,128]{1,0:T(8,128)(2,1)S(1)}, u32[]{:S(2)}, u32[]{:S(2)}) collective-permute-start(bf16[336,128]{1,0:T(8,128)(2,1)S(1)} %get-tuple-element.43.a), channel_id=1, source_target_pairs={{4,0},{17,1},{6,2},{19,3},{0,4},{21,5},{2,6},{23,7},{12,8},{25,9},... | collective-permute-start | bytes 258056 | tf_op jit(solution)/shard_map/ppermute | solution.py:353
  9.5 2.8 %collective-permute-done.1.d = bf16[336,128]{1,0:T(8,128)(2,1)S(1)} collective-permute-done((bf16[336,128]{1,0:T(8,128)(2,1)S(1)}, bf16[336,128]{1,0:T(8,128)(2,1)S(1)}, u32[]{:S(2)}, u32[]{:S(2)}) %collective-permute-start.1) | collective-permute-done | bytes 86048 | tf_op jit(solution)/shard_map/ppermute | solution.py:353
  13.5 1.9 %collective-permute-start.6 = (bf16[4,336,128]{2,1,0:T(8,128)(2,1)S(1)}, bf16[4,336,128]{2,1,0:T(8,128)(2,1)S(1)}, u32[]{:S(2)}, u32[]{:S(2)}) collective-permute-start(bf16[4,336,128]{2,1,0:T(8,128)(2,1)S(1)} %stack.9.refs_0_.g0), channel_id=1, source_target_pairs={{24,0},{7,1},{26,2},{5,3},{28,4},{3,5},{30,6},{1,7},{16,8},{15,9},... | collective-permute-start | bytes 1032200 | tf_op jit(solution)/shard_map/ppermute | solution.py:353
  16.4 2.3 %rows0.1 = (bf16[1024,2048]{1,0:T(8,128)(2,1)S(1)}, f32[8,2048]{1,0:T(8,128)S(1)}) custom-call(s32[18]{0:T(128)S(1)} %pad_add_fusion.pos, bf16[4,336,128]{2,1,0:T(8,128)(2,1)S(1)} %stack.9.refs_0_.g0, bf16[1024,256]{1,0:T(8,128)(2,1)S(1)} %get-tuple-element.46.refs_1_, f32[1,1024]{1,0:T(1,128)S(1)} %get-tuple-element.45.ready.refs_2_, ...), custom_call_target="tpu_custom_call" | custom-call | flops 2147483648 | tf_op jit(solution)/shard_map/rows0/pallas_call | solution.py:43
  18.9 2.3 %rows1.1 = (bf16[1024,2048]{1,0:T(8,128)(2,1)S(1)}, f32[8,2048]{1,0:T(8,128)S(1)}) custom-call(s32[18]{0:T(128)S(1)} %pad_add_fusion.pos, bf16[4,336,128]{2,1,0:T(8,128)(2,1)S(1)} %collective-permute-done.4.refs_0_.g1, bf16[1024,256]{1,0:T(8,128)(2,1)S(1)} %get-tuple-element.46.refs_1_, f32[1,1024]{1,0:T(1,128)S(1)} %get-tuple-element.45.ready.refs_2_, ...), custom_call_target="tpu_custom_call" | custom-call | flops 2147483648 | tf_op jit(solution)/shard_map/rows1/pallas_call | solution.py:43
  21.2 3.5 %collective-permute-done.5.refs_0_.g2 = bf16[4,336,128]{2,1,0:T(8,128)(2,1)S(1)} collective-permute-done((bf16[4,336,128]{2,1,0:T(8,128)(2,1)S(1)}, bf16[4,336,128]{2,1,0:T(8,128)(2,1)S(1)}, u32[]{:S(2)}, u32[]{:S(2)}) %collective-permute-start.5) | collective-permute-done | bytes 344096 | tf_op jit(solution)/shard_map/ppermute | solution.py:353
  24.7 2.3 %rows2.1 = (bf16[1024,2048]{1,0:T(8,128)(2,1)S(1)}, f32[8,2048]{1,0:T(8,128)S(1)}) custom-call(s32[18]{0:T(128)S(1)} %pad_add_fusion.pos, bf16[4,336,128]{2,1,0:T(8,128)(2,1)S(1)} %collective-permute-done.5.refs_0_.g2, bf16[1024,256]{1,0:T(8,128)(2,1)S(1)} %get-tuple-element.46.refs_1_, f32[1,1024]{1,0:T(1,128)S(1)} %get-tuple-element.45.ready.refs_2_, ...), custom_call_target="tpu_custom_call" | custom-call | flops 2147483648 | tf_op jit(solution)/shard_map/rows2/pallas_call | solution.py:43
  27.0 2.4 %rows3.1 = (bf16[1024,2048]{1,0:T(8,128)(2,1)S(1)}, f32[128,1,256]{2,1,0:T(1,128)S(1)}) custom-call(s32[18]{0:T(128)S(1)} %pad_add_fusion.pos, bf16[4,336,128]{2,1,0:T(8,128)(2,1)S(1)} %collective-permute-done.6.refs_0_.g3, bf16[1024,256]{1,0:T(8,128)(2,1)S(1)} %get-tuple-element.46.refs_1_, f32[1,1024]{1,0:T(1,128)S(1)} %get-tuple-element.45.ready.refs_2_, ...), custom_call_target="tpu_custom_call" | custom-call | flops 2147483648 | tf_op jit(solution)/shard_map/rows3/pallas_call | solution.py:43
  29.4 17.9 %all_to_all.25.table = f32[128,1,256]{2,1,0:T(1,128)S(1)} all-to-all(f32[128,1,256]{2,1,0:T(1,128)S(1)} %get-tuple-element.56), channel_id=1, replica_groups=mesh['x'=4,'z'=4,'y'=4,'c'=2] {'y','z','x','c'}, dimensions={0} | all-to-all | bytes 262144 | tf_op jit(solution)/shard_map/all_to_all | solution.py:424
  47.3 2.8 %degree.1 = (f32[1,4096]{1,0:T(1,128)S(1)}, f32[128,1,256]{2,1,0:T(1,128)S(1)}) custom-call(s32[18]{0:T(128)S(1)} %pad_add_fusion.pos, bf16[1024,2048]{1,0:T(8,128)(2,1)S(1)} %get-tuple-element.49.k0, bf16[1024,2048]{1,0:T(8,128)(2,1)S(1)} %get-tuple-element.51.k1, bf16[1024,2048]{1,0:T(8,128)(2,1)S(1)} %get-tuple-element.53.k2, ...), custom_call_target="tpu_custom_call" | custom-call | tf_op jit(solution)/shard_map/degree/pallas_call | solution.py:43
  50.2 14.3 %all_to_all.26.table = f32[128,1,256]{2,1,0:T(1,128)S(1)} all-to-all(f32[128,1,256]{2,1,0:T(1,128)S(1)} %get-tuple-element.58), channel_id=1, replica_groups=mesh['x'=4,'z'=4,'y'=4,'c'=2] {'y','z','x','c'}, dimensions={0} | all-to-all | bytes 262144 | tf_op jit(solution)/shard_map/all_to_all | solution.py:430
  64.5 1.8 %first.1 = (bf16[16,4096]{1,0:T(8,128)(2,1)S(1)}, f32[1,4096]{1,0:T(1,128)S(1)}, f32[8,256]{1,0:T(8,128)S(1)}, f32[16,1024]{1,0:T(8,128)S(1)}) custom-call(s32[18]{0:T(128)S(1)} %pad_add_fusion.pos, bf16[1024,2048]{1,0:T(8,128)(2,1)S(1)} %get-tuple-element.49.k0, bf16[1024,2048]{1,0:T(8,128)(2,1)S(1)} %get-tuple-element.51.k1, ...), custom_call_target="tpu_custom_call" | custom-call | tf_op jit(solution)/shard_map/first/pallas_call | solution.py:43
  66.9 1.2 own1.1.own
  70.2 1.8 %collective-permute-start.10 = (f32[24,256]{1,0:T(8,128)S(1)}, f32[24,256]{1,0:T(8,128)S(1)}, u32[]{:S(2)}, u32[]{:S(2)}) collective-permute-start(f32[24,256]{1,0:T(8,128)S(1)} %get-tuple-element.65), channel_id=1, source_target_pairs={{96,0},{97,1},{98,2},{99,3},{100,4},{101,5},{102,6},{103,7},{104,8... | collective-permute-start | bytes 73736 | tf_op jit(solution)/shard_map/ppermute | solution.py:353
  74.7 10.6 %all_to_all.27.pieces = f32[16,16,256]{2,1,0:T(8,128)S(1)} all-to-all(f32[16,16,256]{2,1,0:T(8,128)S(1)} %get-tuple-element.68), channel_id=1, replica_groups=mesh['x'=4,'z'=4,'y'=4,'c'=2] {'y','z'}, dimensions={0} | all-to-all | bytes 524288 | tf_op jit(solution)/shard_map/all_to_all | solution.py:461
  85.2 2.0 %next1.1 = (bf16[32,4096]{1,0:T(8,128)(2,1)S(1)}, f32[16,128]{1,0:T(8,128)S(1)}, f32[16,1152]{1,0:T(8,128)S(1)}) custom-call(s32[18]{0:T(128)S(1)} %pad_add_fusion.pos, bf16[1024,2048]{1,0:T(8,128)(2,1)S(1)} %get-tuple-element.49.k0, bf16[1024,2048]{1,0:T(8,128)(2,1)S(1)} %get-tuple-element.51.k1, bf16[1024,2048]{1,0:T(8,128)(2,1)S(1)} %get-tuple-element.53.k2, ...), custom_call_target="tpu_custom_call" | custom-call | tf_op jit(solution)/shard_map/next1/pallas_call | solution.py:43
  87.2 3.2 %collective-permute-start.11 = (f32[16,1152]{1,0:T(8,128)S(1)}, f32[16,1152]{1,0:T(8,128)S(1)}, u32[]{:S(2)}, u32[]{:S(2)}) collective-permute-start(f32[16,1152]{1,0:T(8,128)S(1)} %get-tuple-element.70), channel_id=1, source_target_pairs={{1,0},{0,1},{3,2},{2,3},{5,4},{4,5},{7,6},{6,7},{9,8},{8,9},{11,10... | collective-permute-start | bytes 221192 | tf_op jit(solution)/shard_map/ppermute | solution.py:353
  90.4 1.4 %own2.1.own = f32[16,1024]{1,0:T(8,128)S(1)} custom-call(bf16[1024,2048]{1,0:T(8,128)(2,1)S(1)} %get-tuple-element.49.k0, bf16[1024,2048]{1,0:T(8,128)(2,1)S(1)} %get-tuple-element.51.k1, bf16[1024,2048]{1,0:T(8,128)(2,1)S(1)} %get-tuple-element.53.k2, bf16[1024,2048]{1,0:T(8,128)(2,1)S(1)} %get-tuple-element.55.k3, bf16[32,4096]{1,0:T(8,128)(2,1)S(1)} %get-tuple-element.69.vec), custom_call_target="tpu_custom_call" | custom-call | flops 2147483648 | tf_op jit(solution)/shard_map/own2/pallas_call | solution.py:43
  93.4 1.2 collective-permute-start.13
  94.5 1.2 collective-permute-start.14
  96.6 1.8 %collective-permute-done.14.q3 = f32[16,384]{1,0:T(8,128)S(1)} collective-permute-done((f32[16,384]{1,0:T(8,128)S(1)}, f32[16,384]{1,0:T(8,128)S(1)}, u32[]{:S(2)}, u32[]{:S(2)}) %collective-permute-start.14) | collective-permute-done | bytes 24608 | tf_op jit(solution)/shard_map/ppermute | solution.py:353
  98.7 10.5 %all_to_all.28.pieces = f32[16,16,256]{2,1,0:T(8,128)S(1)} all-to-all(f32[16,16,256]{2,1,0:T(8,128)S(1)} %project2.1), channel_id=1, replica_groups=mesh['x'=4,'z'=4,'y'=4,'c'=2] {'y','z'}, dimensions={0} | all-to-all | bytes 524288 | tf_op jit(solution)/shard_map/all_to_all | solution.py:461
  109.3 2.0 %next2.1 = (bf16[32,4096]{1,0:T(8,128)(2,1)S(1)}, f32[16,128]{1,0:T(8,128)S(1)}, f32[16,1152]{1,0:T(8,128)S(1)}) custom-call(s32[18]{0:T(128)S(1)} %pad_add_fusion.pos, bf16[1024,2048]{1,0:T(8,128)(2,1)S(1)} %get-tuple-element.49.k0, bf16[1024,2048]{1,0:T(8,128)(2,1)S(1)} %get-tuple-element.51.k1, bf16[1024,2048]{1,0:T(8,128)(2,1)S(1)} %get-tuple-element.53.k2, ...), custom_call_target="tpu_custom_call" | custom-call | tf_op jit(solution)/shard_map/next2/pallas_call | solution.py:43
  111.3 3.1 %collective-permute-start.15 = (f32[16,1152]{1,0:T(8,128)S(1)}, f32[16,1152]{1,0:T(8,128)S(1)}, u32[]{:S(2)}, u32[]{:S(2)}) collective-permute-start(f32[16,1152]{1,0:T(8,128)S(1)} %get-tuple-element.77), channel_id=1, source_target_pairs={{1,0},{0,1},{3,2},{2,3},{5,4},{4,5},{7,6},{6,7},{9,8},{8,9},{11,10... | collective-permute-start | bytes 221192 | tf_op jit(solution)/shard_map/ppermute | solution.py:353
  114.4 1.4 %own3.1.own = f32[16,1024]{1,0:T(8,128)S(1)} custom-call(bf16[1024,2048]{1,0:T(8,128)(2,1)S(1)} %get-tuple-element.49.k0, bf16[1024,2048]{1,0:T(8,128)(2,1)S(1)} %get-tuple-element.51.k1, bf16[1024,2048]{1,0:T(8,128)(2,1)S(1)} %get-tuple-element.53.k2, bf16[1024,2048]{1,0:T(8,128)(2,1)S(1)} %get-tuple-element.55.k3, bf16[32,4096]{1,0:T(8,128)(2,1)S(1)} %get-tuple-element.76.vec), custom_call_target="tpu_custom_call" | custom-call | flops 2147483648 | tf_op jit(solution)/shard_map/own3/pallas_call | solution.py:43
  115.9 1.5 %collective-permute-start.17 = (f32[16,1152]{1,0:T(8,128)S(1)}, f32[16,1152]{1,0:T(8,128)S(1)}, u32[]{:S(2)}, u32[]{:S(2)}) collective-permute-start(f32[16,1152]{1,0:T(8,128)S(1)} %core_add.1.q0), channel_id=1, source_target_pairs={{96,0},{97,1},{98,2},{99,3},{100,4},{101,5},{102,6},{103,7},{104,8... | collective-permute-start | bytes 221192 | tf_op jit(solution)/shard_map/ppermute | solution.py:353
  117.4 1.2 collective-permute-start.16
  118.6 2.8 %collective-permute-done.18.q3 = f32[16,1152]{1,0:T(8,128)S(1)} collective-permute-done((f32[16,1152]{1,0:T(8,128)S(1)}, f32[16,1152]{1,0:T(8,128)S(1)}, u32[]{:S(2)}, u32[]{:S(2)}) %collective-permute-start.18) | collective-permute-done | bytes 73760 | tf_op jit(solution)/shard_map/ppermute | solution.py:353
  121.4 1.4 %collective-permute-done.17.q2 = f32[16,1152]{1,0:T(8,128)S(1)} collective-permute-done((f32[16,1152]{1,0:T(8,128)S(1)}, f32[16,1152]{1,0:T(8,128)S(1)}, u32[]{:S(2)}, u32[]{:S(2)}) %collective-permute-start.17) | collective-permute-done | bytes 73760 | tf_op jit(solution)/shard_map/ppermute | solution.py:353
  123.4 11.5 %all_to_all.29.grams = f32[32,1,256]{2,1,0:T(1,128)S(1)} all-to-all(f32[32,1,256]{2,1,0:T(1,128)S(1)} %get-tuple-element.80), channel_id=1, replica_groups=mesh['x'=4,'z'=4,'y'=4,'c'=2] {'z','y','c'}, dimensions={0} | all-to-all | bytes 65536 | tf_op jit(solution)/shard_map/all_to_all | solution.py:479
  (35 shorter events, 14.5 us)
Async XLA Ops:
  2.4 13.8 %collective-permute-start.3 = (bf16[1040,128]{1,0:T(8,128)(2,1)S(1)}, bf16[1040,128]{1,0:T(8,128)(2,1)S(1)}, u32[]{:S(2)}, u32[]{:S(2)}) collective-permute-start(bf16[1040,128]{1,0:T(8,128)(2,1)S(1)} %get-tuple-element.44.block), channel_id=1, source_target_pairs={{1,0},{0,1},{3,2},{2,3},{5,4},{4,5},{7,6},{6,7},{9,8},{8,9},{11,10... | collective-permute-start | bytes 798728 | tf_op jit(solution)/shard_map/ppermute | solution.py:353
  3.9 5.7 %collective-permute-start.2 = (bf16[336,128]{1,0:T(8,128)(2,1)S(1)}, bf16[336,128]{1,0:T(8,128)(2,1)S(1)}, u32[]{:S(2)}, u32[]{:S(2)}) collective-permute-start(bf16[336,128]{1,0:T(8,128)(2,1)S(1)} %get-tuple-element.43.a), channel_id=1, source_target_pairs={{4,0},{17,1},{6,2},{19,3},{0,4},{21,5},{2,6},{23,7},{12,8},{25,9},... | collective-permute-start | bytes 258056 | tf_op jit(solution)/shard_map/ppermute | solution.py:353
  7.5 4.8 %collective-permute-start.1 = (bf16[336,128]{1,0:T(8,128)(2,1)S(1)}, bf16[336,128]{1,0:T(8,128)(2,1)S(1)}, u32[]{:S(2)}, u32[]{:S(2)}) collective-permute-start(bf16[336,128]{1,0:T(8,128)(2,1)S(1)} %get-tuple-element.43.a), channel_id=1, source_target_pairs={{6,0},{25,1},{4,2},{27,3},{2,4},{29,5},{0,6},{31,7},{14,8},{17,9},... | collective-permute-start | bytes 258056 | tf_op jit(solution)/shard_map/ppermute | solution.py:353
  8.0 4.4 %collective-permute-start = (bf16[336,128]{1,0:T(8,128)(2,1)S(1)}, bf16[336,128]{1,0:T(8,128)(2,1)S(1)}, u32[]{:S(2)}, u32[]{:S(2)}) collective-permute-start(bf16[336,128]{1,0:T(8,128)(2,1)S(1)} %get-tuple-element.43.a), channel_id=1, source_target_pairs={{2,0},{9,1},{0,2},{11,3},{6,4},{13,5},{4,6},{15,7},{10,8},{1,9},{8... | collective-permute-start | bytes 258056 | tf_op jit(solution)/shard_map/ppermute | solution.py:353
  12.4 6.5 %collective-permute-start.4 = (bf16[4,336,128]{2,1,0:T(8,128)(2,1)S(1)}, bf16[4,336,128]{2,1,0:T(8,128)(2,1)S(1)}, u32[]{:S(2)}, u32[]{:S(2)}) collective-permute-start(bf16[4,336,128]{2,1,0:T(8,128)(2,1)S(1)} %stack.9.refs_0_.g0), channel_id=1, source_target_pairs={{8,0},{3,1},{10,2},{1,3},{12,4},{7,5},{14,6},{5,7},{0,8},{11,9},{2... | collective-permute-start | bytes 1032200 | tf_op jit(solution)/shard_map/ppermute | solution.py:353
  13.5 13.5 %collective-permute-start.6 = (bf16[4,336,128]{2,1,0:T(8,128)(2,1)S(1)}, bf16[4,336,128]{2,1,0:T(8,128)(2,1)S(1)}, u32[]{:S(2)}, u32[]{:S(2)}) collective-permute-start(bf16[4,336,128]{2,1,0:T(8,128)(2,1)S(1)} %stack.9.refs_0_.g0), channel_id=1, source_target_pairs={{24,0},{7,1},{26,2},{5,3},{28,4},{3,5},{30,6},{1,7},{16,8},{15,9},... | collective-permute-start | bytes 1032200 | tf_op jit(solution)/shard_map/ppermute | solution.py:353
  15.4 9.3 %collective-permute-start.5 = (bf16[4,336,128]{2,1,0:T(8,128)(2,1)S(1)}, bf16[4,336,128]{2,1,0:T(8,128)(2,1)S(1)}, u32[]{:S(2)}, u32[]{:S(2)}) collective-permute-start(bf16[4,336,128]{2,1,0:T(8,128)(2,1)S(1)} %stack.9.refs_0_.g0), channel_id=1, source_target_pairs={{16,0},{5,1},{18,2},{7,3},{20,4},{1,5},{22,6},{3,7},{24,8},{13,9},... | collective-permute-start | bytes 1032200 | tf_op jit(solution)/shard_map/ppermute | solution.py:353
  66.2 1.9 %collective-permute-start.7 = (f32[16,1024]{1,0:T(8,128)S(1)}, f32[16,1024]{1,0:T(8,128)S(1)}, u32[]{:S(2)}, u32[]{:S(2)}) collective-permute-start(f32[16,1024]{1,0:T(8,128)S(1)} %get-tuple-element.61), channel_id=1, source_target_pairs={{1,0},{0,1},{3,2},{2,3},{5,4},{4,5},{7,6},{6,7},{9,8},{8,9},{11,10... | collective-permute-start | bytes 196616 | tf_op jit(solution)/shard_map/ppermute | solution.py:353
  68.7 4.3 %collective-permute-start.8 = (f32[24,256]{1,0:T(8,128)S(1)}, f32[24,256]{1,0:T(8,128)S(1)}, u32[]{:S(2)}, u32[]{:S(2)}) collective-permute-start(f32[24,256]{1,0:T(8,128)S(1)} %get-tuple-element.63), channel_id=1, source_target_pairs={{64,0},{65,1},{66,2},{67,3},{68,4},{69,5},{70,6},{71,7},{72,8},{73... | collective-permute-start | bytes 73736 | tf_op jit(solution)/shard_map/ppermute | solution.py:353
  69.6 3.4 %collective-permute-start.9 = (f32[24,256]{1,0:T(8,128)S(1)}, f32[24,256]{1,0:T(8,128)S(1)}, u32[]{:S(2)}, u32[]{:S(2)}) collective-permute-start(f32[24,256]{1,0:T(8,128)S(1)} %get-tuple-element.64), channel_id=1, source_target_pairs={{32,0},{33,1},{34,2},{35,3},{36,4},{37,5},{38,6},{39,7},{40,8},{41... | collective-permute-start | bytes 73736 | tf_op jit(solution)/shard_map/ppermute | solution.py:353
  70.2 3.9 %collective-permute-start.10 = (f32[24,256]{1,0:T(8,128)S(1)}, f32[24,256]{1,0:T(8,128)S(1)}, u32[]{:S(2)}, u32[]{:S(2)}) collective-permute-start(f32[24,256]{1,0:T(8,128)S(1)} %get-tuple-element.65), channel_id=1, source_target_pairs={{96,0},{97,1},{98,2},{99,3},{100,4},{101,5},{102,6},{103,7},{104,8... | collective-permute-start | bytes 73736 | tf_op jit(solution)/shard_map/ppermute | solution.py:353
  87.2 4.6 %collective-permute-start.11 = (f32[16,1152]{1,0:T(8,128)S(1)}, f32[16,1152]{1,0:T(8,128)S(1)}, u32[]{:S(2)}, u32[]{:S(2)}) collective-permute-start(f32[16,1152]{1,0:T(8,128)S(1)} %get-tuple-element.70), channel_id=1, source_target_pairs={{1,0},{0,1},{3,2},{2,3},{5,4},{4,5},{7,6},{6,7},{9,8},{8,9},{11,10... | collective-permute-start | bytes 221192 | tf_op jit(solution)/shard_map/ppermute | solution.py:353
  92.4 4.3 %collective-permute-start.12 = (f32[16,384]{1,0:T(8,128)S(1)}, f32[16,384]{1,0:T(8,128)S(1)}, u32[]{:S(2)}, u32[]{:S(2)}) collective-permute-start(f32[16,384]{1,0:T(8,128)S(1)} %get-tuple-element.73), channel_id=1, source_target_pairs={{64,0},{65,1},{66,2},{67,3},{68,4},{69,5},{70,6},{71,7},{72,8},{73... | collective-permute-start | bytes 73736 | tf_op jit(solution)/shard_map/ppermute | solution.py:353
  93.4 3.3 %collective-permute-start.13 = (f32[16,384]{1,0:T(8,128)S(1)}, f32[16,384]{1,0:T(8,128)S(1)}, u32[]{:S(2)}, u32[]{:S(2)}) collective-permute-start(f32[16,384]{1,0:T(8,128)S(1)} %get-tuple-element.74), channel_id=1, source_target_pairs={{32,0},{33,1},{34,2},{35,3},{36,4},{37,5},{38,6},{39,7},{40,8},{41... | collective-permute-start | bytes 73736 | tf_op jit(solution)/shard_map/ppermute | solution.py:353
  94.5 3.9 %collective-permute-start.14 = (f32[16,384]{1,0:T(8,128)S(1)}, f32[16,384]{1,0:T(8,128)S(1)}, u32[]{:S(2)}, u32[]{:S(2)}) collective-permute-start(f32[16,384]{1,0:T(8,128)S(1)} %get-tuple-element.75), channel_id=1, source_target_pairs={{96,0},{97,1},{98,2},{99,3},{100,4},{101,5},{102,6},{103,7},{104,8... | collective-permute-start | bytes 73736 | tf_op jit(solution)/shard_map/ppermute | solution.py:353
  111.3 4.6 %collective-permute-start.15 = (f32[16,1152]{1,0:T(8,128)S(1)}, f32[16,1152]{1,0:T(8,128)S(1)}, u32[]{:S(2)}, u32[]{:S(2)}) collective-permute-start(f32[16,1152]{1,0:T(8,128)S(1)} %get-tuple-element.77), channel_id=1, source_target_pairs={{1,0},{0,1},{3,2},{2,3},{5,4},{4,5},{7,6},{6,7},{9,8},{8,9},{11,10... | collective-permute-start | bytes 221192 | tf_op jit(solution)/shard_map/ppermute | solution.py:353
  115.8 5.5 %collective-permute-start.18 = (f32[16,1152]{1,0:T(8,128)S(1)}, f32[16,1152]{1,0:T(8,128)S(1)}, u32[]{:S(2)}, u32[]{:S(2)}) collective-permute-start(f32[16,1152]{1,0:T(8,128)S(1)} %core_add.1.q0), channel_id=1, source_target_pairs={{64,0},{65,1},{66,2},{67,3},{68,4},{69,5},{70,6},{71,7},{72,8},{73... | collective-permute-start | bytes 221192 | tf_op jit(solution)/shard_map/ppermute | solution.py:353
  115.9 6.9 %collective-permute-start.17 = (f32[16,1152]{1,0:T(8,128)S(1)}, f32[16,1152]{1,0:T(8,128)S(1)}, u32[]{:S(2)}, u32[]{:S(2)}) collective-permute-start(f32[16,1152]{1,0:T(8,128)S(1)} %core_add.1.q0), channel_id=1, source_target_pairs={{96,0},{97,1},{98,2},{99,3},{100,4},{101,5},{102,6},{103,7},{104,8... | collective-permute-start | bytes 221192 | tf_op jit(solution)/shard_map/ppermute | solution.py:353
  117.4 5.4 %collective-permute-start.16 = (f32[16,1152]{1,0:T(8,128)S(1)}, f32[16,1152]{1,0:T(8,128)S(1)}, u32[]{:S(2)}, u32[]{:S(2)}) collective-permute-start(f32[16,1152]{1,0:T(8,128)S(1)} %core_add.1.q0), channel_id=1, source_target_pairs={{32,0},{33,1},{34,2},{35,3},{36,4},{37,5},{38,6},{39,7},{40,8},{41... | collective-permute-start | bytes 221192 | tf_op jit(solution)/shard_map/ppermute | solution.py:353

commit v8 on v7

--- a/solution.py
+++ b/solution.py
@@ -328,14 +328,7 @@
     wide = terms[0]
     gram = jnp.concatenate([wide[:, k * KV : (k + 1) * KV] for k in range(KV)], axis=0)
     gram = jnp.concatenate([gram, jnp.zeros((KV, 128 - KV), F32)], axis=1)
-    lane = lax.broadcasted_iota(jnp.int32, (KV, 128), 1)
-    row = lax.broadcasted_iota(jnp.int32, (KV, 128), 0)
-    factor = eliminate(gram, jnp.where(lane == row, math.sqrt(NTOT), 0.0))
-    p = proj[...]
-    terms = [factor[:, k : k + 1] * p[k : k + 1, :] for k in range(KV)]
-    while len(terms) > 1:
-        terms = [a + b for a, b in zip(terms[::2], terms[1::2])]
-    out[...] = terms[0]
+    out[...] = eliminate(gram, proj[...]) * math.sqrt(NTOT)
 
 
 def device_number(x, z, y, c):

time: 136 us -> 136 us (level)
  no operation moved by 1% of the time
where the time goes in v8:
time: 136 us
  blocking collectives  64.7 us (48%)
  Pallas kernels  27.8 us (20%)
  starting transfers between devices  26 us (19%)
  waiting for transfers between devices  16.6 us (12%)
    pallas_call x22, Pallas kernels, call(): pl.pallas_call(kernel, out_shape=outs, in_specs=[spec(n, a) for n, a in e...  27.8 us
    ppermute x19, starting transfers between devices, shift(): return lax.ppermute(v, ('x', 'z', 'y', 'c'), pairs)  26 us
    all_to_all x2, blocking collectives, body(): pieces = lax.all_to_all(pieces, ('y', 'z'), 0, 0)  21.1 us
    all_to_all x1, blocking collectives, body(): lax.all_to_all(sums[0], everyone, 0, 0)  17.9 us
    ppermute x19, waiting for transfers between devices, shift(): return lax.ppermute(v, ('x', 'z', 'y', 'c'), pairs)  16.6 us
    all_to_all x1, blocking collectives, body(): lax.all_to_all(table, everyone, 0, 0)  14.3 us
    all_to_all x1, blocking collectives, body(): grams = lax.all_to_all(grams, ('z', 'y', 'c'), 0, 0)  11.5 us
  transfers between devices with their start and end apart: 19, of which 10 were waited for; matrix products, arithmetic and copies ran while one was open for 0% of the time, Pallas kernels for 8%

profile of v8, /device:TPU:1, one launch (start us, length us, event | category | flops | bytes accessed | tf_op | source)
XLA Modules:
  0.0 136.0 jit_solution(7605025130225831919)
XLA Ops:
  0.7 1.6 %pack.1 = (bf16[336,128]{1,0:T(8,128)(2,1)S(1)}, bf16[1040,128]{1,0:T(8,128)(2,1)S(1)}) custom-call(s32[18]{0:T(128)S(1)} %pad_add_fusion.pos, bf16[1024,128]{1,0:T(8,128)(2,1)} %frames.1, s32[8,128]{1,0:T(8,128)} %bitcast.4, f32[16,1024]{1,0:T(8,128)} %start.1), custom_call_target="tpu_custom_call" | custom-call | tf_op jit(solution)/shard_map/pack/pallas_call | solution.py:43
  2.4 1.5 %collective-permute-start.3 = (bf16[1040,128]{1,0:T(8,128)(2,1)S(1)}, bf16[1040,128]{1,0:T(8,128)(2,1)S(1)}, u32[]{:S(2)}, u32[]{:S(2)}) collective-permute-start(bf16[1040,128]{1,0:T(8,128)(2,1)S(1)} %get-tuple-element.44.block), channel_id=1, source_target_pairs={{1,0},{0,1},{3,2},{2,3},{5,4},{4,5},{7,6},{6,7},{9,8},{8,9},{11,10... | collective-permute-start | bytes 798728 | tf_op jit(solution)/shard_map/ppermute | solution.py:346
  3.9 3.7 %collective-permute-start.2 = (bf16[336,128]{1,0:T(8,128)(2,1)S(1)}, bf16[336,128]{1,0:T(8,128)(2,1)S(1)}, u32[]{:S(2)}, u32[]{:S(2)}) collective-permute-start(bf16[336,128]{1,0:T(8,128)(2,1)S(1)} %get-tuple-element.43.a), channel_id=1, source_target_pairs={{4,0},{17,1},{6,2},{19,3},{0,4},{21,5},{2,6},{23,7},{12,8},{25,9},... | collective-permute-start | bytes 258056 | tf_op jit(solution)/shard_map/ppermute | solution.py:346
  9.5 2.8 %collective-permute-done.1.d = bf16[336,128]{1,0:T(8,128)(2,1)S(1)} collective-permute-done((bf16[336,128]{1,0:T(8,128)(2,1)S(1)}, bf16[336,128]{1,0:T(8,128)(2,1)S(1)}, u32[]{:S(2)}, u32[]{:S(2)}) %collective-permute-start.1) | collective-permute-done | bytes 86048 | tf_op jit(solution)/shard_map/ppermute | solution.py:346
  13.5 1.9 %collective-permute-start.6 = (bf16[4,336,128]{2,1,0:T(8,128)(2,1)S(1)}, bf16[4,336,128]{2,1,0:T(8,128)(2,1)S(1)}, u32[]{:S(2)}, u32[]{:S(2)}) collective-permute-start(bf16[4,336,128]{2,1,0:T(8,128)(2,1)S(1)} %stack.9.refs_0_.g0), channel_id=1, source_target_pairs={{24,0},{7,1},{26,2},{5,3},{28,4},{3,5},{30,6},{1,7},{16,8},{15,9},... | collective-permute-start | bytes 1032200 | tf_op jit(solution)/shard_map/ppermute | solution.py:346
  16.4 2.3 %rows0.1 = (bf16[1024,2048]{1,0:T(8,128)(2,1)S(1)}, f32[8,2048]{1,0:T(8,128)S(1)}) custom-call(s32[18]{0:T(128)S(1)} %pad_add_fusion.pos, bf16[4,336,128]{2,1,0:T(8,128)(2,1)S(1)} %stack.9.refs_0_.g0, bf16[1024,256]{1,0:T(8,128)(2,1)S(1)} %get-tuple-element.46.refs_1_, f32[1,1024]{1,0:T(1,128)S(1)} %get-tuple-element.45.ready.refs_2_, ...), custom_call_target="tpu_custom_call" | custom-call | flops 2147483648 | tf_op jit(solution)/shard_map/rows0/pallas_call | solution.py:43
  18.9 2.3 %rows1.1 = (bf16[1024,2048]{1,0:T(8,128)(2,1)S(1)}, f32[8,2048]{1,0:T(8,128)S(1)}) custom-call(s32[18]{0:T(128)S(1)} %pad_add_fusion.pos, bf16[4,336,128]{2,1,0:T(8,128)(2,1)S(1)} %collective-permute-done.4.refs_0_.g1, bf16[1024,256]{1,0:T(8,128)(2,1)S(1)} %get-tuple-element.46.refs_1_, f32[1,1024]{1,0:T(1,128)S(1)} %get-tuple-element.45.ready.refs_2_, ...), custom_call_target="tpu_custom_call" | custom-call | flops 2147483648 | tf_op jit(solution)/shard_map/rows1/pallas_call | solution.py:43
  21.2 3.5 %collective-permute-done.5.refs_0_.g2 = bf16[4,336,128]{2,1,0:T(8,128)(2,1)S(1)} collective-permute-done((bf16[4,336,128]{2,1,0:T(8,128)(2,1)S(1)}, bf16[4,336,128]{2,1,0:T(8,128)(2,1)S(1)}, u32[]{:S(2)}, u32[]{:S(2)}) %collective-permute-start.5) | collective-permute-done | bytes 344096 | tf_op jit(solution)/shard_map/ppermute | solution.py:346
  24.7 2.3 %rows2.1 = (bf16[1024,2048]{1,0:T(8,128)(2,1)S(1)}, f32[8,2048]{1,0:T(8,128)S(1)}) custom-call(s32[18]{0:T(128)S(1)} %pad_add_fusion.pos, bf16[4,336,128]{2,1,0:T(8,128)(2,1)S(1)} %collective-permute-done.5.refs_0_.g2, bf16[1024,256]{1,0:T(8,128)(2,1)S(1)} %get-tuple-element.46.refs_1_, f32[1,1024]{1,0:T(1,128)S(1)} %get-tuple-element.45.ready.refs_2_, ...), custom_call_target="tpu_custom_call" | custom-call | flops 2147483648 | tf_op jit(solution)/shard_map/rows2/pallas_call | solution.py:43
  27.0 2.4 %rows3.1 = (bf16[1024,2048]{1,0:T(8,128)(2,1)S(1)}, f32[128,1,256]{2,1,0:T(1,128)S(1)}) custom-call(s32[18]{0:T(128)S(1)} %pad_add_fusion.pos, bf16[4,336,128]{2,1,0:T(8,128)(2,1)S(1)} %collective-permute-done.6.refs_0_.g3, bf16[1024,256]{1,0:T(8,128)(2,1)S(1)} %get-tuple-element.46.refs_1_, f32[1,1024]{1,0:T(1,128)S(1)} %get-tuple-element.45.ready.refs_2_, ...), custom_call_target="tpu_custom_call" | custom-call | flops 2147483648 | tf_op jit(solution)/shard_map/rows3/pallas_call | solution.py:43
  29.4 17.9 %all_to_all.25.table = f32[128,1,256]{2,1,0:T(1,128)S(1)} all-to-all(f32[128,1,256]{2,1,0:T(1,128)S(1)} %get-tuple-element.56), channel_id=1, replica_groups=mesh['x'=4,'z'=4,'y'=4,'c'=2] {'y','z','x','c'}, dimensions={0} | all-to-all | bytes 262144 | tf_op jit(solution)/shard_map/all_to_all | solution.py:417
  47.3 2.8 %degree.1 = (f32[1,4096]{1,0:T(1,128)S(1)}, f32[128,1,256]{2,1,0:T(1,128)S(1)}) custom-call(s32[18]{0:T(128)S(1)} %pad_add_fusion.pos, bf16[1024,2048]{1,0:T(8,128)(2,1)S(1)} %get-tuple-element.49.k0, bf16[1024,2048]{1,0:T(8,128)(2,1)S(1)} %get-tuple-element.51.k1, bf16[1024,2048]{1,0:T(8,128)(2,1)S(1)} %get-tuple-element.53.k2, ...), custom_call_target="tpu_custom_call" | custom-call | tf_op jit(solution)/shard_map/degree/pallas_call | solution.py:43
  50.2 14.3 %all_to_all.26.table = f32[128,1,256]{2,1,0:T(1,128)S(1)} all-to-all(f32[128,1,256]{2,1,0:T(1,128)S(1)} %get-tuple-element.58), channel_id=1, replica_groups=mesh['x'=4,'z'=4,'y'=4,'c'=2] {'y','z','x','c'}, dimensions={0} | all-to-all | bytes 262144 | tf_op jit(solution)/shard_map/all_to_all | solution.py:423
  64.5 1.8 %first.1 = (bf16[16,4096]{1,0:T(8,128)(2,1)S(1)}, f32[1,4096]{1,0:T(1,128)S(1)}, f32[8,256]{1,0:T(8,128)S(1)}, f32[16,1024]{1,0:T(8,128)S(1)}) custom-call(s32[18]{0:T(128)S(1)} %pad_add_fusion.pos, bf16[1024,2048]{1,0:T(8,128)(2,1)S(1)} %get-tuple-element.49.k0, bf16[1024,2048]{1,0:T(8,128)(2,1)S(1)} %get-tuple-element.51.k1, ...), custom_call_target="tpu_custom_call" | custom-call | tf_op jit(solution)/shard_map/first/pallas_call | solution.py:43
  66.9 1.2 own1.1.own
  70.2 1.8 %collective-permute-start.10 = (f32[24,256]{1,0:T(8,128)S(1)}, f32[24,256]{1,0:T(8,128)S(1)}, u32[]{:S(2)}, u32[]{:S(2)}) collective-permute-start(f32[24,256]{1,0:T(8,128)S(1)} %get-tuple-element.65), channel_id=1, source_target_pairs={{96,0},{97,1},{98,2},{99,3},{100,4},{101,5},{102,6},{103,7},{104,8... | collective-permute-start | bytes 73736 | tf_op jit(solution)/shard_map/ppermute | solution.py:346
  74.7 10.6 %all_to_all.27.pieces = f32[16,16,256]{2,1,0:T(8,128)S(1)} all-to-all(f32[16,16,256]{2,1,0:T(8,128)S(1)} %get-tuple-element.68), channel_id=1, replica_groups=mesh['x'=4,'z'=4,'y'=4,'c'=2] {'y','z'}, dimensions={0} | all-to-all | bytes 524288 | tf_op jit(solution)/shard_map/all_to_all | solution.py:454
  85.2 2.0 %next1.1 = (bf16[32,4096]{1,0:T(8,128)(2,1)S(1)}, f32[16,128]{1,0:T(8,128)S(1)}, f32[16,1152]{1,0:T(8,128)S(1)}) custom-call(s32[18]{0:T(128)S(1)} %pad_add_fusion.pos, bf16[1024,2048]{1,0:T(8,128)(2,1)S(1)} %get-tuple-element.49.k0, bf16[1024,2048]{1,0:T(8,128)(2,1)S(1)} %get-tuple-element.51.k1, bf16[1024,2048]{1,0:T(8,128)(2,1)S(1)} %get-tuple-element.53.k2, ...), custom_call_target="tpu_custom_call" | custom-call | tf_op jit(solution)/shard_map/next1/pallas_call | solution.py:43
  87.2 3.2 %collective-permute-start.11 = (f32[16,1152]{1,0:T(8,128)S(1)}, f32[16,1152]{1,0:T(8,128)S(1)}, u32[]{:S(2)}, u32[]{:S(2)}) collective-permute-start(f32[16,1152]{1,0:T(8,128)S(1)} %get-tuple-element.70), channel_id=1, source_target_pairs={{1,0},{0,1},{3,2},{2,3},{5,4},{4,5},{7,6},{6,7},{9,8},{8,9},{11,10... | collective-permute-start | bytes 221192 | tf_op jit(solution)/shard_map/ppermute | solution.py:346
  90.4 1.4 %own2.1.own = f32[16,1024]{1,0:T(8,128)S(1)} custom-call(bf16[1024,2048]{1,0:T(8,128)(2,1)S(1)} %get-tuple-element.49.k0, bf16[1024,2048]{1,0:T(8,128)(2,1)S(1)} %get-tuple-element.51.k1, bf16[1024,2048]{1,0:T(8,128)(2,1)S(1)} %get-tuple-element.53.k2, bf16[1024,2048]{1,0:T(8,128)(2,1)S(1)} %get-tuple-element.55.k3, bf16[32,4096]{1,0:T(8,128)(2,1)S(1)} %get-tuple-element.69.vec), custom_call_target="tpu_custom_call" | custom-call | flops 2147483648 | tf_op jit(solution)/shard_map/own2/pallas_call | solution.py:43
  93.4 1.2 collective-permute-start.13
  94.5 1.2 collective-permute-start.14
  96.6 1.8 %collective-permute-done.14.q3 = f32[16,384]{1,0:T(8,128)S(1)} collective-permute-done((f32[16,384]{1,0:T(8,128)S(1)}, f32[16,384]{1,0:T(8,128)S(1)}, u32[]{:S(2)}, u32[]{:S(2)}) %collective-permute-start.14) | collective-permute-done | bytes 24608 | tf_op jit(solution)/shard_map/ppermute | solution.py:346
  98.7 10.5 %all_to_all.28.pieces = f32[16,16,256]{2,1,0:T(8,128)S(1)} all-to-all(f32[16,16,256]{2,1,0:T(8,128)S(1)} %project2.1), channel_id=1, replica_groups=mesh['x'=4,'z'=4,'y'=4,'c'=2] {'y','z'}, dimensions={0} | all-to-all | bytes 524288 | tf_op jit(solution)/shard_map/all_to_all | solution.py:454
  109.3 2.0 %next2.1 = (bf16[32,4096]{1,0:T(8,128)(2,1)S(1)}, f32[16,128]{1,0:T(8,128)S(1)}, f32[16,1152]{1,0:T(8,128)S(1)}) custom-call(s32[18]{0:T(128)S(1)} %pad_add_fusion.pos, bf16[1024,2048]{1,0:T(8,128)(2,1)S(1)} %get-tuple-element.49.k0, bf16[1024,2048]{1,0:T(8,128)(2,1)S(1)} %get-tuple-element.51.k1, bf16[1024,2048]{1,0:T(8,128)(2,1)S(1)} %get-tuple-element.53.k2, ...), custom_call_target="tpu_custom_call" | custom-call | tf_op jit(solution)/shard_map/next2/pallas_call | solution.py:43
  111.3 3.1 %collective-permute-start.15 = (f32[16,1152]{1,0:T(8,128)S(1)}, f32[16,1152]{1,0:T(8,128)S(1)}, u32[]{:S(2)}, u32[]{:S(2)}) collective-permute-start(f32[16,1152]{1,0:T(8,128)S(1)} %get-tuple-element.77), channel_id=1, source_target_pairs={{1,0},{0,1},{3,2},{2,3},{5,4},{4,5},{7,6},{6,7},{9,8},{8,9},{11,10... | collective-permute-start | bytes 221192 | tf_op jit(solution)/shard_map/ppermute | solution.py:346
  114.4 1.4 %own3.1.own = f32[16,1024]{1,0:T(8,128)S(1)} custom-call(bf16[1024,2048]{1,0:T(8,128)(2,1)S(1)} %get-tuple-element.49.k0, bf16[1024,2048]{1,0:T(8,128)(2,1)S(1)} %get-tuple-element.51.k1, bf16[1024,2048]{1,0:T(8,128)(2,1)S(1)} %get-tuple-element.53.k2, bf16[1024,2048]{1,0:T(8,128)(2,1)S(1)} %get-tuple-element.55.k3, bf16[32,4096]{1,0:T(8,128)(2,1)S(1)} %get-tuple-element.76.vec), custom_call_target="tpu_custom_call" | custom-call | flops 2147483648 | tf_op jit(solution)/shard_map/own3/pallas_call | solution.py:43
  115.9 1.5 %collective-permute-start.17 = (f32[16,1152]{1,0:T(8,128)S(1)}, f32[16,1152]{1,0:T(8,128)S(1)}, u32[]{:S(2)}, u32[]{:S(2)}) collective-permute-start(f32[16,1152]{1,0:T(8,128)S(1)} %core_add.1.q0), channel_id=1, source_target_pairs={{96,0},{97,1},{98,2},{99,3},{100,4},{101,5},{102,6},{103,7},{104,8... | collective-permute-start | bytes 221192 | tf_op jit(solution)/shard_map/ppermute | solution.py:346
  117.4 1.2 collective-permute-start.16
  118.6 2.8 %collective-permute-done.18.q3 = f32[16,1152]{1,0:T(8,128)S(1)} collective-permute-done((f32[16,1152]{1,0:T(8,128)S(1)}, f32[16,1152]{1,0:T(8,128)S(1)}, u32[]{:S(2)}, u32[]{:S(2)}) %collective-permute-start.18) | collective-permute-done | bytes 73760 | tf_op jit(solution)/shard_map/ppermute | solution.py:346
  121.4 1.4 %collective-permute-done.17.q2 = f32[16,1152]{1,0:T(8,128)S(1)} collective-permute-done((f32[16,1152]{1,0:T(8,128)S(1)}, f32[16,1152]{1,0:T(8,128)S(1)}, u32[]{:S(2)}, u32[]{:S(2)}) %collective-permute-start.17) | collective-permute-done | bytes 73760 | tf_op jit(solution)/shard_map/ppermute | solution.py:346
  123.4 11.5 %all_to_all.29.grams = f32[32,1,256]{2,1,0:T(1,128)S(1)} all-to-all(f32[32,1,256]{2,1,0:T(1,128)S(1)} %get-tuple-element.80), channel_id=1, replica_groups=mesh['x'=4,'z'=4,'y'=4,'c'=2] {'z','y','c'}, dimensions={0} | all-to-all | bytes 65536 | tf_op jit(solution)/shard_map/all_to_all | solution.py:472
  (35 shorter events, 14.4 us)
Async XLA Ops:
  2.4 13.8 %collective-permute-start.3 = (bf16[1040,128]{1,0:T(8,128)(2,1)S(1)}, bf16[1040,128]{1,0:T(8,128)(2,1)S(1)}, u32[]{:S(2)}, u32[]{:S(2)}) collective-permute-start(bf16[1040,128]{1,0:T(8,128)(2,1)S(1)} %get-tuple-element.44.block), channel_id=1, source_target_pairs={{1,0},{0,1},{3,2},{2,3},{5,4},{4,5},{7,6},{6,7},{9,8},{8,9},{11,10... | collective-permute-start | bytes 798728 | tf_op jit(solution)/shard_map/ppermute | solution.py:346
  3.9 5.7 %collective-permute-start.2 = (bf16[336,128]{1,0:T(8,128)(2,1)S(1)}, bf16[336,128]{1,0:T(8,128)(2,1)S(1)}, u32[]{:S(2)}, u32[]{:S(2)}) collective-permute-start(bf16[336,128]{1,0:T(8,128)(2,1)S(1)} %get-tuple-element.43.a), channel_id=1, source_target_pairs={{4,0},{17,1},{6,2},{19,3},{0,4},{21,5},{2,6},{23,7},{12,8},{25,9},... | collective-permute-start | bytes 258056 | tf_op jit(solution)/shard_map/ppermute | solution.py:346
  7.5 4.8 %collective-permute-start.1 = (bf16[336,128]{1,0:T(8,128)(2,1)S(1)}, bf16[336,128]{1,0:T(8,128)(2,1)S(1)}, u32[]{:S(2)}, u32[]{:S(2)}) collective-permute-start(bf16[336,128]{1,0:T(8,128)(2,1)S(1)} %get-tuple-element.43.a), channel_id=1, source_target_pairs={{6,0},{25,1},{4,2},{27,3},{2,4},{29,5},{0,6},{31,7},{14,8},{17,9},... | collective-permute-start | bytes 258056 | tf_op jit(solution)/shard_map/ppermute | solution.py:346
  8.0 4.4 %collective-permute-start = (bf16[336,128]{1,0:T(8,128)(2,1)S(1)}, bf16[336,128]{1,0:T(8,128)(2,1)S(1)}, u32[]{:S(2)}, u32[]{:S(2)}) collective-permute-start(bf16[336,128]{1,0:T(8,128)(2,1)S(1)} %get-tuple-element.43.a), channel_id=1, source_target_pairs={{2,0},{9,1},{0,2},{11,3},{6,4},{13,5},{4,6},{15,7},{10,8},{1,9},{8... | collective-permute-start | bytes 258056 | tf_op jit(solution)/shard_map/ppermute | solution.py:346
  12.4 6.5 %collective-permute-start.4 = (bf16[4,336,128]{2,1,0:T(8,128)(2,1)S(1)}, bf16[4,336,128]{2,1,0:T(8,128)(2,1)S(1)}, u32[]{:S(2)}, u32[]{:S(2)}) collective-permute-start(bf16[4,336,128]{2,1,0:T(8,128)(2,1)S(1)} %stack.9.refs_0_.g0), channel_id=1, source_target_pairs={{8,0},{3,1},{10,2},{1,3},{12,4},{7,5},{14,6},{5,7},{0,8},{11,9},{2... | collective-permute-start | bytes 1032200 | tf_op jit(solution)/shard_map/ppermute | solution.py:346
  13.5 13.5 %collective-permute-start.6 = (bf16[4,336,128]{2,1,0:T(8,128)(2,1)S(1)}, bf16[4,336,128]{2,1,0:T(8,128)(2,1)S(1)}, u32[]{:S(2)}, u32[]{:S(2)}) collective-permute-start(bf16[4,336,128]{2,1,0:T(8,128)(2,1)S(1)} %stack.9.refs_0_.g0), channel_id=1, source_target_pairs={{24,0},{7,1},{26,2},{5,3},{28,4},{3,5},{30,6},{1,7},{16,8},{15,9},... | collective-permute-start | bytes 1032200 | tf_op jit(solution)/shard_map/ppermute | solution.py:346
  15.4 9.3 %collective-permute-start.5 = (bf16[4,336,128]{2,1,0:T(8,128)(2,1)S(1)}, bf16[4,336,128]{2,1,0:T(8,128)(2,1)S(1)}, u32[]{:S(2)}, u32[]{:S(2)}) collective-permute-start(bf16[4,336,128]{2,1,0:T(8,128)(2,1)S(1)} %stack.9.refs_0_.g0), channel_id=1, source_target_pairs={{16,0},{5,1},{18,2},{7,3},{20,4},{1,5},{22,6},{3,7},{24,8},{13,9},... | collective-permute-start | bytes 1032200 | tf_op jit(solution)/shard_map/ppermute | solution.py:346
  66.2 1.9 %collective-permute-start.7 = (f32[16,1024]{1,0:T(8,128)S(1)}, f32[16,1024]{1,0:T(8,128)S(1)}, u32[]{:S(2)}, u32[]{:S(2)}) collective-permute-start(f32[16,1024]{1,0:T(8,128)S(1)} %get-tuple-element.61), channel_id=1, source_target_pairs={{1,0},{0,1},{3,2},{2,3},{5,4},{4,5},{7,6},{6,7},{9,8},{8,9},{11,10... | collective-permute-start | bytes 196616 | tf_op jit(solution)/shard_map/ppermute | solution.py:346
  68.7 4.3 %collective-permute-start.8 = (f32[24,256]{1,0:T(8,128)S(1)}, f32[24,256]{1,0:T(8,128)S(1)}, u32[]{:S(2)}, u32[]{:S(2)}) collective-permute-start(f32[24,256]{1,0:T(8,128)S(1)} %get-tuple-element.63), channel_id=1, source_target_pairs={{64,0},{65,1},{66,2},{67,3},{68,4},{69,5},{70,6},{71,7},{72,8},{73... | collective-permute-start | bytes 73736 | tf_op jit(solution)/shard_map/ppermute | solution.py:346
  69.6 3.4 %collective-permute-start.9 = (f32[24,256]{1,0:T(8,128)S(1)}, f32[24,256]{1,0:T(8,128)S(1)}, u32[]{:S(2)}, u32[]{:S(2)}) collective-permute-start(f32[24,256]{1,0:T(8,128)S(1)} %get-tuple-element.64), channel_id=1, source_target_pairs={{32,0},{33,1},{34,2},{35,3},{36,4},{37,5},{38,6},{39,7},{40,8},{41... | collective-permute-start | bytes 73736 | tf_op jit(solution)/shard_map/ppermute | solution.py:346
  70.2 3.9 %collective-permute-start.10 = (f32[24,256]{1,0:T(8,128)S(1)}, f32[24,256]{1,0:T(8,128)S(1)}, u32[]{:S(2)}, u32[]{:S(2)}) collective-permute-start(f32[24,256]{1,0:T(8,128)S(1)} %get-tuple-element.65), channel_id=1, source_target_pairs={{96,0},{97,1},{98,2},{99,3},{100,4},{101,5},{102,6},{103,7},{104,8... | collective-permute-start | bytes 73736 | tf_op jit(solution)/shard_map/ppermute | solution.py:346
  87.2 4.6 %collective-permute-start.11 = (f32[16,1152]{1,0:T(8,128)S(1)}, f32[16,1152]{1,0:T(8,128)S(1)}, u32[]{:S(2)}, u32[]{:S(2)}) collective-permute-start(f32[16,1152]{1,0:T(8,128)S(1)} %get-tuple-element.70), channel_id=1, source_target_pairs={{1,0},{0,1},{3,2},{2,3},{5,4},{4,5},{7,6},{6,7},{9,8},{8,9},{11,10... | collective-permute-start | bytes 221192 | tf_op jit(solution)/shard_map/ppermute | solution.py:346
  92.4 4.3 %collective-permute-start.12 = (f32[16,384]{1,0:T(8,128)S(1)}, f32[16,384]{1,0:T(8,128)S(1)}, u32[]{:S(2)}, u32[]{:S(2)}) collective-permute-start(f32[16,384]{1,0:T(8,128)S(1)} %get-tuple-element.73), channel_id=1, source_target_pairs={{64,0},{65,1},{66,2},{67,3},{68,4},{69,5},{70,6},{71,7},{72,8},{73... | collective-permute-start | bytes 73736 | tf_op jit(solution)/shard_map/ppermute | solution.py:346
  93.4 3.3 %collective-permute-start.13 = (f32[16,384]{1,0:T(8,128)S(1)}, f32[16,384]{1,0:T(8,128)S(1)}, u32[]{:S(2)}, u32[]{:S(2)}) collective-permute-start(f32[16,384]{1,0:T(8,128)S(1)} %get-tuple-element.74), channel_id=1, source_target_pairs={{32,0},{33,1},{34,2},{35,3},{36,4},{37,5},{38,6},{39,7},{40,8},{41... | collective-permute-start | bytes 73736 | tf_op jit(solution)/shard_map/ppermute | solution.py:346
  94.5 3.9 %collective-permute-start.14 = (f32[16,384]{1,0:T(8,128)S(1)}, f32[16,384]{1,0:T(8,128)S(1)}, u32[]{:S(2)}, u32[]{:S(2)}) collective-permute-start(f32[16,384]{1,0:T(8,128)S(1)} %get-tuple-element.75), channel_id=1, source_target_pairs={{96,0},{97,1},{98,2},{99,3},{100,4},{101,5},{102,6},{103,7},{104,8... | collective-permute-start | bytes 73736 | tf_op jit(solution)/shard_map/ppermute | solution.py:346
  111.3 4.6 %collective-permute-start.15 = (f32[16,1152]{1,0:T(8,128)S(1)}, f32[16,1152]{1,0:T(8,128)S(1)}, u32[]{:S(2)}, u32[]{:S(2)}) collective-permute-start(f32[16,1152]{1,0:T(8,128)S(1)} %get-tuple-element.77), channel_id=1, source_target_pairs={{1,0},{0,1},{3,2},{2,3},{5,4},{4,5},{7,6},{6,7},{9,8},{8,9},{11,10... | collective-permute-start | bytes 221192 | tf_op jit(solution)/shard_map/ppermute | solution.py:346
  115.8 5.5 %collective-permute-start.18 = (f32[16,1152]{1,0:T(8,128)S(1)}, f32[16,1152]{1,0:T(8,128)S(1)}, u32[]{:S(2)}, u32[]{:S(2)}) collective-permute-start(f32[16,1152]{1,0:T(8,128)S(1)} %core_add.1.q0), channel_id=1, source_target_pairs={{64,0},{65,1},{66,2},{67,3},{68,4},{69,5},{70,6},{71,7},{72,8},{73... | collective-permute-start | bytes 221192 | tf_op jit(solution)/shard_map/ppermute | solution.py:346
  115.9 6.9 %collective-permute-start.17 = (f32[16,1152]{1,0:T(8,128)S(1)}, f32[16,1152]{1,0:T(8,128)S(1)}, u32[]{:S(2)}, u32[]{:S(2)}) collective-permute-start(f32[16,1152]{1,0:T(8,128)S(1)} %core_add.1.q0), channel_id=1, source_target_pairs={{96,0},{97,1},{98,2},{99,3},{100,4},{101,5},{102,6},{103,7},{104,8... | collective-permute-start | bytes 221192 | tf_op jit(solution)/shard_map/ppermute | solution.py:346
  117.4 5.4 %collective-permute-start.16 = (f32[16,1152]{1,0:T(8,128)S(1)}, f32[16,1152]{1,0:T(8,128)S(1)}, u32[]{:S(2)}, u32[]{:S(2)}) collective-permute-start(f32[16,1152]{1,0:T(8,128)S(1)} %core_add.1.q0), channel_id=1, source_target_pairs={{32,0},{33,1},{34,2},{35,3},{36,4},{37,5},{38,6},{39,7},{40,8},{41... | collective-permute-start | bytes 221192 | tf_op jit(solution)/shard_map/ppermute | solution.py:346
